TPU v7x, 32 devices: a whole 2x2x4 slice. The times are simulated.
32 devices in a mesh: dp: 4 (over y, core), seq: 8 (over z, x).
Axes of the slice: x: 2, y: 2, z: 4, core: 2. Of those that a mesh axis runs over, the one named last changes fastest.
Arguments:
- tokens: bfloat16 [32, 1024, 768], P('dp', 'seq'), may hold values from -6 to 6
- offsets: int32 [32], P('dp'), may hold values from 0 to 511, as said below
- norm_gain: float32 [768], replicated, may hold values from 0.5 to 1.5
- norm_bias: float32 [768], replicated, may hold values from -1.5 to 1.5
- proj_weight: bfloat16 [768, 2304], replicated, may hold values from -0.21875 to 0.21875
- proj_bias: float32 [2304], replicated, may hold values from -1.5 to 1.5
- short_filter: float32 [2304, 3], replicated, may hold values from -3 to 3
- short_bias: float32 [2304], replicated, may hold values from -1.5 to 1.5
- long_kernel: float32 [768, 1024], P(None, 'seq'), may hold values from -0.1875 to 0.1875
- skip_bias: float32 [768], replicated, may hold values from -4 to 4
- out_weight: bfloat16 [768, 768], replicated, may hold values from -0.21875 to 0.21875
- out_bias: float32 [768], replicated, may hold values from -1.5 to 1.5
- second_gain: float32 [768], replicated, may hold values from 0.5 to 1.5
- second_bias: float32 [768], replicated, may hold values from -1.5 to 1.5
- up_weight: bfloat16 [768, 3072], replicated, may hold values from -0.21875 to 0.21875
- up_bias: float32 [3072], replicated, may hold values from -1.5 to 1.5
- down_weight: bfloat16 [3072, 768], replicated, may hold values from -0.21875 to 0.21875
- down_bias: float32 [768], replicated, may hold values from -1.5 to 1.5
- cotangent: bfloat16 [32, 1024, 768], P('dp', 'seq'), may hold values from -6 to 6
Outputs:
- output: float32 [32, 1024, 768], P('dp', 'seq')
- input_grad: float32 [32, 1024, 768], P('dp', 'seq')
- norm_gain_grad: float32 [768], P('seq')
- norm_bias_grad: float32 [768], P('seq')
- proj_grad: float32 [768, 2304], P('seq')
- proj_bias_grad: float32 [2304], P('seq')
- filter_grad: float32 [2304, 3], P('seq')
- short_bias_grad: float32 [2304], P('seq')
- kernel_grad: float32 [768, 1024], P('seq')
- skip_bias_grad: float32 [768], P('seq')
- out_grad: float32 [768, 768], P('seq')
- out_bias_grad: float32 [768], P('seq')
- second_gain_grad: float32 [768], P('seq')
- second_bias_grad: float32 [768], P('seq')
- up_grad: float32 [768, 3072], P('seq')
- up_bias_grad: float32 [3072], P('seq')
- down_grad: float32 [3072, 768], P('seq')
- down_bias_grad: float32 [768], P('seq')
Inputs may be any that keep to these rules, and one draw needn't show every extreme that they name: `offsets`: in each group of 8 consecutive sequences one starts within its first 128 tokens; the others start below 512.
All inputs are finite; a program needn't handle non-finite values.
Results may differ from a plain program's by a relative error of at most 0.0072.
Values sent between devices are 32-bit elements; how exact they have to be, the bound alone decides.
No kernel may reach another device: no remote copies, remote signals or barrier semaphores. Data moves between devices by JAX's collectives and lax.ppermute only.
A program may use at most 256 MiB of HBM per device.

v0:
```python
import math

import jax
import jax.numpy as jnp
from jax import lax
from jax.sharding import PartitionSpec as P

EPSILON = 1e-05
PRECISE = lax.Precision.HIGHEST


def passed_along(array, axis, by):
    count = lax.axis_size(axis)
    pairs = [(i, i + by) for i in range(count) if 0 <= i + by < count]
    return lax.ppermute(array, axis, pairs)


def layer_norm(values, gain, offset):
    centered = values - jnp.mean(values, axis=-1, keepdims=True)
    spread = lax.rsqrt(jnp.mean(centered * centered, axis=-1, keepdims=True) + EPSILON)
    return centered * spread * gain + offset


def angle_table(rows, cols, modulus):
    product = (
        jnp.arange(rows, dtype=jnp.int32)[:, None]
        * jnp.arange(cols, dtype=jnp.int32)[None, :]
        % modulus
    )
    angles = product.astype(jnp.float32) * (2.0 * math.pi / modulus)
    return (jnp.cos(angles), jnp.sin(angles))


def fourier_tables(blocks, width):
    coarse_cos, coarse_sin = angle_table(blocks, 2 * blocks, 2 * blocks)
    twist_cos, twist_sin = angle_table(2 * blocks, width, 2 * blocks * width)
    fine_cos, fine_sin = angle_table(width, width, width)
    return (coarse_cos, coarse_sin, twist_cos, twist_sin, fine_cos, fine_sin)


def forward_transform(signal, tables):
    coarse_cos, coarse_sin, twist_cos, twist_sin, fine_cos, fine_sin = tables
    first_real = jnp.einsum("rpc,pk->rkc", signal, coarse_cos, precision=PRECISE)
    first_imag = -jnp.einsum("rpc,pk->rkc", signal, coarse_sin, precision=PRECISE)
    turned_real = first_real * twist_cos + first_imag * twist_sin
    turned_imag = first_imag * twist_cos - first_real * twist_sin
    spectrum_real = jnp.einsum(
        "rkc,cm->rkm", turned_real, fine_cos, precision=PRECISE
    ) + jnp.einsum("rkc,cm->rkm", turned_imag, fine_sin, precision=PRECISE)
    spectrum_imag = jnp.einsum(
        "rkc,cm->rkm", turned_imag, fine_cos, precision=PRECISE
    ) - jnp.einsum("rkc,cm->rkm", turned_real, fine_sin, precision=PRECISE)
    return (spectrum_real, spectrum_imag)


def inverse_transform(spectrum_real, spectrum_imag, tables):
    coarse_cos, coarse_sin, twist_cos, twist_sin, fine_cos, fine_sin = tables
    back_real = jnp.einsum("rkm,cm->rkc", spectrum_real, fine_cos, precision=PRECISE) - jnp.einsum(
        "rkm,cm->rkc", spectrum_imag, fine_sin, precision=PRECISE
    )
    back_imag = jnp.einsum("rkm,cm->rkc", spectrum_real, fine_sin, precision=PRECISE) + jnp.einsum(
        "rkm,cm->rkc", spectrum_imag, fine_cos, precision=PRECISE
    )
    turned_real = back_real * twist_cos - back_imag * twist_sin
    turned_imag = back_real * twist_sin + back_imag * twist_cos
    total = 2 * coarse_cos.shape[0] * twist_cos.shape[1]
    signal = jnp.einsum("rkc,pk->rpc", turned_real, coarse_cos, precision=PRECISE) - jnp.einsum(
        "rkc,pk->rpc", turned_imag, coarse_sin, precision=PRECISE
    )
    return signal / total


def per_device(
    tokens,
    offsets,
    norm_gain,
    norm_bias,
    proj_weight,
    proj_bias,
    short_filter,
    short_bias,
    long_kernel,
    skip_bias,
    out_weight,
    out_bias,
    second_gain,
    second_bias,
    up_weight,
    up_bias,
    down_weight,
    down_bias,
    cotangent,
):
    seq_count, tok_count, features = tokens.shape
    parts = lax.axis_size("seq")
    chans = features // parts
    length = parts * tok_count
    tables = fourier_tables(parts, tok_count)
    spectral = (seq_count, chans, 2 * parts, tok_count)
    positions = lax.axis_index("seq") * tok_count + jnp.arange(tok_count, dtype=jnp.int32)
    live = (positions[None, :] >= offsets[:, None]).astype(jnp.float32)[:, :, None]
    hidden = tokens.astype(jnp.float32)
    normed, norm_pull = jax.vjp(layer_norm, hidden, norm_gain, norm_bias)
    normed_low = normed.astype(jnp.bfloat16)
    mixed = (
        jnp.einsum("sti,ij->stj", normed_low, proj_weight, preferred_element_type=jnp.float32)
        + proj_bias
    )
    rim = passed_along(mixed[:, tok_count - 2 :, :], "seq", 1)
    extended = jnp.concatenate([rim, mixed], axis=1)
    filtered = (
        short_filter[:, 0] * extended[:, :tok_count]
        + short_filter[:, 1] * extended[:, 1 : tok_count + 1]
        + short_filter[:, 2] * extended[:, 2:]
        + short_bias
    )
    outer_gate = filtered[:, :, :features]
    inner_gate = filtered[:, :, features : 2 * features]
    values = filtered[:, :, 2 * features :]
    gated = values * inner_gate * live
    gated_chan, kernel_chan = (
        lax.all_to_all(jnp.swapaxes(gated, 1, 2), "seq", split_axis=1, concat_axis=2, tiled=True),
        lax.all_to_all(long_kernel[None], "seq", split_axis=1, concat_axis=2, tiled=True),
    )
    gated_real, gated_imag = forward_transform(
        gated_chan.reshape(seq_count * chans, parts, tok_count), tables
    )
    gated_real = gated_real.reshape(spectral)
    gated_imag = gated_imag.reshape(spectral)
    kernel_real, kernel_imag = forward_transform(
        kernel_chan.reshape(chans, parts, tok_count), tables
    )
    prod_real = gated_real * kernel_real - gated_imag * kernel_imag
    prod_imag = gated_real * kernel_imag + gated_imag * kernel_real
    conv_chan = inverse_transform(
        prod_real.reshape(-1, 2 * parts, tok_count),
        prod_imag.reshape(-1, 2 * parts, tok_count),
        tables,
    )
    conv_chan = conv_chan.reshape(seq_count, chans, length)
    conv_tokens = jnp.swapaxes(
        lax.all_to_all(conv_chan, "seq", split_axis=2, concat_axis=1, tiled=True), 1, 2
    )
    convolved = conv_tokens + gated * skip_bias
    branch = convolved * outer_gate
    branch_low = branch.astype(jnp.bfloat16)
    residual = (
        hidden
        + jnp.einsum("sti,ij->stj", branch_low, out_weight, preferred_element_type=jnp.float32)
        + out_bias
    )
    normed_two, second_pull = jax.vjp(layer_norm, residual, second_gain, second_bias)
    normed_two_low = normed_two.astype(jnp.bfloat16)
    expanded = (
        jnp.einsum("sti,ij->stj", normed_two_low, up_weight, preferred_element_type=jnp.float32)
        + up_bias
    )
    activated, gelu_pull = jax.vjp(jax.nn.gelu, expanded)
    activated_low = activated.astype(jnp.bfloat16)
    output = (
        residual
        + jnp.einsum("sti,ij->stj", activated_low, down_weight, preferred_element_type=jnp.float32)
        + down_bias
    )
    upstream = cotangent.astype(jnp.float32)
    down_grad = jnp.einsum(
        "sti,stj->ij", activated_low, cotangent, preferred_element_type=jnp.float32
    )
    down_bias_grad = jnp.sum(upstream, axis=(0, 1))
    act_grad = jnp.einsum("stj,ij->sti", cotangent, down_weight, preferred_element_type=jnp.float32)
    (expanded_grad,) = gelu_pull(act_grad)
    expanded_low = expanded_grad.astype(jnp.bfloat16)
    up_grad = jnp.einsum(
        "sti,stj->ij", normed_two_low, expanded_low, preferred_element_type=jnp.float32
    )
    up_bias_grad = jnp.sum(expanded_low.astype(jnp.float32), axis=(0, 1))
    normed_two_grad = jnp.einsum(
        "stj,ij->sti", expanded_low, up_weight, preferred_element_type=jnp.float32
    )
    residual_part, second_gain_grad, second_bias_grad = second_pull(normed_two_grad)
    residual_grad = upstream + residual_part
    residual_low = residual_grad.astype(jnp.bfloat16)
    out_grad = jnp.einsum(
        "sti,stj->ij", branch_low, residual_low, preferred_element_type=jnp.float32
    )
    out_bias_grad = jnp.sum(residual_low.astype(jnp.float32), axis=(0, 1))
    branch_grad = jnp.einsum(
        "stj,ij->sti", residual_low, out_weight, preferred_element_type=jnp.float32
    )
    conv_grad = branch_grad * outer_gate
    outer_grad = branch_grad * convolved
    skip_bias_grad = jnp.sum(conv_grad * gated, axis=(0, 1))
    conv_grad_chan = lax.all_to_all(
        jnp.swapaxes(conv_grad, 1, 2), "seq", split_axis=1, concat_axis=2, tiled=True
    )
    grad_real, grad_imag = forward_transform(
        conv_grad_chan.reshape(seq_count * chans, parts, tok_count), tables
    )
    grad_real = grad_real.reshape(spectral)
    grad_imag = grad_imag.reshape(spectral)
    back_real = kernel_real * grad_real + kernel_imag * grad_imag
    back_imag = kernel_real * grad_imag - kernel_imag * grad_real
    gated_back_chan = inverse_transform(
        back_real.reshape(-1, 2 * parts, tok_count),
        back_imag.reshape(-1, 2 * parts, tok_count),
        tables,
    )
    gated_back_chan = gated_back_chan.reshape(seq_count, chans, length)
    tap_real = jnp.sum(gated_real * grad_real + gated_imag * grad_imag, axis=0)
    tap_imag = jnp.sum(gated_real * grad_imag - gated_imag * grad_real, axis=0)
    kernel_grad = inverse_transform(tap_real, tap_imag, tables).reshape(chans, length)
    gated_back = jnp.swapaxes(
        lax.all_to_all(gated_back_chan, "seq", split_axis=2, concat_axis=1, tiled=True), 1, 2
    )
    gated_grad = (gated_back + conv_grad * skip_bias) * live
    value_grad = gated_grad * inner_gate
    inner_grad = gated_grad * values
    filtered_grad = jnp.concatenate([outer_grad, inner_grad, value_grad], axis=2)
    following = passed_along(filtered_grad[:, :2, :], "seq", -1)
    grad_extended = jnp.concatenate([filtered_grad, following], axis=1)
    mixed_grad = (
        short_filter[:, 2] * grad_extended[:, :tok_count]
        + short_filter[:, 1] * grad_extended[:, 1 : tok_count + 1]
        + short_filter[:, 0] * grad_extended[:, 2:]
    )
    filter_grad = jnp.stack(
        [
            jnp.sum(filtered_grad * extended[:, position : position + tok_count], axis=(0, 1))
            for position in range(3)
        ],
        axis=1,
    )
    short_bias_grad = jnp.sum(filtered_grad, axis=(0, 1))
    mixed_low = mixed_grad.astype(jnp.bfloat16)
    proj_grad = jnp.einsum("sti,stj->ij", normed_low, mixed_low, preferred_element_type=jnp.float32)
    proj_bias_grad = jnp.sum(mixed_low.astype(jnp.float32), axis=(0, 1))
    normed_grad = jnp.einsum(
        "stj,ij->sti", mixed_low, proj_weight, preferred_element_type=jnp.float32
    )
    hidden_part, norm_gain_grad, norm_bias_grad = norm_pull(normed_grad)
    input_grad = residual_grad + hidden_part
    (
        norm_gain_share,
        norm_bias_share,
        proj_share,
        proj_bias_share,
        filter_share,
        short_bias_share,
        skip_share,
        out_share,
        out_bias_share,
        second_gain_share,
        second_bias_share,
        up_share,
        up_bias_share,
        down_share,
        down_bias_share,
    ) = (
        lax.psum_scatter(norm_gain_grad, "seq", scatter_dimension=0, tiled=True),
        lax.psum_scatter(norm_bias_grad, "seq", scatter_dimension=0, tiled=True),
        lax.psum_scatter(proj_grad, "seq", scatter_dimension=0, tiled=True),
        lax.psum_scatter(proj_bias_grad, "seq", scatter_dimension=0, tiled=True),
        lax.psum_scatter(filter_grad, "seq", scatter_dimension=0, tiled=True),
        lax.psum_scatter(short_bias_grad, "seq", scatter_dimension=0, tiled=True),
        lax.psum_scatter(skip_bias_grad, "seq", scatter_dimension=0, tiled=True),
        lax.psum_scatter(out_grad, "seq", scatter_dimension=0, tiled=True),
        lax.psum_scatter(out_bias_grad, "seq", scatter_dimension=0, tiled=True),
        lax.psum_scatter(second_gain_grad, "seq", scatter_dimension=0, tiled=True),
        lax.psum_scatter(second_bias_grad, "seq", scatter_dimension=0, tiled=True),
        lax.psum_scatter(up_grad, "seq", scatter_dimension=0, tiled=True),
        lax.psum_scatter(up_bias_grad, "seq", scatter_dimension=0, tiled=True),
        lax.psum_scatter(down_grad, "seq", scatter_dimension=0, tiled=True),
        lax.psum_scatter(down_bias_grad, "seq", scatter_dimension=0, tiled=True),
    )
    (
        norm_gain_grad,
        norm_bias_grad,
        proj_grad,
        proj_bias_grad,
        filter_grad,
        short_bias_grad,
        skip_bias_grad,
        out_grad,
        out_bias_grad,
        second_gain_grad,
        second_bias_grad,
        up_grad,
        up_bias_grad,
        down_grad,
        down_bias_grad,
        kernel_grad,
    ) = lax.psum(
        (
            norm_gain_share,
            norm_bias_share,
            proj_share,
            proj_bias_share,
            filter_share,
            short_bias_share,
            skip_share,
            out_share,
            out_bias_share,
            second_gain_share,
            second_bias_share,
            up_share,
            up_bias_share,
            down_share,
            down_bias_share,
            kernel_grad,
        ),
        "dp",
    )
    return (
        output,
        input_grad,
        norm_gain_grad,
        norm_bias_grad,
        proj_grad,
        proj_bias_grad,
        filter_grad,
        short_bias_grad,
        kernel_grad,
        skip_bias_grad,
        out_grad,
        out_bias_grad,
        second_gain_grad,
        second_bias_grad,
        up_grad,
        up_bias_grad,
        down_grad,
        down_bias_grad,
    )


def solution(mesh):
    return jax.shard_map(
        per_device,
        mesh=mesh,
        in_specs=(
            P("dp", "seq", None),
            P("dp"),
            P(),
            P(),
            P(),
            P(),
            P(),
            P(),
            P(None, "seq"),
            P(),
            P(),
            P(),
            P(),
            P(),
            P(),
            P(),
            P(),
            P(),
            P("dp", "seq", None),
        ),
        out_specs=(
            P("dp", "seq", None),
            P("dp", "seq", None),
            P("seq"),
            P("seq"),
            P("seq", None),
            P("seq"),
            P("seq", None),
            P("seq"),
            P("seq", None),
            P("seq"),
            P("seq", None),
            P("seq"),
            P("seq"),
            P("seq"),
            P("seq", None),
            P("seq"),
            P("seq", None),
            P("seq"),
        ),
        check_vma=False,
    )
```

profile of v0, /device:TPU:0, one launch (start us, length us, event | category | flops | bytes accessed | tf_op | source)
XLA Modules:
  0.0 1239.6 jit_solution(8293341268720507816)
XLA Ops:
  35.8 10.6 add_add_fusion
  72.7 58.5 %all-to-all-done = f32[8,768,128]{2,0,1:T(8,128)} async-done(((f32[8,768,128]{2,0,1:T(8,128)}), f32[8,768,128]{2,0,1:T(8,128)}, u32[]{:S(2)}, u32[]{:S(2)}) %all-to-all-start) | async-done | bytes 3145760 | tf_op jit(solution)/shard_map/all_to_all | solution.py:122
  171.8 16.1 %fusion.12 = (f32[768,16,128]{2,0,1:T(8,128)}, f32[768,16,128]{2,0,1:T(8,128)}, f32[768,16,128]{2,0,1:T(8,128)}) fusion(f32[768,16,128]{2,0,1:T(8,128)S(1)} %fusion.65, f32[96,16,128]{2,0,1:T(8,128)S(1)} %copy-done.14, f32[96,16,128]{2,0,1:T(8,128)S(1)} %copy-done.15, f32[768,16,128]{2,0,1:T(8,128)} %fusion.31, f32[768,16,128]{2,1,0:T(8,128)} %copy-done.6), kind=kOutput, calls=%fused_computation.37 | convolution fusion | flops 2427158528 | bytes 39321600 | tf_op jit(solution)/shard_map/rkc,cm->rkm/dot_general | solution.py:52
  213.1 12.5 %multiply_subtract_fusion.2 = (f32[768,16,128]{2,0,1:T(8,128)S(1)}, f32[768,16,128]{2,0,1:T(8,128)}) fusion(f32[16,128]{1,0:T(8,128)S(1)} %get-tuple-element.96, f32[16,128]{1,0:T(8,128)S(1)} %get-tuple-element.97, f32[768,16,128]{2,0,1:T(8,128)} %fusion.147, f32[768,16,128]{2,0,1:T(8,128)} %fusion.149, f32[768,16,128]{2,0,1:T(8,128)} %fusion.133, ...), kind=kOutput, calls=%fused_computation.55 | convolution fusion | flops 2428731392 | bytes 37765120 | tf_op jit(solution)/shard_map/rkm,cm->rkc/dot_general | solution.py:61
  225.6 11.1 fusion.19
  254.7 97.5 %all_to_all.81 = f32[8,96,1024]{1,0,2:T(8,128)} all-to-all(f32[8,96,1024]{1,0,2:T(8,128)} %copy.96), channel_id=1, replica_groups=mesh['dp'=4,'seq'=8] {'seq'}, dimensions={2} | all-to-all | bytes 6291456 | tf_op jit(solution)/shard_map/all_to_all | solution.py:142
  368.7 11.1 fusion.49
  379.8 15.9 %convert_reduce_fusion = (f32[3072]{0:T(1024)}, bf16[8,128,3072]{2,1,0:T(8,128)(2,1)S(1)}) fusion(f32[8,128,3072]{2,1,0:T(8,128)} %fusion.49, f32[3072]{0:T(1024)S(1)} %copy-done.54, bf16[8,128,768]{2,1,0:T(8,128)(2,1)S(1)} %copy-done.18, bf16[3072,768]{1,0:T(8,128)(2,1)} %param.35), kind=kOutput, calls=%fused_computation.17 | convolution fusion | flops 4904186880 | bytes 25190400 | tf_op jit(solution)/shard_map/stj,ij->sti/dot_general | solution.py:170
  395.7 10.9 multiply_reduce_fusion.3
  415.0 13.8 %convolution_bitcast_fusion = f32[3072,768]{1,0:T(8,128)} fusion(bf16[8,128,768]{2,1,0:T(8,128)(2,1)} %param.37, f32[8,128,3072]{2,1,0:T(8,128)} %fusion.49, f32[3072]{0:T(1024)} %param.34), kind=kOutput, calls=%fused_computation.74 | convolution fusion | flops 4863295488 | bytes 23605248 | tf_op jit(solution)/shard_map/sti,stj->ij/dot_general | solution.py:166
  428.8 10.7 multiply_reduce_fusion.4
  447.6 11.0 convolution_bitcast_fusion.1
  458.9 67.9 %all-to-all-done.3 = f32[8,768,128]{2,0,1:T(8,128)} async-done(((f32[8,768,128]{2,0,1:T(8,128)}), f32[8,768,128]{2,0,1:T(8,128)}, u32[]{:S(2)}, u32[]{:S(2)}) %all-to-all-start.3) | async-done | bytes 3145760 | tf_op jit(solution)/shard_map/all_to_all | solution.py:193
  569.0 24.1 %multiply_subtract_fusion = (f32[768,16,128]{2,0,1:T(8,128)}, f32[768,16,128]{2,0,1:T(8,128)}, f32[768,16,128]{2,0,1:T(8,128)}, f32[768,16,128]{2,0,1:T(8,128)}) fusion(f32[768,16,128]{2,0,1:T(8,128)} %get-tuple-element.89, f32[768,16,128]{2,0,1:T(8,128)} %copy-done.2, f32[768,16,128]{2,0,1:T(8,128)} %fusion.74, f32[96,16,128]{2,0,1:T(8,128)} %copy.93, ...), kind=kOutput, calls=%fused_computation.48 | convolution fusion | flops 2436595712 | bytes 58195968 | tf_op jit(solution)/shard_map/rkc,cm->rkm/dot_general | solution.py:47
  593.1 10.2 fusion.141
  618.1 12.7 %multiply_subtract_fusion.1 = (f32[768,16,128]{2,0,1:T(8,128)S(1)}, f32[768,16,128]{2,0,1:T(8,128)}) fusion(f32[16,128]{1,0:T(8,128)S(1)} %get-tuple-element.96, f32[16,128]{1,0:T(8,128)S(1)} %get-tuple-element.97, f32[768,16,128]{2,0,1:T(8,128)} %fusion.141, f32[768,16,128]{2,0,1:T(8,128)} %fusion.143, f32[768,16,128]{2,0,1:T(8,128)} %fusion.127, ...), kind=kOutput, calls=%fused_computation.51 | convolution fusion | flops 2428731392 | bytes 37765120 | tf_op jit(solution)/shard_map/rkm,cm->rkc/dot_general | solution.py:61
  630.8 11.2 fusion.15
  660.7 181.2 %all_to_all.82 = f32[8,96,1024]{1,0,2:T(8,128)} all-to-all(f32[8,96,1024]{1,0,2:T(8,128)} %copy.109), channel_id=1, replica_groups=mesh['dp'=4,'seq'=8] {'seq'}, dimensions={2} | all-to-all | bytes 6291456 | tf_op jit(solution)/shard_map/all_to_all | solution.py:213
  882.3 18.1 %multiply_reduce_fusion.2 = (f32[2304]{0:T(1024)}, f32[2304]{0:T(1024)}, f32[2304]{0:T(1024)}, f32[2304]{0:T(1024)}, f32[2304]{0:T(1024)}, /*index=5*/bf16[8,128,2304]{2,1,0:T(8,128)(2,1)}) fusion(f32[8,128,2304]{2,1,0:T(8,128)} %copy-done.10, f32[8,2,2304]{2,1,0:T(2,128)} %collective-permute-done, f32[8,128,768]{2,1,0:T(8,128)} %get-tuple-element.73, ...), kind=kLoop, calls=%fused_computation.32 | loop fusion | flops 44815104 | bytes 42688512 | tf_op jit(solution)/shard_map/reduce_sum | solution.py:228
  912.2 13.9 %add_add_fusion.4 = f32[8,128,768]{2,1,0:T(8,128)} fusion(f32[8,128,768]{2,1,0:T(8,128)} %copy-done.11, bf16[3072,768]{1,0:T(8,128)(2,1)} %param.35, f32[768]{0:T(1024)} %param.36, f32[8,128,3072]{2,1,0:T(8,128)} %fusion.49, f32[3072]{0:T(1024)} %param.34), kind=kOutput, calls=%fused_computation.116 | convolution fusion | flops 4864868352 | bytes 23608320 | tf_op jit(solution)/shard_map/sti,ij->stj/dot_general | solution.py:162
  952.8 118.9 %reduce-scatter.8.cloned.1.call-done = f32[96,2304]{1,0:T(8,128)} async-done(((f32[768,2304]{1,0:T(8,128)}), f32[96,2304]{1,0:T(8,128)}) %reduce-scatter.8.cloned.1.call-update) | async-done | bytes 884752 | tf_op jit(solution)/shard_map/reduce_scatter | solution.py:261
  1084.5 37.0 %all-reduce.10 = (f32[768]{0:T(1024)}, f32[768]{0:T(1024)}, f32[2304]{0:T(1024)}, f32[2304]{0:T(1024)}, f32[768]{0:T(1024)}, /*index=5*/f32[768]{0:T(1024)}, f32...) all-reduce(f32[768]{0:T(1024)} %get-tuple-element.24, ...), channel_id=2, replica_groups=mesh['dp'=4,'seq'=8] {'seq'}, use_global_device_ids=true, to_apply=%region_9.10.clone | all-reduce | flops 13056 | bytes 104448
  1140.0 11.8 all-reduce.11
  1151.8 71.6 %all-reduce.15.cloned.1.call-done = (f32[96,2304]{1,0:T(8,128)}, f32[96,1024]{1,0:T(8,128)}, f32[96,768]{1,0:T(8,128)}, f32[96,3072]{1,0:T(8,128)}, f32[384,768]{1,0:T(8,128)}) async-done(((f32[96,2304]{1,0:T(8,128)}, f32[96,1024]{1,0:T(8,128)}, f32[96,768]{1,0:T(8,128)}, f32[96,3072]{1,0:T(8,128)}, f32[384,768]{1,0:T(8,128)}), (f32[96,2304]{1,0:T(8,128)}, f32[96,1024]{1,0:T(8,128)}, f32[96,768]{1,0:T(8,128)}, ...) | async-done | bytes 3932176 | tf_op jit(solution)/shard_map/psum | solution.py:292
  (245 shorter events, 364.2 us)
Async XLA Ops:
  7.2 48.5 %all-to-all-start.1 = ((f32[1,768,128]{2,0,1:T(1,128)}), f32[1,768,128]{2,0,1:T(1,128)}, u32[]{:S(2)}, u32[]{:S(2)}) async-start(f32[1,768,128]{2,0,1:T(1,128)} %bitcast.270), calls=%async_computation.1 | async-start | bytes 786432 | tf_op jit(solution)/shard_map/all_to_all | solution.py:123
  19.0 16.8 %copy-start.52 = (f32[2304]{0:T(1024)S(1)}, f32[2304]{0:T(1024)}, u32[]{:S(2)}) copy-start(f32[2304]{0:T(1024)} %param.26) | copy-start | bytes 27652
  28.9 6.9 collective-permute-start
  55.7 75.5 %all-to-all-start = ((f32[8,768,128]{2,0,1:T(8,128)}), f32[8,768,128]{2,0,1:T(8,128)}, u32[]{:S(2)}, u32[]{:S(2)}) async-start(f32[8,768,128]{2,0,1:T(8,128)} %copy.84), calls=%async_computation | async-start | bytes 6291456 | tf_op jit(solution)/shard_map/all_to_all | solution.py:122
  62.1 890.6 %reduce-scatter.10.cloned.1.call-start = ((), (), s32[]{:S(2)}) async-start(), calls=%async_computation.11 | async-start | bytes 2654208 | tf_op jit(solution)/shard_map/reduce_scatter | solution.py:266
  147.8 16.5 %copy-start.6 = (f32[768,16,128]{2,1,0:T(8,128)}, f32[768,16,128]{2,1,0:T(8,128)S(1)}, u32[]{:S(2)}) copy-start(f32[768,16,128]{2,1,0:T(8,128)S(1)} %get-tuple-element.80) | copy-start | bytes 18874372
  187.9 17.4 %slice-start.2 = ((s8[6291456]{0:T(1024)(128)(4,1)}), s8[4194304]{0:T(1024)(128)(4,1)S(1)}, s32[]{:S(2)}) async-start(s8[6291456]{0:T(1024)(128)(4,1)} %bitcast.255), calls=%async_computation.18 | async-start | bytes 8388608
  368.2 38.4 %copy-start.11 = (f32[8,128,768]{2,1,0:T(8,128)}, f32[8,128,768]{2,1,0:T(8,128)S(1)}, u32[]{:S(2)}) copy-start(f32[8,128,768]{2,1,0:T(8,128)S(1)} %get-tuple-element.91) | copy-start | bytes 9437188
  368.2 38.4 %copy-start.30 = (f32[8,128]{1,0:T(8,128)}, f32[8,128]{1,0:T(8,128)S(1)}, u32[]{:S(2)}) copy-start(f32[8,128]{1,0:T(8,128)S(1)} %broadcast_multiply_fusion) | copy-start | bytes 12292
  368.7 37.9 %copy-start.31 = (f32[8,128]{1,0:T(8,128)}, f32[8,128]{1,0:T(8,128)S(1)}, u32[]{:S(2)}) copy-start(f32[8,128]{1,0:T(8,128)S(1)} %fusion.215) | copy-start | bytes 12292
  415.0 537.8 %reduce-scatter.14.cloned.1.call-start = ((), (), s32[]{:S(2)}) async-start(), calls=%async_computation.13 | async-start | bytes 10616832 | tf_op jit(solution)/shard_map/reduce_scatter | solution.py:272
  443.1 83.7 %all-to-all-start.3 = ((f32[8,768,128]{2,0,1:T(8,128)}), f32[8,768,128]{2,0,1:T(8,128)}, u32[]{:S(2)}, u32[]{:S(2)}) async-start(f32[8,768,128]{2,0,1:T(8,128)} %copy.100), calls=%async_computation.3 | async-start | bytes 6291456 | tf_op jit(solution)/shard_map/all_to_all | solution.py:193
  447.6 505.2 %reduce-scatter.12.cloned.1.call-start = ((), (), s32[]{:S(2)}) async-start(), calls=%async_computation.12 | async-start | bytes 10616832 | tf_op jit(solution)/shard_map/reduce_scatter | solution.py:270
  458.7 612.9 %reduce-scatter.8.cloned.1.call-start = ((), (), s32[]{:S(2)}) async-start(), calls=%async_computation.10 | async-start | bytes 7962624 | tf_op jit(solution)/shard_map/reduce_scatter | solution.py:261
  543.1 16.6 %copy-start.5 = (f32[768,16,128]{2,1,0:T(8,128)}, f32[768,16,128]{2,1,0:T(8,128)S(1)}, u32[]{:S(2)}) copy-start(f32[768,16,128]{2,1,0:T(8,128)S(1)} %get-tuple-element.78) | copy-start | bytes 18874372
  593.1 17.6 %slice-start = ((s8[6291456]{0:T(1024)(128)(4,1)}), s8[4194304]{0:T(1024)(128)(4,1)S(1)}, s32[]{:S(2)}) async-start(s8[6291456]{0:T(1024)(128)(4,1)} %bitcast.253), calls=%async_computation.16 | async-start | bytes 8388608
  868.2 9.9 collective-permute-start.1
  882.3 18.1 %copy-start.8 = (bf16[8,128,768]{2,1,0:T(8,128)(2,1)S(1)}, bf16[8,128,768]{2,1,0:T(8,128)(2,1)}, u32[]{:S(2)}) copy-start(bf16[8,128,768]{2,1,0:T(8,128)(2,1)} %param.19) | copy-start | bytes 4718596
  882.3 18.1 %copy-start.25 = (f32[8,128]{1,0:T(8,128)S(1)}, f32[8,128]{1,0:T(8,128)}, u32[]{:S(2)}) copy-start(f32[8,128]{1,0:T(8,128)} %copy-done.24) | copy-start | bytes 12292
  882.3 18.1 %copy-start.28 = (f32[8,128]{1,0:T(8,128)S(1)}, f32[8,128]{1,0:T(8,128)}, u32[]{:S(2)}) copy-start(f32[8,128]{1,0:T(8,128)} %copy-done.27) | copy-start | bytes 12292
  882.3 18.1 %copy-start.34 = (f32[768]{0:T(1024)S(1)}, f32[768]{0:T(1024)}, u32[]{:S(2)}) copy-start(f32[768]{0:T(1024)} %param.21) | copy-start | bytes 9220
  882.3 18.1 %copy-start.43 = (f32[768]{0:T(1024)S(1)}, f32[768]{0:T(1024)}, u32[]{:S(2)}) copy-start(f32[768]{0:T(1024)} %param.22) | copy-start | bytes 9220
  909.0 230.1 %reduce-scatter.16.cloned.1.call-start = ((), (), s32[]{:S(2)}) async-start(), calls=%async_computation.14 | async-start | bytes 1327104
  949.5 273.9 %all-reduce.15.cloned.1.call-start = ((), (), s32[]{:S(2)}) async-start(), calls=%async_computation.15 | async-start | bytes 7864320 | tf_op jit(solution)/shard_map/psum | solution.py:292
  (47 other events, 375.8 us)
Sparse Core Ops, SparseCore 0:
  415.1 104.6 reduce-scatter.9
  523.4 200.2 reduce-scatter.13
  727.3 212.6 reduce-scatter.11
  943.5 128.0 reduce-scatter.7
  1075.8 63.1 reduce-scatter.15
  1142.4 81.0 all-reduce.14
where the time goes:
time: 1250 us; the launch traced here: 1240 us
  matrix products  365 us (29%)
  waiting for transfers between devices  332 us (27%)
  blocking collectives  328 us (26%)
  local copies, waits for them, and re-layouts  93.8 us (8%)
  other arithmetic  78 us (6%)
  starting transfers between devices  25.2 us (2%)
  between operations  17.2 us (1%)
    all_to_all x1, blocking collectives, per_device(): lax.all_to_all(gated_back_chan, 'seq', split_axis=2, concat_axis=1, tiled...  181 us
    reduce_scatter x1, waiting for transfers between devices, per_device(): lax.psum_scatter(proj_grad, 'seq', scatter_dimension=0, tiled=True)  119 us
    all_to_all x1, blocking collectives, per_device(): lax.all_to_all(conv_chan, 'seq', split_axis=2, concat_axis=1, tiled=True)  97.5 us
    psum x1, waiting for transfers between devices, per_device(): lax.psum((norm_gain_share, norm_bias_share, proj_share, proj_bias_share,...  71.6 us
    all_to_all x1, waiting for transfers between devices, per_device(): lax.all_to_all(jnp.swapaxes(conv_grad, 1, 2), 'seq', split_axis=1, concat...  67.9 us
    all_to_all x1, waiting for transfers between devices, per_device(): lax.all_to_all(jnp.swapaxes(gated, 1, 2), 'seq', split_axis=1, concat_axi...  58.5 us
    unnamed x139, local copies, waits for them, and re-layouts  37 us
    unnamed x1, blocking collectives  37 us
  transfers between devices with their start and end apart: 11, of which 7 were waited for; matrix products, arithmetic and copies ran while one was open for 27% of the time, Pallas kernels for 0%

commit v1 on v0

--- a/solution.py
+++ b/solution.py
@@ -1,12 +1,18 @@
+import functools
 import math
 
 import jax
 import jax.numpy as jnp
+import ml_dtypes
+import numpy as np
 from jax import lax
+from jax.experimental import pallas as pl
+from jax.experimental.pallas import tpu as pltpu
 from jax.sharding import PartitionSpec as P
 
 EPSILON = 1e-05
 PRECISE = lax.Precision.HIGHEST
+NO_COST = pl.CostEstimate(flops=0, bytes_accessed=0, transcendentals=0)
 
 
 def passed_along(array, axis, by):
@@ -70,7 +76,7 @@
     return signal / total
 
 
-def per_device(
+def by_channels(
     tokens,
     offsets,
     norm_gain,
@@ -332,6 +338,895 @@
     )
 
 
+def block_tables(width):
+    def stacked(matrix):
+        high = matrix.astype(np.float32).astype(ml_dtypes.bfloat16)
+        low = (matrix - high.astype(np.float64)).astype(ml_dtypes.bfloat16)
+        return np.concatenate([high, high, low], axis=1)
+
+    odd = 2 * np.arange(width) + 1
+    angles = np.pi / (2 * width) * (odd[:, None] * np.arange(width)[None, :] % (4 * width))
+    analysis = np.concatenate([np.cos(angles), -np.sin(angles)], axis=0)
+    angles = np.pi / (2 * width) * (np.arange(2 * width)[:, None] * odd[None, :] % (4 * width))
+    synthesis = np.concatenate([np.cos(angles), -np.sin(angles)], axis=1) / width
+    return stacked(analysis), stacked(synthesis)
+
+
+def in_parts(values):
+    high = values.astype(jnp.bfloat16)
+    low = (values - high.astype(jnp.float32)).astype(jnp.bfloat16)
+    return high, low
+
+
+def earlier(values, by):
+    rows = lax.broadcasted_iota(jnp.int32, values.shape, 0)
+    return jnp.where(rows >= by, pltpu.roll(values, by, 0), 0.0)
+
+
+def later(values, by):
+    count = values.shape[0]
+    rows = lax.broadcasted_iota(jnp.int32, values.shape, 0)
+    return jnp.where(rows < count - by, pltpu.roll(values, count - by, 0), 0.0)
+
+
+def short_filtered(mixed, taps):
+    return (
+        taps[0:1] * earlier(mixed, 2) + taps[1:2] * earlier(mixed, 1) + taps[2:3] * mixed + taps[3:4]
+    )
+
+
+def analyse(signal, table_ref, spectra_ref):
+    blocks, double, lanes = spectra_ref.shape
+    width = double // 2
+    high, low = in_parts(signal)
+    for first in range(0, blocks, 2):
+        columns = []
+        for block in (first, first + 1):
+            rows = slice(block * width, (block + 1) * width)
+            columns.append(jnp.concatenate([high[rows], low[rows], high[rows]], axis=0))
+        found = jnp.dot(
+            table_ref[...], jnp.concatenate(columns, axis=1), preferred_element_type=jnp.float32
+        )
+        spectra_ref[first] = found[:, :lanes]
+        spectra_ref[first + 1] = found[:, lanes:]
+
+
+def analyse_kernel(kernel_ref, table_ref, spectra_ref):
+    blocks, double, lanes = spectra_ref.shape
+    for first in range(0, blocks, 2):
+        rows = []
+        for block in (first, first + 1):
+            high, low = in_parts(kernel_ref[block])
+            rows.append(jnp.concatenate([high, low, high], axis=1))
+        found = lax.dot_general(
+            table_ref[...],
+            jnp.concatenate(rows, axis=0),
+            (((1,), (1,)), ((), ())),
+            preferred_element_type=jnp.float32,
+        )
+        spectra_ref[first] = found[:, :lanes]
+        spectra_ref[first + 1] = found[:, lanes:]
+
+
+def synthesise(spectra_ref, table_ref):
+    blocks, double, lanes = spectra_ref.shape
+    found = []
+    for first in range(0, blocks, 2):
+        columns = []
+        for block in (first, first + 1):
+            high, low = in_parts(spectra_ref[block])
+            columns.append(jnp.concatenate([high, low, high], axis=0))
+        pair = jnp.dot(
+            table_ref[...], jnp.concatenate(columns, axis=1), preferred_element_type=jnp.float32
+        )
+        found.append(pair[:, :lanes])
+        found.append(pair[:, lanes:])
+    return found
+
+
+def multiply(left_ref, right_ref, out_ref, reverse):
+    blocks, double, lanes = out_ref.shape
+    width = double // 2
+
+    def step(index, carry):
+        real_rows = pl.ds(pl.multiple_of(index * 8, 8), 8)
+        imag_rows = pl.ds(pl.multiple_of(width + index * 8, 8), 8)
+        left_real = [left_ref[block, real_rows] for block in range(blocks)]
+        left_imag = [left_ref[block, imag_rows] for block in range(blocks)]
+        right_real = [right_ref[block, real_rows] for block in range(blocks)]
+        right_imag = [right_ref[block, imag_rows] for block in range(blocks)]
+        for m in range(blocks):
+            real = imag = None
+            for l in range(blocks - m if reverse else m + 1):
+                r = m + l if reverse else m - l
+                if reverse:
+                    new_real = left_real[l] * right_real[r] + left_imag[l] * right_imag[r]
+                    new_imag = left_real[l] * right_imag[r] - left_imag[l] * right_real[r]
+                else:
+                    new_real = left_real[l] * right_real[r] - left_imag[l] * right_imag[r]
+                    new_imag = left_real[l] * right_imag[r] + left_imag[l] * right_real[r]
+                real = new_real if real is None else real + new_real
+                imag = new_imag if imag is None else imag + new_imag
+            out_ref[m, real_rows] = real
+            out_ref[m, imag_rows] = imag
+        return carry
+
+    lax.fori_loop(0, width // 8, step, 0)
+
+
+def gates(start_ref, mixed_refs, taps_ref):
+    outer, inner, values = [
+        short_filtered(ref[...], taps_ref[group]) for group, ref in enumerate(mixed_refs)
+    ]
+    rows = lax.broadcasted_iota(jnp.int32, outer.shape, 0)
+    live = (rows >= start_ref[0]).astype(jnp.float32)
+    return outer, inner, values, live
+
+
+def forward_kernel(
+    start_ref,
+    outer_ref,
+    inner_ref,
+    value_ref,
+    kernel_ref,
+    taps_ref,
+    skip_ref,
+    analysis_ref,
+    synthesis_ref,
+    convolved_ref,
+    branch_ref,
+    signal_spectra,
+    kernel_spectra,
+    spectra,
+):
+    width = kernel_ref.shape[2]
+    outer, inner, values, live = gates(start_ref, (outer_ref, inner_ref, value_ref), taps_ref)
+    gated = values * inner * live
+    analyse(gated, analysis_ref, signal_spectra)
+    analyse_kernel(kernel_ref, analysis_ref, kernel_spectra)
+    multiply(kernel_spectra, signal_spectra, spectra, False)
+    found = synthesise(spectra, synthesis_ref)
+    pieces = [found[0][:width]]
+    for block in range(1, len(found)):
+        pieces.append(found[block][:width] + found[block - 1][width:])
+    convolved = jnp.concatenate(pieces, axis=0) + gated * skip_ref[...]
+    convolved_ref[...] = convolved
+    branch_ref[...] = (convolved * outer).astype(jnp.bfloat16)
+
+
+def lag_blocks(found, width):
+    pieces = []
+    for block in range(len(found)):
+        piece = found[block][:width]
+        if block + 1 < len(found):
+            piece = piece - found[block + 1][width:]
+        pieces.append(piece)
+    return pieces
+
+
+def backward_kernel(
+    start_ref,
+    grad_ref,
+    convolved_ref,
+    outer_ref,
+    inner_ref,
+    value_ref,
+    kernel_ref,
+    taps_ref,
+    skip_ref,
+    analysis_ref,
+    synthesis_ref,
+    mixed_grad_ref,
+    kernel_grad_ref,
+    sums_ref,
+    signal_spectra,
+    kernel_spectra,
+    grad_spectra,
+    spectra,
+):
+    width = kernel_ref.shape[2]
+    mixed_refs = (outer_ref, inner_ref, value_ref)
+    outer, inner, values, live = gates(start_ref, mixed_refs, taps_ref)
+    gated = values * inner * live
+    branch_grad = grad_ref[...]
+    conv_grad = branch_grad * outer
+    outer_grad = branch_grad * convolved_ref[...]
+    analyse(gated, analysis_ref, signal_spectra)
+    analyse_kernel(kernel_ref, analysis_ref, kernel_spectra)
+    analyse(conv_grad, analysis_ref, grad_spectra)
+    multiply(signal_spectra, grad_spectra, spectra, True)
+    lags = lag_blocks(synthesise(spectra, synthesis_ref), width)
+    half = len(lags) // 2
+    for block, piece in enumerate(lags):
+        first = block % half * width
+        kernel_grad_ref[block // half, :, first : first + width] = piece.T
+    multiply(kernel_spectra, grad_spectra, spectra, True)
+    back = jnp.concatenate(lag_blocks(synthesise(spectra, synthesis_ref), width), axis=0)
+    gated_grad = (back + conv_grad * skip_ref[...]) * live
+
+    def total(array):
+        return jnp.sum(array, axis=0, keepdims=True)
+
+    filter_rows, bias_rows, low_rows = [], [], []
+    grads = (outer_grad, gated_grad * values, gated_grad * inner)
+    for group in range(3):
+        grad, mixed, taps = grads[group], mixed_refs[group][...], taps_ref[group]
+        next_one, next_two = later(grad, 1), later(grad, 2)
+        mixed_grad = taps[2:3] * grad + taps[1:2] * next_one + taps[0:1] * next_two
+        low = mixed_grad.astype(jnp.bfloat16)
+        mixed_grad_ref[group] = low
+        filter_rows += [total(next_two * mixed), total(next_one * mixed), total(grad * mixed)]
+        bias_rows.append(total(grad))
+        low_rows.append(total(low.astype(jnp.float32)))
+    rows = filter_rows + bias_rows + low_rows + [total(conv_grad * gated)]
+    sums_ref[...] = jnp.concatenate(rows, axis=0)
+
+
+def kernel_parameters():
+    return pltpu.CompilerParams(
+        vmem_limit_bytes=56 * 1024 * 1024
+    )
+
+
+def kernel_specs(tokens, parts, width, lanes, features):
+    groups = features // lanes
+
+    def mixed(group):
+        return pl.BlockSpec((tokens, lanes), lambda tile, *_: (0, group * groups + tile))
+
+    return (
+        [pl.BlockSpec(memory_space=pltpu.SMEM)],
+        [mixed(0), mixed(1), mixed(2)],
+        [
+            pl.BlockSpec((parts, lanes, width), lambda tile, *_: (0, tile, 0)),
+            pl.BlockSpec((3, 4, lanes), lambda tile, *_: (0, 0, tile)),
+            pl.BlockSpec((1, lanes), lambda tile, *_: (0, tile)),
+            pl.BlockSpec((2 * width, 3 * width), lambda *_: (0, 0)),
+            pl.BlockSpec((2 * width, 6 * width), lambda *_: (0, 0)),
+        ],
+        pl.BlockSpec((tokens, lanes), lambda tile, *_: (0, tile)),
+        pltpu.VMEM((parts, 2 * width, lanes), jnp.float32),
+    )
+
+
+def forward_convolution(start, mixed, kernel, taps, skip, tables, lanes=128):
+    parts, features, width = kernel.shape
+    tokens = mixed.shape[0]
+    start_spec, mixed_specs, rest, plain, spectra = kernel_specs(tokens, parts, width, lanes, features)
+    return pl.pallas_call(
+        forward_kernel,
+        grid=(features // lanes,),
+        in_specs=start_spec + mixed_specs + rest,
+        out_specs=(plain, plain),
+        out_shape=(
+            jax.ShapeDtypeStruct((tokens, features), jnp.float32),
+            jax.ShapeDtypeStruct((tokens, features), jnp.bfloat16),
+        ),
+        scratch_shapes=[spectra] * 3,
+        compiler_params=kernel_parameters(),
+        cost_estimate=NO_COST,
+        name="forward_convolution",
+    )(start, mixed, mixed, mixed, kernel, taps, skip, *tables)
+
+
+def backward_convolution(start, grad, convolved, mixed, kernel, taps, skip, tables, lanes=128):
+    parts, features, width = kernel.shape
+    tokens = mixed.shape[0]
+    start_spec, mixed_specs, rest, plain, spectra = kernel_specs(tokens, parts, width, lanes, features)
+    return pl.pallas_call(
+        backward_kernel,
+        grid=(features // lanes,),
+        in_specs=start_spec + [plain, plain] + mixed_specs + rest,
+        out_specs=(
+            pl.BlockSpec((3, tokens, lanes), lambda tile: (0, 0, tile)),
+            pl.BlockSpec((2, lanes, tokens // 2), lambda tile: (0, tile, 0)),
+            pl.BlockSpec((16, lanes), lambda tile: (0, tile)),
+        ),
+        out_shape=(
+            jax.ShapeDtypeStruct((3, tokens, features), jnp.bfloat16),
+            jax.ShapeDtypeStruct((2, features, tokens // 2), jnp.float32),
+            jax.ShapeDtypeStruct((16, features), jnp.float32),
+        ),
+        scratch_shapes=[spectra] * 4,
+        compiler_params=kernel_parameters(),
+        cost_estimate=NO_COST,
+        name="backward_convolution",
+    )(start, grad, convolved, mixed, mixed, mixed, kernel, taps, skip, *tables)
+
+
+def unit_rows(values):
+    centered = values - jnp.mean(values, axis=-1, keepdims=True)
+    spread = lax.rsqrt(jnp.mean(centered * centered, axis=-1, keepdims=True) + EPSILON)
+    return centered * spread, spread
+
+
+def unit_rows_back(grad, unit, spread, gain):
+    scaled = grad * gain
+    inner = scaled - jnp.mean(scaled, axis=-1, keepdims=True)
+    return (inner - unit * jnp.mean(scaled * unit, axis=-1, keepdims=True)) * spread
+
+
+def matmul(left, right):
+    return jnp.dot(left, right, preferred_element_type=jnp.float32)
+
+
+def matmul_back(left, right):
+    return lax.dot_general(left, right, (((1,), (1,)), ((), ())), preferred_element_type=jnp.float32)
+
+
+def column_pair(array):
+    half = array.shape[1] // 2
+    return array[:, :half], array[:, half:]
+
+
+def column_sums(array):
+    return jnp.sum(array, axis=0, keepdims=True)
+
+
+def project_kernel(x_ref, gain_ref, bias_ref, weight_ref, offset_ref, normed_ref, mixed_ref):
+    unit, _ = unit_rows(x_ref[...])
+    normed = (unit * gain_ref[...] + bias_ref[...]).astype(jnp.bfloat16)
+    normed_ref[...] = normed
+    mixed_ref[...] = matmul(normed, weight_ref[...]) + offset_ref[...]
+
+
+def feed_kernel(
+    x_ref,
+    branch_ref,
+    out_weight_ref,
+    out_bias_ref,
+    gain_ref,
+    bias_ref,
+    up_weight_ref,
+    up_bias_ref,
+    down_weight_ref,
+    down_bias_ref,
+    residual_ref,
+    normed_ref,
+    activated_ref,
+    slope_ref,
+    *output_refs,
+):
+    residual = x_ref[...] + matmul(branch_ref[...], out_weight_ref[...]) + out_bias_ref[...]
+    residual_ref[...] = residual
+    unit, _ = unit_rows(residual)
+    normed = (unit * gain_ref[...] + bias_ref[...]).astype(jnp.bfloat16)
+    normed_ref[...] = normed
+    total = residual + down_bias_ref[...]
+    factor = math.sqrt(2.0 / math.pi)
+    chunk = residual.shape[1]
+    for first in range(0, up_weight_ref.shape[1], chunk):
+        columns = slice(first, first + chunk)
+        expanded = matmul(normed, up_weight_ref[:, columns]) + up_bias_ref[:, columns]
+        square = expanded * expanded
+        turned = jnp.tanh(factor * (expanded + 0.044715 * (square * expanded)))
+        half = 0.5 + 0.5 * turned
+        activated = (expanded * half).astype(jnp.bfloat16)
+        activated_ref[:, columns] = activated
+        slope_ref[:, columns] = half + (0.5 * factor) * expanded * (1.0 - turned * turned) * (
+            1.0 + (3 * 0.044715) * square
+        )
+        total = total + matmul(activated, down_weight_ref[columns, :])
+    for ref, half in zip(output_refs, column_pair(total)):
+        ref[...] = half
+
+
+def feed_back_kernel(
+    grad_ref,
+    residual_ref,
+    slope_ref,
+    gain_ref,
+    out_weight_ref,
+    up_weight_ref,
+    down_weight_ref,
+    expanded_ref,
+    residual_grad_ref,
+    residual_low_ref,
+    branch_grad_ref,
+    sums_ref,
+    wide_sums_ref,
+):
+    grad = grad_ref[...]
+    grad_low = grad.astype(jnp.bfloat16)
+    chunk = grad.shape[1]
+    normed_grad = None
+    wide = []
+    for first in range(0, up_weight_ref.shape[1], chunk):
+        columns = slice(first, first + chunk)
+        expanded = matmul_back(grad_low, down_weight_ref[columns, :]) * slope_ref[:, columns]
+        low = expanded.astype(jnp.bfloat16)
+        expanded_ref[:, columns] = low
+        wide.append(column_sums(low.astype(jnp.float32)))
+        part = matmul_back(low, up_weight_ref[:, columns])
+        normed_grad = part if normed_grad is None else normed_grad + part
+    unit, spread = unit_rows(residual_ref[...])
+    residual_grad = grad + unit_rows_back(normed_grad, unit, spread, gain_ref[...])
+    residual_grad_ref[...] = residual_grad
+    low = residual_grad.astype(jnp.bfloat16)
+    residual_low_ref[...] = low
+    branch_grad_ref[...] = matmul_back(low, out_weight_ref[...])
+    sums = [
+        column_sums(normed_grad * unit),
+        column_sums(normed_grad),
+        column_sums(low.astype(jnp.float32)),
+        column_sums(grad),
+    ]
+
+    @pl.when(pl.program_id(0) == 0)
+    def _():
+        sums_ref[...] = jnp.zeros_like(sums_ref)
+        wide_sums_ref[...] = jnp.zeros_like(wide_sums_ref)
+
+    sums_ref[...] += jnp.concatenate(sums, axis=0)
+    wide_sums_ref[...] += jnp.concatenate(wide, axis=1)
+
+
+def input_grad_kernel(
+    mixed_ref, weight_ref, x_ref, gain_ref, residual_grad_ref, first_ref, second_ref, sums_ref
+):
+    features = x_ref.shape[1]
+    normed_grad = None
+    for group in range(3):
+        columns = slice(group * features, (group + 1) * features)
+        part = matmul_back(mixed_ref[group], weight_ref[:, columns])
+        normed_grad = part if normed_grad is None else normed_grad + part
+    unit, spread = unit_rows(x_ref[...])
+    total = residual_grad_ref[...] + unit_rows_back(normed_grad, unit, spread, gain_ref[...])
+    first_ref[...], second_ref[...] = column_pair(total)
+    sums = jnp.concatenate([column_sums(normed_grad * unit), column_sums(normed_grad)], axis=0)
+
+    @pl.when(pl.program_id(0) == 0)
+    def _():
+        sums_ref[...] = jnp.zeros_like(sums_ref)
+
+    sums_ref[...] += sums
+
+
+def by_rows(kernel, name, rows, inputs, outputs, height=256):
+    def spec(shape, held):
+        if len(shape) == 3:
+            return pl.BlockSpec((shape[0], height, shape[2]), lambda step: (0, step, 0))
+        if shape[0] == rows and not held:
+            return pl.BlockSpec((height, shape[1]), lambda step: (step, 0))
+        return pl.BlockSpec(shape, lambda step: (0, 0))
+
+    return pl.pallas_call(
+        kernel,
+        grid=(rows // height,),
+        in_specs=[spec(array.shape, held) for array, held in inputs],
+        out_specs=tuple(spec(shape, False) for shape, _ in outputs),
+        out_shape=tuple(jax.ShapeDtypeStruct(shape, kind) for shape, kind in outputs),
+        compiler_params=kernel_parameters(),
+        cost_estimate=NO_COST,
+        name=name,
+    )(*[array for array, _ in inputs])
+
+
+def product_kernel(half_ref, left_ref, right_ref, out_ref):
+    out_ref[...] = product_tile(left_ref, right_ref)
+
+
+def product_tile(left_ref, right_ref):
+    if len(right_ref.shape) == 2:
+        return product(left_ref[...], right_ref[...])
+    return jnp.concatenate(
+        [product(left_ref[...], right_ref[group]) for group in range(right_ref.shape[0])], axis=1
+    )
+
+
+def product_specs(left, right, tile):
+    tokens = left.shape[0]
+    half = right.shape[-1] // 2
+    left_spec = pl.BlockSpec((tokens, tile), lambda step, half_ref: (0, step))
+    if right.ndim == 2:
+        right_spec = pl.BlockSpec((tokens, half), lambda step, half_ref: (0, half_ref[0]))
+        return half, left_spec, right_spec
+    right_spec = pl.BlockSpec((right.shape[0], tokens, half), lambda step, half_ref: (0, 0, half_ref[0]))
+    return half * right.shape[0], left_spec, right_spec
+
+
+def half_product(left, right, half, tile=384):
+    rows = left.shape[1]
+    columns, left_spec, right_spec = product_specs(left, right, tile)
+    return pl.pallas_call(
+        product_kernel,
+        grid_spec=pltpu.PrefetchScalarGridSpec(
+            num_scalar_prefetch=1,
+            grid=(rows // tile,),
+            in_specs=[left_spec, right_spec],
+            out_specs=pl.BlockSpec((tile, columns), lambda step, half_ref: (step, 0)),
+        ),
+        out_shape=jax.ShapeDtypeStruct((rows, columns), jnp.float32),
+        compiler_params=kernel_parameters(),
+        cost_estimate=NO_COST,
+        name="half_product",
+    )(half, left, right)
+
+
+def parted_product_kernel(bits_ref, left_ref, right_ref, taken_ref, kept_ref, given_ref):
+    total = product_tile(left_ref, right_ref) + taken_ref[...]
+    pieces, rows, _ = kept_ref.shape
+    first = bits_ref[1] == 0
+    for piece in range(pieces):
+        one = total[2 * piece * rows : (2 * piece + 1) * rows]
+        two = total[(2 * piece + 1) * rows : (2 * piece + 2) * rows]
+        kept_ref[piece] = jnp.where(first, one, two)
+        given_ref[piece] = jnp.where(first, two, one)
+
+
+def parted_product(left, right, half, taken, which, pieces, tile=384):
+    rows = left.shape[1]
+    columns, left_spec, right_spec = product_specs(left, right, tile)
+    height = rows // (2 * pieces)
+    steps = rows // tile
+    part = pl.BlockSpec((pieces // steps, height, columns), lambda step, bits_ref: (step, 0, 0))
+    shape = jax.ShapeDtypeStruct((pieces, height, columns), jnp.float32)
+    return pl.pallas_call(
+        parted_product_kernel,
+        grid_spec=pltpu.PrefetchScalarGridSpec(
+            num_scalar_prefetch=1,
+            grid=(steps,),
+            in_specs=[
+                left_spec,
+                right_spec,
+                pl.BlockSpec((tile, columns), lambda step, bits_ref: (step, 0)),
+            ],
+            out_specs=(part, part),
+        ),
+        out_shape=(shape, shape),
+        compiler_params=kernel_parameters(),
+        cost_estimate=NO_COST,
+        name="parted_product",
+    )(jnp.concatenate([half, which]), left, right, taken)
+
+
+def fold_kernel(bit_ref, kept_ref, taken_ref, kept_out_ref, given_out_ref):
+    total = kept_ref[...] + taken_ref[...]
+    first = bit_ref[0] == 0
+    kept_out_ref[0] = jnp.where(first, total[0], total[1])
+    given_out_ref[0] = jnp.where(first, total[1], total[0])
+
+
+def fold(kept, taken, which):
+    count, rows, columns = kept.shape
+    pair = pl.BlockSpec((2, rows, columns), lambda step: (step, 0, 0))
+    one = pl.BlockSpec((1, rows, columns), lambda step: (step, 0, 0))
+    shape = jax.ShapeDtypeStruct((count // 2, rows, columns), jnp.float32)
+    return pl.pallas_call(
+        fold_kernel,
+        grid=(count // 2,),
+        in_specs=[pl.BlockSpec(memory_space=pltpu.SMEM), pair, pair],
+        out_specs=(one, one),
+        out_shape=(shape, shape),
+        compiler_params=kernel_parameters(),
+        cost_estimate=NO_COST,
+        name="fold",
+    )(which, kept, taken)
+
+
+def swapped(array, axis, by):
+    count = lax.axis_size(axis)
+    return lax.ppermute(array, axis, [(i, i ^ by) for i in range(count)])
+
+
+def bit(axis, by):
+    return (lax.axis_index(axis) // by) % 2
+
+
+def doubled(array, dim, axis, by):
+    other = swapped(array, axis, by)
+    first = bit(axis, by) == 0
+    return jnp.concatenate(
+        [jnp.where(first, array, other), jnp.where(first, other, array)], axis=dim
+    )
+
+
+def dp_gathered(share):
+    return doubled(doubled(share, 0, "dp", 2), 1, "dp", 1)
+
+
+def product(left, columns):
+    return lax.dot_general(left, columns, (((0,), (0,)), ((), ())), preferred_element_type=jnp.float32)
+
+
+def flag(axis, by):
+    return bit(axis, by).astype(jnp.int32).reshape(1)
+
+
+def shards(array, seq_parts):
+    rows, columns = array.shape
+    return array.reshape(2 * seq_parts, rows // (2 * seq_parts), columns)
+
+
+def reduced(kept, given, steps):
+    for (axis, by), following in zip(steps, steps[1:] + [None]):
+        taken = swapped(given, axis, by)
+        if following is None:
+            return dp_gathered((kept + taken)[0])
+        kept, given = fold(kept, taken, flag(*following))
+
+
+def by_sequences(
+    tokens,
+    offsets,
+    norm_gain,
+    norm_bias,
+    proj_weight,
+    proj_bias,
+    short_filter,
+    short_bias,
+    long_kernel,
+    skip_bias,
+    out_weight,
+    out_bias,
+    second_gain,
+    second_bias,
+    up_weight,
+    up_bias,
+    down_weight,
+    down_bias,
+    cotangent,
+):
+    parts, width, features = tokens.shape
+    length = parts * width
+    hidden_units = up_weight.shape[1]
+    hold = lax.optimization_barrier
+    tables = tuple(jnp.asarray(table) for table in block_tables(width))
+    start = lax.dynamic_slice_in_dim(offsets, lax.axis_index("seq"), 1, 0)
+    core, other_core = flag("dp", 1), 1 - flag("dp", 1)
+    low, single = jnp.bfloat16, jnp.float32
+    y_step, x_step = ("dp", 2), ("seq", 1)
+    z_steps = [("seq", 1 << place) for place in range(1, parts.bit_length() - 1)]
+
+    share = features // 4
+    chunk = bit("dp", 1) * 2 + bit("dp", 2)
+    piece = lax.dynamic_slice_in_dim(long_kernel, chunk * share, share, 0)[None]
+    for axis, by in z_steps[::-1]:
+        piece = doubled(piece[:, None], 1, axis, by)
+        piece = piece.reshape((-1,) + piece.shape[2:])
+    hidden = tokens.astype(single)
+    hidden, piece = hold((hidden, piece))
+    hidden = lax.all_to_all(hidden, "seq", 0, 0, tiled=True)
+    piece = doubled(piece[:, None], 1, *x_step).reshape(parts, share, width)
+    kernel = doubled(doubled(piece, 1, "dp", 2), 1, "dp", 1)
+    upstream = cotangent.astype(single)
+    taps = jnp.concatenate([short_filter.T, short_bias[None]], axis=0)
+    taps = jnp.swapaxes(taps.reshape(4, 3, features), 0, 1)
+    skip = skip_bias[None]
+    hidden, kernel, upstream, taps, start = hold((hidden, kernel, upstream, taps, start))
+
+    upstream = lax.all_to_all(upstream, "seq", 0, 0, tiled=True)
+    hidden = hidden.reshape(length, features)
+    normed_low, mixed = by_rows(
+        project_kernel,
+        "project",
+        length,
+        [
+            (hidden, False),
+            (norm_gain[None], True),
+            (norm_bias[None], True),
+            (proj_weight, True),
+            (proj_bias[None], True),
+        ],
+        [((length, features), low), ((length, 3 * features), single)],
+    )
+    convolved, branch_low = forward_convolution(start, mixed, kernel, taps, skip, tables)
+    residual, normed_two_low, activated_low, slope, *output = by_rows(
+        feed_kernel,
+        "feed",
+        length,
+        [
+            (hidden, False),
+            (branch_low, False),
+            (out_weight, True),
+            (out_bias[None], True),
+            (second_gain[None], True),
+            (second_bias[None], True),
+            (up_weight, True),
+            (up_bias[None], True),
+            (down_weight, True),
+            (down_bias[None], True),
+        ],
+        [
+            ((length, features), single),
+            ((length, features), low),
+            ((length, hidden_units), low),
+            ((length, hidden_units), single),
+            ((length, features // 2), single),
+            ((length, features // 2), single),
+        ],
+    )
+    upstream, output = hold((upstream, output))
+
+    def sent(half):
+        half = half.reshape(parts, width, features // 2)
+        return lax.all_to_all(half, "seq", 0, 0, tiled=True)
+
+    output[0] = sent(output[0])
+    upstream = upstream.reshape(length, features)
+    upstream_low = upstream.astype(low)
+    down_given = half_product(activated_low, upstream_low, other_core)
+    upstream, down_given = hold((upstream, down_given))
+
+    down_taken = swapped(down_given, "dp", 1)
+    expanded_low, residual_grad, residual_low, branch_grad, sums_two, wide_sums = by_rows(
+        feed_back_kernel,
+        "feed_back",
+        length,
+        [
+            (upstream, False),
+            (residual, False),
+            (slope, False),
+            (second_gain[None], True),
+            (out_weight, True),
+            (up_weight, True),
+            (down_weight, True),
+        ],
+        [
+            ((length, hidden_units), low),
+            ((length, features), single),
+            ((length, features), low),
+            ((length, features), single),
+            ((4, features), single),
+            ((1, hidden_units), single),
+        ],
+    )
+    up_given = half_product(normed_two_low, expanded_low, other_core)
+    out_given = half_product(branch_low, residual_low, other_core)
+    output, up_given, out_given, down_taken = hold((output, up_given, out_given, down_taken))
+
+    up_taken = swapped(up_given, "dp", 1)
+    out_taken = swapped(out_given, "dp", 1)
+    down_kept, down_given = parted_product(
+        activated_low, upstream_low, core, down_taken, flag(*y_step), parts
+    )
+    output, down_given, up_taken, out_taken = hold((output, down_given, up_taken, out_taken))
+
+    output[1] = sent(output[1])
+    down_taken = swapped(down_given, *y_step)
+    up_kept, up_given = parted_product(
+        normed_two_low, expanded_low, core, up_taken, flag(*x_step), parts // 2
+    )
+    branch_grad, up_given = hold((branch_grad, up_given))
+    up_taken = swapped(up_given, *x_step)
+    mixed_low, kernel_grad, sums = backward_convolution(
+        start, branch_grad, convolved, mixed, kernel, taps, skip, tables
+    )
+    mixed_low, kernel_grad, down_taken, output = hold((mixed_low, kernel_grad, down_taken, output))
+
+    down_kept, down_given = fold(down_kept, down_taken, flag(*x_step))
+    kernel_kept = lax.dynamic_index_in_dim(kernel_grad, core[0], 0, keepdims=False)
+    kernel_given = lax.dynamic_index_in_dim(kernel_grad, other_core[0], 0, keepdims=False)
+    mixed_low, down_given, kernel_given = hold((mixed_low, down_given, kernel_given))
+    down_taken = swapped(down_given, *x_step)
+    kernel_taken = swapped(kernel_given, "dp", 1)
+    *input_grad, sums_one = by_rows(
+        input_grad_kernel,
+        "input_grad",
+        length,
+        [
+            (mixed_low, False),
+            (proj_weight, True),
+            (hidden, False),
+            (norm_gain[None], True),
+            (residual_grad, False),
+        ],
+        [
+            ((length, features // 2), single),
+            ((length, features // 2), single),
+            ((2, features), single),
+        ],
+    )
+    input_grad, mixed_low, kernel_taken, up_taken, sums_one, out_taken = hold(
+        (input_grad, mixed_low, kernel_taken, up_taken, sums_one, out_taken)
+    )
+
+    input_grad[0] = sent(input_grad[0])
+    proj_given = half_product(normed_low, mixed_low, other_core)
+    proj_taken = swapped(proj_given, "dp", 1)
+    rows = features // (2 * parts)
+    up_kept, up_taken = [array.reshape(parts, rows, -1) for array in (up_kept, up_taken)]
+    up_kept, up_given = fold(up_kept, up_taken, flag(*y_step))
+    up_taken = swapped(up_given, *y_step)
+    out_kept, out_given = parted_product(
+        branch_low, residual_low, core, out_taken, flag(*y_step), parts
+    )
+    kernel_sum = shards(kernel_kept + kernel_taken, parts)
+    input_grad, proj_taken, up_taken, down_taken, sums, out_given, kernel_sum = hold(
+        (input_grad, proj_taken, up_taken, down_taken, sums, out_given, kernel_sum)
+    )
+
+    input_grad[1] = sent(input_grad[1])
+    proj_kept, proj_given = parted_product(
+        normed_low, mixed_low, core, proj_taken, flag(*y_step), parts
+    )
+    proj_taken = swapped(proj_given, *y_step)
+    down_kept, down_given = fold(down_kept, down_taken, flag(*z_steps[0]))
+    up_kept, up_given = fold(up_kept, up_taken, flag(*z_steps[0]))
+    vectors = [
+        sums_one[0],
+        sums_one[1],
+        sums[12:15].reshape(-1),
+        jnp.swapaxes(sums[:9].reshape(3, 3, features), 1, 2).reshape(-1),
+        sums[9:12].reshape(-1),
+        sums[15],
+        sums_two[2],
+        sums_two[0],
+        sums_two[1],
+        wide_sums[0],
+        sums_two[3],
+    ]
+    sizes = [vector.shape[0] // parts for vector in vectors]
+    packed = jnp.concatenate([vector.reshape(parts, -1) for vector in vectors], axis=1)
+    packed = jnp.pad(packed, ((0, 0), (0, 4 * rows * 128 - packed.shape[1])))
+    packed = packed.reshape(parts, 2, 2 * rows, 128)
+    packed_kept = lax.dynamic_index_in_dim(packed, core[0], 1, keepdims=False)
+    packed_given = lax.dynamic_index_in_dim(packed, other_core[0], 1, keepdims=False)
+    packed = packed_kept + swapped(packed_given, "dp", 1)
+    rest = jnp.concatenate([kernel_sum, packed.reshape(2 * parts, rows, 128)], axis=2)
+    rest = rest.reshape(parts, 2, rows, -1)
+    rest_kept = lax.dynamic_index_in_dim(rest, flag(*y_step)[0], 1, keepdims=False)
+    rest_given = lax.dynamic_index_in_dim(rest, 1 - flag(*y_step)[0], 1, keepdims=False)
+    rest_kept = jnp.concatenate([out_kept, rest_kept], axis=2)
+    rest_given = jnp.concatenate([out_given, rest_given], axis=2)
+
+    rest_taken = swapped(rest_given, *y_step)
+    input_grad, proj_taken, rest_taken, down_given, up_given = hold(
+        (input_grad, proj_taken, rest_taken, down_given, up_given)
+    )
+    proj_share = reduced(*fold(proj_kept, proj_taken, flag(*x_step)), [x_step] + z_steps)
+    rest = reduced(*fold(rest_kept, rest_taken, flag(*x_step)), [x_step] + z_steps)
+    down_share = reduced(down_kept, down_given, z_steps)
+    up_share = reduced(up_kept, up_given, z_steps)
+    output = jnp.concatenate(output, axis=2)
+    input_grad = jnp.concatenate(input_grad, axis=2)
+
+    proj_share = proj_share.reshape(-1, 2, 3, features // 2)
+    proj_share = jnp.swapaxes(proj_share, 1, 2).reshape(-1, 3 * features)
+    columns = rest.shape[1] // 2
+    ends = [features // 2, features // 2 + length // 2, columns]
+    out_share, kernel_share, packed = [
+        jnp.concatenate([rest[:, first:end], rest[:, columns + first : columns + end]], axis=1)
+        for first, end in zip([0] + ends, ends)
+    ]
+    packed = jnp.swapaxes(packed.reshape(2, rows, 2, 128), 1, 2)
+    packed = jnp.swapaxes(packed, 0, 1).reshape(-1)
+    ends = np.cumsum(sizes)
+    vectors = [packed[end - size : end] for size, end in zip(sizes, ends)]
+    return (
+        output,
+        input_grad,
+        vectors[0],
+        vectors[1],
+        proj_share,
+        vectors[2],
+        vectors[3].reshape(-1, 3),
+        vectors[4],
+        kernel_share,
+        vectors[5],
+        out_share,
+        vectors[6],
+        vectors[7],
+        vectors[8],
+        up_share,
+        vectors[9],
+        down_share,
+        vectors[10],
+    )
+
+
+def per_device(tokens, offsets, *rest):
+    fits = (
+        tokens.shape[0] == lax.axis_size("seq")
+        and lax.axis_size("dp") == 4
+        and tokens.shape[0] % 2 == 0
+        and tokens.shape[1] % 128 == 0
+        and lax.axis_size("seq") & (lax.axis_size("seq") - 1) == 0
+    )
+    plan = by_sequences if fits else by_channels
+    return plan(tokens, offsets, *rest)
+
+
 def solution(mesh):
     return jax.shard_map(
         per_device,

time: 1250 us -> 577 us (0.46)
  matrix products: 365 us -> 0 us
  blocking collectives: 328 us -> 0 us
  Pallas kernels: 0 us -> 215 us
  waiting for transfers between devices: 332 us -> 222 us
  local copies, waits for them, and re-layouts: 93.8 us -> 30.4 us
  starting transfers between devices: 25.2 us -> 65.9 us
  other arithmetic: 78 us -> 39.9 us
  between operations: 17.2 us -> 1.33 us
    dot_general x48 -> x0, matrix products: 365 us -> none  [the longest x3 32.5 us: forward_transform(): jnp.einsum('rkc,cm->rkm', turned_real, fine_cos, precision=PRECISE)]
    all_to_all x2 -> x0, blocking collectives: 279 us -> none  [the longest x1 181 us: per_device(): lax.all_to_all(gated_back_chan, 'seq', split_axis=2, concat_axis=1, tiled...]
    pallas_call x0 -> x26, Pallas kernels: none -> 215 us  [the longest x4 65.8 us: by_rows(): pl.pallas_call(kernel, grid=(rows // height,), in_specs=[spec(array.shape...]
    ppermute x2 -> x35, waiting for transfers between devices: 9.75 us -> 202 us  [swapped(): return lax.ppermute(array, axis, [(i, i ^ by) for i in range(count)])]
    reduce_scatter x4 -> x0, waiting for transfers between devices: 119 us -> none  [the longest x1 119 us: per_device(): lax.psum_scatter(proj_grad, 'seq', scatter_dimension=0, tiled=True)]
    all_to_all x3 -> x6, waiting for transfers between devices: 126 us -> 20.1 us  [the longest x1 11.8 us: by_sequences(): upstream = lax.all_to_all(upstream, 'seq', 0, 0, tiled=True)]
    psum x1 -> x0, waiting for transfers between devices: 71.6 us -> none  [per_device(): lax.psum((norm_gain_share, norm_bias_share, proj_share, proj_bias_share,...]
    reduce_sum x10 -> x0, other arithmetic: 38.6 us -> none  [the longest x1 18.1 us: per_device(): jnp.sum(filtered_grad * extended[:, position:position + tok_count], axis=...]
  transfers between devices with their start and end apart: 11 -> 41, of which waited for: 7 -> 20; matrix products, arithmetic and copies ran while one was open for 27% -> 9% of each run, Pallas kernels for 0% -> 35%
where the time goes in v1:
time: 577 us; the launch traced here: 575 us
  waiting for transfers between devices  222 us (38%)
  Pallas kernels  215 us (37%)
  starting transfers between devices  65.9 us (11%)
  other arithmetic  39.9 us (7%)
  local copies, waits for them, and re-layouts  30.4 us (5%)
    ppermute x35, waiting for transfers between devices, swapped(): return lax.ppermute(array, axis, [(i, i ^ by) for i in range(count)])  202 us
    pallas_call x4, Pallas kernels, by_rows(): pl.pallas_call(kernel, grid=(rows // height,), in_specs=[spec(array.shape...  65.8 us
    pallas_call x1, Pallas kernels, backward_convolution(): pl.pallas_call(backward_kernel, grid=(features // lanes,), in_specs=start...  37.6 us
    ppermute x35, starting transfers between devices, swapped(): return lax.ppermute(array, axis, [(i, i ^ by) for i in range(count)])  35.7 us
    pallas_call x12, Pallas kernels, fold(): pl.pallas_call(fold_kernel, grid=(count // 2,), in_specs=[pl.BlockSpec(me...  35 us
    pallas_call x4, Pallas kernels, parted_product(): pl.pallas_call(parted_product_kernel, grid_spec=pltpu.PrefetchScalarGridS...  30.6 us
    pallas_call x4, Pallas kernels, half_product(): pl.pallas_call(product_kernel, grid_spec=pltpu.PrefetchScalarGridSpec(num...  26 us
    pallas_call x1, Pallas kernels, forward_convolution(): pl.pallas_call(forward_kernel, grid=(features // lanes,), in_specs=start_...  20.4 us
  transfers between devices with their start and end apart: 41, of which 20 were waited for; matrix products, arithmetic and copies ran while one was open for 9% of the time, Pallas kernels for 35%

profile of v1, /device:TPU:0, one launch (start us, length us, event | category | flops | bytes accessed | tf_op | source)
XLA Modules:
  0.0 574.5 jit_solution(14129208817011983384)
XLA Ops:
  17.7 6.5 %all-to-all-start = ((f32[8,128,768]{2,1,0:T(8,128)}), f32[8,128,768]{2,1,0:T(8,128)S(1)}, u32[]{:S(2)}, u32[]{:S(2)}) async-start(f32[8,128,768]{2,1,0:T(8,128)} %convert_element_type.11), calls=%async_computation | async-start | bytes 6291456 | tf_op jit(solution)/shard_map/all_to_all | solution.py:989
  26.2 32.8 %collective-permute-done.2 = f32[4,1,192,128]{3,2,1,0:T(8,128)} collective-permute-done((f32[4,1,192,128]{3,2,1,0:T(8,128)S(1)}, f32[4,1,192,128]{3,2,1,0:T(8,128)}, u32[]{:S(2)}, u32[]{:S(2)}) %collective-permute-start.2) | collective-permute-done | bytes 393248 | tf_op jit(solution)/shard_map/ppermute | solution.py:909
  62.5 17.0 %collective-permute-done.3 = f32[8,192,128]{2,1,0:T(8,128)} collective-permute-done((f32[8,192,128]{2,1,0:T(8,128)}, f32[8,192,128]{2,1,0:T(8,128)}, u32[]{:S(2)}, u32[]{:S(2)}) %collective-permute-start.3) | collective-permute-done | bytes 786464 | tf_op jit(solution)/shard_map/ppermute | solution.py:909
  105.1 9.5 %project.1 = (bf16[1024,768]{1,0:T(8,128)(2,1)}, f32[1024,2304]{1,0:T(8,128)}) custom-call(f32[1024,768]{1,0:T(8,128)} %bitcast.80, f32[1,768]{1,0:T(1,128)} %broadcast_in_dim.34.gain_ref, f32[1,768]{1,0:T(1,128)} %broadcast_in_dim.35.bias_ref, bf16[768,2304]{1,0:T(8,128)(2,1)} %weight_ref.3, f32[1,2304]{1,0:T(1,128)} %broadcast_in_dim.36.offset_ref), custom_call_target="tpu_custom_call" | custom-call | tf_op jit(solution)/shard_map/project/pallas_call | solution.py:793
  114.6 20.4 %forward_convolution.1 = (f32[1024,768]{1,0:T(8,128)}, bf16[1024,768]{1,0:T(8,128)(2,1)}) custom-call(s32[1]{0:T(128)} %dynamic_slice.28.start_ref, f32[1024,2304]{1,0:T(8,128)} %get-tuple-element.130.outer_ref.inner_ref.value_ref, f32[1024,2304]{1,0:T(8,128)} %get-tuple-element.130.outer_ref.inner_ref.value_ref, ...), custom_call_target="tpu_custom_call" | custom-call | tf_op jit(solution)/shard_map/forward_convolution/pallas_call | solution.py:596
  135.0 24.1 %feed.1 = (f32[1024,768]{1,0:T(8,128)}, bf16[1024,768]{1,0:T(8,128)(2,1)}, bf16[1024,3072]{1,0:T(8,128)(2,1)}, f32[1024,3072]{1,0:T(8,128)}, f32[1024,384]{1,0:T(8,128)}, /*index=5*/f32[1024,384]{1,0:T(8,128)}) custom-call(f32[1024,768]{1,0:T(8,128)} %bitcast.81, bf16[1024,768]{1,0:T(8,128)(2,1)} %get-tuple-element.133.branch_ref.left_ref, ...), custom_call_target="tpu_custom_call" | custom-call | tf_op jit(solution)/shard_map/feed/pallas_call | solution.py:793
  159.0 11.8 %all-to-all-done.1 = f32[8,128,768]{2,1,0:T(8,128)} async-done(((f32[8,128,768]{2,1,0:T(8,128)}), f32[8,128,768]{2,1,0:T(8,128)}, u32[]{:S(2)}, u32[]{:S(2)}) %all-to-all-start.1) | async-done | bytes 3145760 | tf_op jit(solution)/shard_map/all_to_all | solution.py:998
  174.0 9.4 %half_product.4 = f32[3072,384]{1,0:T(8,128)} custom-call(s32[1]{0:T(128)} %sub.51.half_ref, bf16[1024,3072]{1,0:T(8,128)(2,1)} %get-tuple-element.137.left_ref, bf16[1024,768]{1,0:T(8,128)(2,1)} %bitcast_convert_fusion.right_ref), custom_call_target="tpu_custom_call" | custom-call | tf_op jit(solution)/shard_map/half_product/pallas_call | solution.py:831
  187.2 22.2 %feed_back.1 = (bf16[1024,3072]{1,0:T(8,128)(2,1)}, f32[1024,768]{1,0:T(8,128)}, bf16[1024,768]{1,0:T(8,128)(2,1)}, f32[1024,768]{1,0:T(8,128)}, f32[4,768]{1,0:T(4,128)}, /*index=5*/f32[1,3072]{1,0:T(1,128)}) custom-call(f32[1024,768]{1,0:T(8,128)} %bitcast.15.grad_ref, f32[1024,768]{1,0:T(8,128)} %get-tuple-element.139.residual_ref, ...), custom_call_target="tpu_custom_call" | custom-call | tf_op jit(solution)/shard_map/feed_back/pallas_call | solution.py:793
  212.9 6.5 %half_product.5 = f32[768,1536]{1,0:T(8,128)} custom-call(s32[1]{0:T(128)} %sub.51.half_ref, bf16[1024,768]{1,0:T(8,128)(2,1)} %get-tuple-element.142.left_ref, bf16[1024,3072]{1,0:T(8,128)(2,1)} %get-tuple-element.143.right_ref), custom_call_target="tpu_custom_call" | custom-call | tf_op jit(solution)/shard_map/half_product/pallas_call | solution.py:831
  226.0 11.0 %parted_product.4 = (f32[8,192,384]{2,1,0:T(8,128)}, f32[8,192,384]{2,1,0:T(8,128)}) custom-call(s32[2]{0:T(128)} %get-tuple-element.316.bits_ref, bf16[1024,3072]{1,0:T(8,128)(2,1)} %get-tuple-element.137.left_ref, bf16[1024,768]{1,0:T(8,128)(2,1)} %bitcast_convert_fusion.right_ref, f32[3072,384]{1,0:T(8,128)} %collective-permute-done.5.taken_ref), custom_call_target="tpu_custom_call" | custom-call | tf_op jit(solution)/shard_map/parted_product/pallas_call | solution.py:864
  242.3 7.9 %parted_product.5 = (f32[4,96,1536]{2,1,0:T(8,128)}, f32[4,96,1536]{2,1,0:T(8,128)}) custom-call(s32[2]{0:T(128)} %get-tuple-element.315.bits_ref, bf16[1024,768]{1,0:T(8,128)(2,1)} %get-tuple-element.142.left_ref, bf16[1024,3072]{1,0:T(8,128)(2,1)} %get-tuple-element.143.right_ref, f32[768,1536]{1,0:T(8,128)} %collective-permute-done.6.taken_ref), custom_call_target="tpu_custom_call" | custom-call | tf_op jit(solution)/shard_map/parted_product/pallas_call | solution.py:864
  252.1 37.6 %backward_convolution.1 = (bf16[3,1024,768]{2,1,0:T(8,128)(2,1)}, f32[2,768,512]{2,1,0:T(8,128)}, f32[16,768]{1,0:T(8,128)}) custom-call(s32[1]{0:T(128)} %dynamic_slice.28.start_ref, f32[1024,768]{1,0:T(8,128)} %get-tuple-element.156.grad_ref, f32[1024,768]{1,0:T(8,128)} %get-tuple-element.157.convolved_ref, ...), custom_call_target="tpu_custom_call" | custom-call | tf_op jit(solution)/shard_map/backward_convolution/pallas_call | solution.py:616
  299.6 10.0 %input_grad.1 = (f32[1024,384]{1,0:T(8,128)}, f32[1024,384]{1,0:T(8,128)}, f32[2,768]{1,0:T(2,128)}) custom-call(bf16[3,1024,768]{2,1,0:T(8,128)(2,1)} %get-tuple-element.181.mixed_ref.right_ref, bf16[768,2304]{1,0:T(8,128)(2,1)} %weight_ref.3, f32[1024,768]{1,0:T(8,128)} %bitcast.82, f32[1,768]{1,0:T(1,128)} %broadcast_in_dim.34.gain_ref, ...), custom_call_target="tpu_custom_call" | custom-call | tf_op jit(solution)/shard_map/input_grad/pallas_call | solution.py:793
  311.9 6.6 %half_product.7 = f32[768,1152]{1,0:T(8,128)} custom-call(s32[1]{0:T(128)} %sub.51.half_ref, bf16[1024,768]{1,0:T(8,128)(2,1)} %get-tuple-element.180.left_ref, bf16[3,1024,768]{2,1,0:T(8,128)(2,1)} %get-tuple-element.181.mixed_ref.right_ref), custom_call_target="tpu_custom_call" | custom-call | tf_op jit(solution)/shard_map/half_product/pallas_call | solution.py:831
  318.5 7.4 %all-to-all-start.4 = ((f32[8,128,384]{2,1,0:T(8,128)}), f32[8,128,384]{2,1,0:T(8,128)}, u32[]{:S(2)}, u32[]{:S(2)}) async-start(f32[8,128,384]{2,1,0:T(8,128)} %bitcast.23), calls=%async_computation.4 | async-start | bytes 3145728 | tf_op jit(solution)/shard_map/all_to_all | solution.py:1043
  341.6 29.5 %collective-permute-done.13.taken_ref = f32[4,192,384]{2,1,0:T(8,128)} collective-permute-done((f32[4,192,384]{2,1,0:T(8,128)}, f32[4,192,384]{2,1,0:T(8,128)}, u32[]{:S(2)}, u32[]{:S(2)}) %collective-permute-start.13) | collective-permute-done | bytes 1179680 | tf_op jit(solution)/shard_map/ppermute | solution.py:909
  380.2 7.2 %parted_product.7 = (f32[8,48,1152]{2,1,0:T(8,128)}, f32[8,48,1152]{2,1,0:T(8,128)}) custom-call(s32[2]{0:T(128)} %get-tuple-element.316.bits_ref, bf16[1024,768]{1,0:T(8,128)(2,1)} %get-tuple-element.180.left_ref, bf16[3,1024,768]{2,1,0:T(8,128)(2,1)} %get-tuple-element.181.mixed_ref.right_ref, f32[768,1152]{1,0:T(8,128)} %collective-permute-done.11.taken_ref), custom_call_target="tpu_custom_call" | custom-call | tf_op jit(solution)/shard_map/parted_product/pallas_call | solution.py:864
  397.0 32.2 %collective-permute-done.14.taken_ref = f32[8,48,1152]{2,1,0:T(8,128)} collective-permute-done((f32[8,48,1152]{2,1,0:T(8,128)}, f32[8,48,1152]{2,1,0:T(8,128)}, u32[]{:S(2)}, u32[]{:S(2)}) %collective-permute-start.14) | collective-permute-done | bytes 1769504 | tf_op jit(solution)/shard_map/ppermute | solution.py:909
  429.2 33.3 %collective-permute-done.16.taken_ref = f32[8,48,1024]{2,1,0:T(8,128)} collective-permute-done((f32[8,48,1024]{2,1,0:T(8,128)S(1)}, f32[8,48,1024]{2,1,0:T(8,128)}, u32[]{:S(2)}, u32[]{:S(2)}) %collective-permute-start.16) | collective-permute-done | bytes 1572896 | tf_op jit(solution)/shard_map/ppermute | solution.py:909
  473.0 5.9 %collective-permute-done.31.taken_ref = f32[2,192,384]{2,1,0:T(8,128)S(1)} collective-permute-done((f32[2,192,384]{2,1,0:T(8,128)}, f32[2,192,384]{2,1,0:T(8,128)S(1)}, u32[]{:S(2)}, u32[]{:S(2)}) %collective-permute-start.31) | collective-permute-done | bytes 589856 | tf_op jit(solution)/shard_map/ppermute | solution.py:909
  527.8 7.4 %collective-permute-done.23.taken_ref = f32[2,48,1152]{2,1,0:T(8,128)S(1)} collective-permute-done((f32[2,48,1152]{2,1,0:T(8,128)}, f32[2,48,1152]{2,1,0:T(8,128)S(1)}, u32[]{:S(2)}, u32[]{:S(2)}) %collective-permute-start.23) | collective-permute-done | bytes 442400 | tf_op jit(solution)/shard_map/ppermute | solution.py:909
  539.7 10.5 %collective-permute-done.24 = f32[1,48,1152]{2,1,0:T(8,128)S(1)} collective-permute-done((f32[1,48,1152]{2,1,0:T(8,128)}, f32[1,48,1152]{2,1,0:T(8,128)S(1)}, u32[]{:S(2)}, u32[]{:S(2)}) %collective-permute-start.24) | collective-permute-done | bytes 221216 | tf_op jit(solution)/shard_map/ppermute | solution.py:909
  552.4 6.2 %collective-permute-done.25 = f32[48,1152]{1,0:T(8,128)S(1)} collective-permute-done((f32[48,1152]{1,0:T(8,128)S(1)}, f32[48,1152]{1,0:T(8,128)S(1)}, u32[]{:S(2)}, u32[]{:S(2)}) %collective-permute-start.25) | collective-permute-done | bytes 221216 | tf_op jit(solution)/shard_map/ppermute | solution.py:909
  (251 shorter events, 200.3 us)
Async XLA Ops:
  17.7 76.5 %all-to-all-start = ((f32[8,128,768]{2,1,0:T(8,128)}), f32[8,128,768]{2,1,0:T(8,128)S(1)}, u32[]{:S(2)}, u32[]{:S(2)}) async-start(f32[8,128,768]{2,1,0:T(8,128)} %convert_element_type.11), calls=%async_computation | async-start | bytes 6291456 | tf_op jit(solution)/shard_map/all_to_all | solution.py:989
  24.2 34.8 %collective-permute-start.2 = (f32[4,1,192,128]{3,2,1,0:T(8,128)S(1)}, f32[4,1,192,128]{3,2,1,0:T(8,128)}, u32[]{:S(2)}, u32[]{:S(2)}) collective-permute-start(f32[4,1,192,128]{3,2,1,0:T(8,128)S(1)} %bitcast.91), channel_id=1, source_target_pairs={{0,1},{1,0},{2,3},{3,2},{4,5},{5,4},{6,7},{7,6},{8,9},{9,8},{10,11... | collective-permute-start | bytes 1179656 | tf_op jit(solution)/shard_map/ppermute | solution.py:909
  61.0 18.5 %collective-permute-start.3 = (f32[8,192,128]{2,1,0:T(8,128)}, f32[8,192,128]{2,1,0:T(8,128)}, u32[]{:S(2)}, u32[]{:S(2)}) collective-permute-start(f32[8,192,128]{2,1,0:T(8,128)} %bitcast.9), channel_id=1, source_target_pairs={{0,16},{8,24},{16,0},{24,8},{1,17},{9,25},{17,1},{25,9},{2,18},{10... | collective-permute-start | bytes 2359304 | tf_op jit(solution)/shard_map/ppermute | solution.py:909
  95.9 74.9 %all-to-all-start.1 = ((f32[8,128,768]{2,1,0:T(8,128)}), f32[8,128,768]{2,1,0:T(8,128)}, u32[]{:S(2)}, u32[]{:S(2)}) async-start(f32[8,128,768]{2,1,0:T(8,128)} %convert_element_type.12), calls=%async_computation.1 | async-start | bytes 6291456 | tf_op jit(solution)/shard_map/all_to_all | solution.py:998
  183.5 41.5 %collective-permute-start.5 = (f32[3072,384]{1,0:T(8,128)}, f32[3072,384]{1,0:T(8,128)}, u32[]{:S(2)}, u32[]{:S(2)}) collective-permute-start(f32[3072,384]{1,0:T(8,128)} %half_product.4), channel_id=1, source_target_pairs={{0,8},{8,0},{16,24},{24,16},{1,9},{9,1},{17,25},{25,17},{2,10},{10... | collective-permute-start | bytes 14155784 | tf_op jit(solution)/shard_map/ppermute | solution.py:909
  183.5 41.5 %all-to-all-start.2 = ((f32[8,128,384]{2,1,0:T(8,128)}), f32[8,128,384]{2,1,0:T(8,128)S(1)}, u32[]{:S(2)}, u32[]{:S(2)}) async-start(f32[8,128,384]{2,1,0:T(8,128)} %bitcast.18), calls=%async_computation.2 | async-start | bytes 3145728 | tf_op jit(solution)/shard_map/all_to_all | solution.py:1043
  237.1 57.2 %all-to-all-start.3 = ((f32[8,128,384]{2,1,0:T(8,128)}), f32[8,128,384]{2,1,0:T(8,128)S(1)}, u32[]{:S(2)}, u32[]{:S(2)}) async-start(f32[8,128,384]{2,1,0:T(8,128)} %bitcast.89), calls=%async_computation.3 | async-start | bytes 3145728 | tf_op jit(solution)/shard_map/all_to_all | solution.py:1043
  240.7 53.6 %collective-permute-start.8 = (f32[8,192,384]{2,1,0:T(8,128)}, f32[8,192,384]{2,1,0:T(8,128)}, u32[]{:S(2)}, u32[]{:S(2)}) collective-permute-start(f32[8,192,384]{2,1,0:T(8,128)} %get-tuple-element.160), channel_id=1, source_target_pairs={{0,16},{8,24},{16,0},{24,8},{1,17},{9,25},{17,1},{25,9},{2,18},{10... | collective-permute-start | bytes 7077896 | tf_op jit(solution)/shard_map/ppermute | solution.py:909
  250.1 61.7 %collective-permute-start.10 = (f32[4,96,1536]{2,1,0:T(8,128)}, f32[4,96,1536]{2,1,0:T(8,128)}, u32[]{:S(2)}, u32[]{:S(2)}) collective-permute-start(f32[4,96,1536]{2,1,0:T(8,128)} %get-tuple-element.175), channel_id=1, source_target_pairs={{0,1},{1,0},{2,3},{3,2},{4,5},{5,4},{6,7},{7,6},{8,9},{9,8},{10,11... | collective-permute-start | bytes 7077896 | tf_op jit(solution)/shard_map/ppermute | solution.py:909
  318.5 52.6 %collective-permute-start.11 = (f32[768,1152]{1,0:T(8,128)}, f32[768,1152]{1,0:T(8,128)}, u32[]{:S(2)}, u32[]{:S(2)}) collective-permute-start(f32[768,1152]{1,0:T(8,128)} %half_product.7), channel_id=1, source_target_pairs={{0,8},{8,0},{16,24},{24,16},{1,9},{9,1},{17,25},{25,17},{2,10},{10... | collective-permute-start | bytes 10616840 | tf_op jit(solution)/shard_map/ppermute | solution.py:909
  318.5 52.6 %all-to-all-start.4 = ((f32[8,128,384]{2,1,0:T(8,128)}), f32[8,128,384]{2,1,0:T(8,128)}, u32[]{:S(2)}, u32[]{:S(2)}) async-start(f32[8,128,384]{2,1,0:T(8,128)} %bitcast.23), calls=%async_computation.4 | async-start | bytes 3145728 | tf_op jit(solution)/shard_map/all_to_all | solution.py:1043
  325.9 45.3 %collective-permute-start.13 = (f32[4,192,384]{2,1,0:T(8,128)}, f32[4,192,384]{2,1,0:T(8,128)}, u32[]{:S(2)}, u32[]{:S(2)}) collective-permute-start(f32[4,192,384]{2,1,0:T(8,128)} %get-tuple-element.185), channel_id=1, source_target_pairs={{0,1},{1,0},{2,3},{3,2},{4,5},{5,4},{6,7},{7,6},{8,9},{9,8},{10,11... | collective-permute-start | bytes 3538952 | tf_op jit(solution)/shard_map/ppermute | solution.py:909
  332.2 38.9 %collective-permute-start.12 = (f32[4,48,1536]{2,1,0:T(8,128)}, f32[4,48,1536]{2,1,0:T(8,128)}, u32[]{:S(2)}, u32[]{:S(2)}) collective-permute-start(f32[4,48,1536]{2,1,0:T(8,128)} %get-tuple-element.184), channel_id=1, source_target_pairs={{0,16},{8,24},{16,0},{24,8},{1,17},{9,25},{17,1},{25,9},{2,18},{10... | collective-permute-start | bytes 3538952 | tf_op jit(solution)/shard_map/ppermute | solution.py:909
  374.5 88.0 %all-to-all-start.5 = ((f32[8,128,384]{2,1,0:T(8,128)}), f32[8,128,384]{2,1,0:T(8,128)}, u32[]{:S(2)}, u32[]{:S(2)}) async-start(f32[8,128,384]{2,1,0:T(8,128)} %bitcast.88), calls=%async_computation.5 | async-start | bytes 3145728 | tf_op jit(solution)/shard_map/all_to_all | solution.py:1043
  387.5 41.7 %collective-permute-start.14 = (f32[8,48,1152]{2,1,0:T(8,128)}, f32[8,48,1152]{2,1,0:T(8,128)}, u32[]{:S(2)}, u32[]{:S(2)}) collective-permute-start(f32[8,48,1152]{2,1,0:T(8,128)} %get-tuple-element.193), channel_id=1, source_target_pairs={{0,16},{8,24},{16,0},{24,8},{1,17},{9,25},{17,1},{25,9},{2,18},{10... | collective-permute-start | bytes 5308424 | tf_op jit(solution)/shard_map/ppermute | solution.py:909
  390.9 71.6 %collective-permute-start.16 = (f32[8,48,1024]{2,1,0:T(8,128)S(1)}, f32[8,48,1024]{2,1,0:T(8,128)}, u32[]{:S(2)}, u32[]{:S(2)}) collective-permute-start(f32[8,48,1024]{2,1,0:T(8,128)S(1)} %pad_maximum_fusion.4), channel_id=1, source_target_pairs={{0,16},{8,24},{16,0},{24,8},{1,17},{9,25},{17,1},{25,9},{2,18},{10... | collective-permute-start | bytes 4718600 | tf_op jit(solution)/shard_map/ppermute | solution.py:909
  462.5 16.4 %collective-permute-start.31 = (f32[2,192,384]{2,1,0:T(8,128)}, f32[2,192,384]{2,1,0:T(8,128)S(1)}, u32[]{:S(2)}, u32[]{:S(2)}) collective-permute-start(f32[2,192,384]{2,1,0:T(8,128)} %get-tuple-element.229), channel_id=1, source_target_pairs={{0,2},{1,3},{2,0},{3,1},{4,6},{5,7},{6,4},{7,5},{8,10},{9,11},{10,... | collective-permute-start | bytes 1769480 | tf_op jit(solution)/shard_map/ppermute | solution.py:909
  471.0 34.3 %collective-permute-start.17 = (f32[4,48,1024]{2,1,0:T(8,128)}, f32[4,48,1024]{2,1,0:T(8,128)S(1)}, u32[]{:S(2)}, u32[]{:S(2)}) collective-permute-start(f32[4,48,1024]{2,1,0:T(8,128)} %get-tuple-element.211), channel_id=1, source_target_pairs={{0,1},{1,0},{2,3},{3,2},{4,5},{5,4},{6,7},{7,6},{8,9},{9,8},{10,11... | collective-permute-start | bytes 2359304 | tf_op jit(solution)/shard_map/ppermute | solution.py:909
  472.4 24.5 %collective-permute-start.27 = (f32[2,48,1536]{2,1,0:T(8,128)S(1)}, f32[2,48,1536]{2,1,0:T(8,128)S(1)}, u32[]{:S(2)}, u32[]{:S(2)}) collective-permute-start(f32[2,48,1536]{2,1,0:T(8,128)S(1)} %copy-done.33), channel_id=1, source_target_pairs={{0,2},{1,3},{2,0},{3,1},{4,6},{5,7},{6,4},{7,5},{8,10},{9,11},{10,... | collective-permute-start | bytes 1769480 | tf_op jit(solution)/shard_map/ppermute | solution.py:909
  481.9 29.0 %collective-permute-start.32 = (f32[1,192,384]{2,1,0:T(8,128)}, f32[1,192,384]{2,1,0:T(8,128)S(1)}, u32[]{:S(2)}, u32[]{:S(2)}) collective-permute-start(f32[1,192,384]{2,1,0:T(8,128)} %get-tuple-element.231), channel_id=1, source_target_pairs={{0,4},{1,5},{2,6},{3,7},{4,0},{5,1},{6,2},{7,3},{8,12},{9,13},{10,... | collective-permute-start | bytes 884744 | tf_op jit(solution)/shard_map/ppermute | solution.py:909
  490.7 25.9 %collective-permute-start.22 = (f32[4,48,1152]{2,1,0:T(8,128)}, f32[4,48,1152]{2,1,0:T(8,128)S(1)}, u32[]{:S(2)}, u32[]{:S(2)}) collective-permute-start(f32[4,48,1152]{2,1,0:T(8,128)} %get-tuple-element.219), channel_id=1, source_target_pairs={{0,1},{1,0},{2,3},{3,2},{4,5},{5,4},{6,7},{7,6},{8,9},{9,8},{10,11... | collective-permute-start | bytes 2654216 | tf_op jit(solution)/shard_map/ppermute | solution.py:909
  510.9 16.1 %collective-permute-start.33 = (f32[192,384]{1,0:T(8,128)S(1)}, f32[192,384]{1,0:T(8,128)S(1)}, u32[]{:S(2)}, u32[]{:S(2)}) collective-permute-start(f32[192,384]{1,0:T(8,128)S(1)} %add_bitcast_fusion), channel_id=1, source_target_pairs={{0,16},{8,24},{16,0},{24,8},{1,17},{9,25},{17,1},{25,9},{2,18},{10... | collective-permute-start | bytes 884744 | tf_op jit(solution)/shard_map/ppermute | solution.py:909
  527.0 31.7 %collective-permute-start.34 = (f32[384,384]{1,0:T(8,128)S(1)}, f32[384,384]{1,0:T(8,128)S(1)}, u32[]{:S(2)}, u32[]{:S(2)}) collective-permute-start(f32[384,384]{1,0:T(8,128)S(1)} %pad_maximum_fusion.11), channel_id=1, source_target_pairs={{0,8},{8,0},{16,24},{24,16},{1,9},{9,1},{17,25},{25,17},{2,10},{10... | collective-permute-start | bytes 1769480 | tf_op jit(solution)/shard_map/ppermute | solution.py:909
  527.2 31.6 %collective-permute-start.30 = (f32[96,1536]{1,0:T(8,128)S(1)}, f32[96,1536]{1,0:T(8,128)S(1)}, u32[]{:S(2)}, u32[]{:S(2)}) collective-permute-start(f32[96,1536]{1,0:T(8,128)S(1)} %pad_maximum_fusion.10), channel_id=1, source_target_pairs={{0,8},{8,0},{16,24},{24,16},{1,9},{9,1},{17,25},{25,17},{2,10},{10... | collective-permute-start | bytes 1769480 | tf_op jit(solution)/shard_map/ppermute | solution.py:909
  (52 other events, 498.5 us)

commit v2 on v1

--- a/solution.py
+++ b/solution.py
@@ -517,7 +517,8 @@
     analysis_ref,
     synthesis_ref,
     mixed_grad_ref,
-    kernel_grad_ref,
+    kernel_kept_ref,
+    kernel_given_ref,
     sums_ref,
     signal_spectra,
     kernel_spectra,
@@ -537,9 +538,12 @@
     multiply(signal_spectra, grad_spectra, spectra, True)
     lags = lag_blocks(synthesise(spectra, synthesis_ref), width)
     half = len(lags) // 2
-    for block, piece in enumerate(lags):
-        first = block % half * width
-        kernel_grad_ref[block // half, :, first : first + width] = piece.T
+    first = start_ref[1] == 0
+    for block in range(half):
+        columns = slice(block * width, (block + 1) * width)
+        one, two = lags[block].T, lags[half + block].T
+        kernel_kept_ref[:, columns] = jnp.where(first, one, two)
+        kernel_given_ref[:, columns] = jnp.where(first, two, one)
     multiply(kernel_spectra, grad_spectra, spectra, True)
     back = jnp.concatenate(lag_blocks(synthesise(spectra, synthesis_ref), width), axis=0)
     gated_grad = (back + conv_grad * skip_ref[...]) * live
@@ -555,10 +559,11 @@
         mixed_grad = taps[2:3] * grad + taps[1:2] * next_one + taps[0:1] * next_two
         low = mixed_grad.astype(jnp.bfloat16)
         mixed_grad_ref[group] = low
-        filter_rows += [total(next_two * mixed), total(next_one * mixed), total(grad * mixed)]
+        filter_rows.append([total(next_two * mixed), total(next_one * mixed), total(grad * mixed)])
         bias_rows.append(total(grad))
         low_rows.append(total(low.astype(jnp.float32)))
-    rows = filter_rows + bias_rows + low_rows + [total(conv_grad * gated)]
+    rows = [filter_rows[group][tap] for tap in range(3) for group in range(3)]
+    rows = rows + bias_rows + low_rows + [total(conv_grad * gated)]
     sums_ref[...] = jnp.concatenate(rows, axis=0)
 
 
@@ -619,12 +624,14 @@
         in_specs=start_spec + [plain, plain] + mixed_specs + rest,
         out_specs=(
             pl.BlockSpec((3, tokens, lanes), lambda tile: (0, 0, tile)),
-            pl.BlockSpec((2, lanes, tokens // 2), lambda tile: (0, tile, 0)),
+            pl.BlockSpec((lanes, tokens // 2), lambda tile: (tile, 0)),
+            pl.BlockSpec((lanes, tokens // 2), lambda tile: (tile, 0)),
             pl.BlockSpec((16, lanes), lambda tile: (0, tile)),
         ),
         out_shape=(
             jax.ShapeDtypeStruct((3, tokens, features), jnp.bfloat16),
-            jax.ShapeDtypeStruct((2, features, tokens // 2), jnp.float32),
+            jax.ShapeDtypeStruct((features, tokens // 2), jnp.float32),
+            jax.ShapeDtypeStruct((features, tokens // 2), jnp.float32),
             jax.ShapeDtypeStruct((16, features), jnp.float32),
         ),
         scratch_shapes=[spectra] * 4,
@@ -654,9 +661,11 @@
     return lax.dot_general(left, right, (((1,), (1,)), ((), ())), preferred_element_type=jnp.float32)
 
 
-def column_pair(array):
-    half = array.shape[1] // 2
-    return array[:, :half], array[:, half:]
+def columns_of(array, refs):
+    first = 0
+    for ref in refs:
+        ref[...] = array[:, first : first + ref.shape[1]]
+        first += ref.shape[1]
 
 
 def column_sums(array):
@@ -707,8 +716,7 @@
             1.0 + (3 * 0.044715) * square
         )
         total = total + matmul(activated, down_weight_ref[columns, :])
-    for ref, half in zip(output_refs, column_pair(total)):
-        ref[...] = half
+    columns_of(total, output_refs)
 
 
 def feed_back_kernel(
@@ -772,7 +780,7 @@
         normed_grad = part if normed_grad is None else normed_grad + part
     unit, spread = unit_rows(x_ref[...])
     total = residual_grad_ref[...] + unit_rows_back(normed_grad, unit, spread, gain_ref[...])
-    first_ref[...], second_ref[...] = column_pair(total)
+    columns_of(total, (first_ref, second_ref))
     sums = jnp.concatenate([column_sums(normed_grad * unit), column_sums(normed_grad)], axis=0)
 
     @pl.when(pl.program_id(0) == 0)
@@ -808,7 +816,7 @@
 
 def product_tile(left_ref, right_ref):
     if len(right_ref.shape) == 2:
-        return product(left_ref[...], right_ref[...])
+        return product(left_ref[...], right_ref[...].astype(jnp.bfloat16))
     return jnp.concatenate(
         [product(left_ref[...], right_ref[group]) for group in range(right_ref.shape[0])], axis=1
     )
@@ -880,28 +888,82 @@
     )(jnp.concatenate([half, which]), left, right, taken)
 
 
-def fold_kernel(bit_ref, kept_ref, taken_ref, kept_out_ref, given_out_ref):
-    total = kept_ref[...] + taken_ref[...]
+def fold_kernel(bit_ref, *refs):
+    *sources, kept_ref, given_ref = refs
     first = bit_ref[0] == 0
-    kept_out_ref[0] = jnp.where(first, total[0], total[1])
-    given_out_ref[0] = jnp.where(first, total[1], total[0])
-
-
-def fold(kept, taken, which):
-    count, rows, columns = kept.shape
-    pair = pl.BlockSpec((2, rows, columns), lambda step: (step, 0, 0))
-    one = pl.BlockSpec((1, rows, columns), lambda step: (step, 0, 0))
-    shape = jax.ShapeDtypeStruct((count // 2, rows, columns), jnp.float32)
+    height, lane = kept_ref.shape[1], 0
+    for kept, taken in zip(sources[::2], sources[1::2]):
+        total = kept[...] + taken[...]
+        for row in range(0, total.shape[1], height):
+            columns = slice(lane, lane + total.shape[2])
+            one, two = total[0, row : row + height], total[1, row : row + height]
+            kept_ref[0, :, columns] = jnp.where(first, one, two)
+            given_ref[0, :, columns] = jnp.where(first, two, one)
+            lane += total.shape[2]
+
+
+def fold(pairs, which, height):
+    count = pairs[0][0].shape[0]
+    operands = [array for pair in pairs for array in pair]
+    columns = sum(kept.shape[1] // height * kept.shape[2] for kept, _ in pairs)
+    one = pl.BlockSpec((1, height, columns), lambda step: (step, 0, 0))
+    shape = jax.ShapeDtypeStruct((count // 2, height, columns), jnp.float32)
     return pl.pallas_call(
         fold_kernel,
         grid=(count // 2,),
-        in_specs=[pl.BlockSpec(memory_space=pltpu.SMEM), pair, pair],
+        in_specs=[pl.BlockSpec(memory_space=pltpu.SMEM)]
+        + [pl.BlockSpec((2,) + array.shape[1:], lambda step: (step, 0, 0)) for array in operands],
         out_specs=(one, one),
         out_shape=(shape, shape),
         compiler_params=kernel_parameters(),
         cost_estimate=NO_COST,
         name="fold",
-    )(which, kept, taken)
+    )(which, *operands)
+
+
+def unpack_kernel(bits_ref, own_ref, y_ref, core_ref, both_ref, *out_refs):
+    core_first, y_first = bits_ref[0] == 0, bits_ref[1] == 0
+    own, beside = own_ref[...], y_ref[...]
+    mine = [jnp.where(y_first, own, beside), jnp.where(y_first, beside, own)]
+    own, beside = core_ref[...], both_ref[...]
+    theirs = [jnp.where(y_first, own, beside), jnp.where(y_first, beside, own)]
+    height = own.shape[0]
+    for y in range(2):
+        for core in range(2):
+            block = jnp.where(core_first, mine[y], theirs[y])
+            if core == 1:
+                block = jnp.where(core_first, theirs[y], mine[y])
+            lane = 0
+            for ref in out_refs:
+                rows, columns = ref.shape
+                if columns == 128:
+                    ref[(2 * core + y) * height : (2 * core + y + 1) * height] = block[:, lane:]
+                    continue
+                groups = 3 if columns == 3 * height * 16 and rows == 2 * height else 1
+                half = columns // (2 * groups)
+                for place in range(rows // (2 * height)):
+                    for group in range(groups):
+                        top = y * (rows // 2) + place * height
+                        left = group * 2 * half + core * half
+                        ref[top : top + height, left : left + half] = block[:, lane : lane + half]
+                        lane += half
+
+
+def gathered(share):
+    y_other, core_other = swapped(share, "dp", 2), swapped(share, "dp", 1)
+    return share, y_other, core_other, swapped(y_other, "dp", 1)
+
+
+def unpacked(shares, shapes):
+    return pl.pallas_call(
+        unpack_kernel,
+        in_specs=[pl.BlockSpec(memory_space=pltpu.SMEM)] + [pl.BlockSpec(memory_space=pltpu.VMEM)] * 4,
+        out_specs=[pl.BlockSpec(memory_space=pltpu.VMEM)] * len(shapes),
+        out_shape=[jax.ShapeDtypeStruct(shape, jnp.float32) for shape in shapes],
+        compiler_params=kernel_parameters(),
+        cost_estimate=NO_COST,
+        name="unpack",
+    )(jnp.concatenate([flag("dp", 1), flag("dp", 2)]), *shares)
 
 
 def swapped(array, axis, by):
@@ -921,29 +983,20 @@
     )
 
 
-def dp_gathered(share):
-    return doubled(doubled(share, 0, "dp", 2), 1, "dp", 1)
-
-
 def product(left, columns):
     return lax.dot_general(left, columns, (((0,), (0,)), ((), ())), preferred_element_type=jnp.float32)
 
 
 def flag(axis, by):
     return bit(axis, by).astype(jnp.int32).reshape(1)
-
-
-def shards(array, seq_parts):
-    rows, columns = array.shape
-    return array.reshape(2 * seq_parts, rows // (2 * seq_parts), columns)
 
 
 def reduced(kept, given, steps):
     for (axis, by), following in zip(steps, steps[1:] + [None]):
         taken = swapped(given, axis, by)
         if following is None:
-            return dp_gathered((kept + taken)[0])
-        kept, given = fold(kept, taken, flag(*following))
+            return (kept + taken)[0]
+        kept, given = fold([(kept, taken)], flag(*following), kept.shape[1])
 
 
 def by_sequences(
@@ -974,26 +1027,28 @@
     tables = tuple(jnp.asarray(table) for table in block_tables(width))
     start = lax.dynamic_slice_in_dim(offsets, lax.axis_index("seq"), 1, 0)
     core, other_core = flag("dp", 1), 1 - flag("dp", 1)
+    scalars = jnp.concatenate([start, core])
     low, single = jnp.bfloat16, jnp.float32
     y_step, x_step = ("dp", 2), ("seq", 1)
     z_steps = [("seq", 1 << place) for place in range(1, parts.bit_length() - 1)]
 
     share = features // 4
     chunk = bit("dp", 1) * 2 + bit("dp", 2)
-    piece = lax.dynamic_slice_in_dim(long_kernel, chunk * share, share, 0)[None]
-    for axis, by in z_steps[::-1]:
-        piece = doubled(piece[:, None], 1, axis, by)
-        piece = piece.reshape((-1,) + piece.shape[2:])
-    hidden = tokens.astype(single)
-    hidden, piece = hold((hidden, piece))
+    piece = lax.dynamic_slice_in_dim(long_kernel, chunk * share, share, 0)
+    pieces = jnp.stack([piece] + [swapped(piece, "seq", by) for by in range(2, parts, 2)])
+    z = lax.axis_index("seq") // 2
+    pieces = jnp.concatenate(
+        [lax.dynamic_index_in_dim(pieces, z ^ other, 0) for other in range(parts // 2)]
+    )
+    hidden, pieces = hold((tokens.astype(single), pieces))
     hidden = lax.all_to_all(hidden, "seq", 0, 0, tiled=True)
-    piece = doubled(piece[:, None], 1, *x_step).reshape(parts, share, width)
-    kernel = doubled(doubled(piece, 1, "dp", 2), 1, "dp", 1)
+    pieces = doubled(pieces[:, None], 1, *x_step).reshape(parts, share, width)
+    kernel = doubled(doubled(pieces, 1, "dp", 2), 1, "dp", 1)
     upstream = cotangent.astype(single)
     taps = jnp.concatenate([short_filter.T, short_bias[None]], axis=0)
     taps = jnp.swapaxes(taps.reshape(4, 3, features), 0, 1)
     skip = skip_bias[None]
-    hidden, kernel, upstream, taps, start = hold((hidden, kernel, upstream, taps, start))
+    hidden, kernel, upstream, taps, scalars = hold((hidden, kernel, upstream, taps, scalars))
 
     upstream = lax.all_to_all(upstream, "seq", 0, 0, tiled=True)
     hidden = hidden.reshape(length, features)
@@ -1010,7 +1065,7 @@
         ],
         [((length, features), low), ((length, 3 * features), single)],
     )
-    convolved, branch_low = forward_convolution(start, mixed, kernel, taps, skip, tables)
+    convolved, branch_low = forward_convolution(scalars, mixed, kernel, taps, skip, tables)
     residual, normed_two_low, activated_low, slope, *output = by_rows(
         feed_kernel,
         "feed",
@@ -1033,19 +1088,19 @@
             ((length, hidden_units), low),
             ((length, hidden_units), single),
             ((length, features // 2), single),
-            ((length, features // 2), single),
+            ((length, features // 3), single),
+            ((length, features // 6), single),
         ],
     )
     upstream, output = hold((upstream, output))
 
-    def sent(half):
-        half = half.reshape(parts, width, features // 2)
-        return lax.all_to_all(half, "seq", 0, 0, tiled=True)
+    def sent(columns):
+        columns = columns.reshape(parts, width, -1)
+        return lax.all_to_all(columns, "seq", 0, 0, tiled=True)
 
     output[0] = sent(output[0])
     upstream = upstream.reshape(length, features)
-    upstream_low = upstream.astype(low)
-    down_given = half_product(activated_low, upstream_low, other_core)
+    down_given = half_product(activated_low, upstream, other_core, 768)
     upstream, down_given = hold((upstream, down_given))
 
     down_taken = swapped(down_given, "dp", 1)
@@ -1072,34 +1127,34 @@
         ],
     )
     up_given = half_product(normed_two_low, expanded_low, other_core)
-    out_given = half_product(branch_low, residual_low, other_core)
-    output, up_given, out_given, down_taken = hold((output, up_given, out_given, down_taken))
-
+    out_given = half_product(branch_low, residual_low, other_core, 768)
+    branch_grad, up_given, out_given, down_taken, output = hold(
+        (branch_grad, up_given, out_given, down_taken, output)
+    )
+
+    output[1] = sent(output[1])
     up_taken = swapped(up_given, "dp", 1)
     out_taken = swapped(out_given, "dp", 1)
     down_kept, down_given = parted_product(
-        activated_low, upstream_low, core, down_taken, flag(*y_step), parts
-    )
-    output, down_given, up_taken, out_taken = hold((output, down_given, up_taken, out_taken))
-
-    output[1] = sent(output[1])
-    down_taken = swapped(down_given, *y_step)
+        activated_low, upstream, core, down_taken, flag(*y_step), parts, 768
+    )
     up_kept, up_given = parted_product(
         normed_two_low, expanded_low, core, up_taken, flag(*x_step), parts // 2
     )
-    branch_grad, up_given = hold((branch_grad, up_given))
+    out_kept, out_given = parted_product(
+        branch_low, residual_low, core, out_taken, flag(*y_step), parts, 768
+    )
+    branch_grad, down_given, up_given, out_given, output = hold(
+        (branch_grad, down_given, up_given, out_given, output)
+    )
+
+    output[2] = sent(output[2])
+    down_taken = swapped(down_given, *y_step)
     up_taken = swapped(up_given, *x_step)
-    mixed_low, kernel_grad, sums = backward_convolution(
-        start, branch_grad, convolved, mixed, kernel, taps, skip, tables
-    )
-    mixed_low, kernel_grad, down_taken, output = hold((mixed_low, kernel_grad, down_taken, output))
-
-    down_kept, down_given = fold(down_kept, down_taken, flag(*x_step))
-    kernel_kept = lax.dynamic_index_in_dim(kernel_grad, core[0], 0, keepdims=False)
-    kernel_given = lax.dynamic_index_in_dim(kernel_grad, other_core[0], 0, keepdims=False)
-    mixed_low, down_given, kernel_given = hold((mixed_low, down_given, kernel_given))
-    down_taken = swapped(down_given, *x_step)
-    kernel_taken = swapped(kernel_given, "dp", 1)
+    mixed_low, kernel_kept, kernel_given, sums = backward_convolution(
+        scalars, branch_grad, convolved, mixed, kernel, taps, skip, tables
+    )
+    proj_given = half_product(normed_low, mixed_low, other_core)
     *input_grad, sums_one = by_rows(
         input_grad_kernel,
         "input_grad",
@@ -1112,85 +1167,101 @@
             (residual_grad, False),
         ],
         [
-            ((length, features // 2), single),
-            ((length, features // 2), single),
+            ((length, features * 2 // 3), single),
+            ((length, features // 3), single),
             ((2, features), single),
         ],
     )
-    input_grad, mixed_low, kernel_taken, up_taken, sums_one, out_taken = hold(
-        (input_grad, mixed_low, kernel_taken, up_taken, sums_one, out_taken)
-    )
-
+    input_grad, mixed_low, proj_given, kernel_given, down_taken, up_taken, sums_one, sums, output = hold(
+        (input_grad, mixed_low, proj_given, kernel_given, down_taken, up_taken, sums_one, sums, output)
+    )
+
+    rows = features // (2 * parts)
     input_grad[0] = sent(input_grad[0])
-    proj_given = half_product(normed_low, mixed_low, other_core)
+    out_taken = swapped(out_given, *y_step)
+    up_kept, up_taken = [array.reshape(parts, rows, -1) for array in (up_kept, up_taken)]
+    up_kept, up_given = fold([(up_kept, up_taken)], flag(*y_step), rows)
+    up_taken = swapped(up_given, *y_step)
+    down_kept, down_given = fold([(down_kept, down_taken)], flag(*x_step), down_kept.shape[1])
+    down_taken = swapped(down_given, *x_step)
+    kernel_taken = swapped(kernel_given, "dp", 1)
     proj_taken = swapped(proj_given, "dp", 1)
-    rows = features // (2 * parts)
-    up_kept, up_taken = [array.reshape(parts, rows, -1) for array in (up_kept, up_taken)]
-    up_kept, up_given = fold(up_kept, up_taken, flag(*y_step))
-    up_taken = swapped(up_given, *y_step)
-    out_kept, out_given = parted_product(
-        branch_low, residual_low, core, out_taken, flag(*y_step), parts
-    )
-    kernel_sum = shards(kernel_kept + kernel_taken, parts)
-    input_grad, proj_taken, up_taken, down_taken, sums, out_given, kernel_sum = hold(
-        (input_grad, proj_taken, up_taken, down_taken, sums, out_given, kernel_sum)
-    )
-
-    input_grad[1] = sent(input_grad[1])
     proj_kept, proj_given = parted_product(
         normed_low, mixed_low, core, proj_taken, flag(*y_step), parts
     )
-    proj_taken = swapped(proj_given, *y_step)
-    down_kept, down_given = fold(down_kept, down_taken, flag(*z_steps[0]))
-    up_kept, up_given = fold(up_kept, up_taken, flag(*z_steps[0]))
-    vectors = [
-        sums_one[0],
-        sums_one[1],
-        sums[12:15].reshape(-1),
-        jnp.swapaxes(sums[:9].reshape(3, 3, features), 1, 2).reshape(-1),
-        sums[9:12].reshape(-1),
-        sums[15],
-        sums_two[2],
-        sums_two[0],
-        sums_two[1],
-        wide_sums[0],
-        sums_two[3],
-    ]
+    output = jnp.concatenate(output, axis=2)
+    vectors = [sums_one[0], sums_one[1]]
+    vectors += [sums[first : first + 3].reshape(-1) for first in range(0, 15, 3)]
+    vectors += [sums[15], sums_two[2], sums_two[0], sums_two[1], wide_sums[0], sums_two[3]]
     sizes = [vector.shape[0] // parts for vector in vectors]
     packed = jnp.concatenate([vector.reshape(parts, -1) for vector in vectors], axis=1)
     packed = jnp.pad(packed, ((0, 0), (0, 4 * rows * 128 - packed.shape[1])))
     packed = packed.reshape(parts, 2, 2 * rows, 128)
     packed_kept = lax.dynamic_index_in_dim(packed, core[0], 1, keepdims=False)
     packed_given = lax.dynamic_index_in_dim(packed, other_core[0], 1, keepdims=False)
-    packed = packed_kept + swapped(packed_given, "dp", 1)
-    rest = jnp.concatenate([kernel_sum, packed.reshape(2 * parts, rows, 128)], axis=2)
-    rest = rest.reshape(parts, 2, rows, -1)
-    rest_kept = lax.dynamic_index_in_dim(rest, flag(*y_step)[0], 1, keepdims=False)
-    rest_given = lax.dynamic_index_in_dim(rest, 1 - flag(*y_step)[0], 1, keepdims=False)
-    rest_kept = jnp.concatenate([out_kept, rest_kept], axis=2)
-    rest_given = jnp.concatenate([out_given, rest_given], axis=2)
-
+    packed_taken = swapped(packed_given, "dp", 1)
+    kernel_kept, kernel_taken = [
+        array.reshape(parts, 2 * rows, -1) for array in (kernel_kept, kernel_taken)
+    ]
+    rest_kept, rest_given = fold(
+        [(kernel_kept, kernel_taken), (packed_kept, packed_taken)], flag(*x_step), 2 * rows
+    )
+    input_grad, down_taken, up_taken, out_taken, proj_given, rest_given, output = hold(
+        (input_grad, down_taken, up_taken, out_taken, proj_given, rest_given, output)
+    )
+
+    input_grad[1] = sent(input_grad[1])
+    proj_taken = swapped(proj_given, *y_step)
+    rest_taken = swapped(rest_given, *x_step)
+    feed_kept, feed_given = fold(
+        [(down_kept, down_taken), (up_kept, up_taken)], flag(*z_steps[0]), rows
+    )
+    feed_taken = swapped(feed_given, *z_steps[0])
+    out_kept, out_given = fold([(out_kept, out_taken)], flag(*x_step), rows)
+    input_grad, proj_taken, rest_taken, out_given, feed_taken = hold(
+        (input_grad, proj_taken, rest_taken, out_given, feed_taken)
+    )
+
+    feed_kept, feed_given = fold([(feed_kept, feed_taken)], flag(*z_steps[1]), rows)
+    feed_given, proj_taken, rest_taken = hold((feed_given, proj_taken, rest_taken))
+    feed_taken = swapped(feed_given, *z_steps[1])
+    out_taken = swapped(out_given, *x_step)
+    proj_kept, proj_given = fold([(proj_kept, proj_taken)], flag(*x_step), rows)
+    proj_taken = swapped(proj_given, *x_step)
+    rest_kept, rest_taken = [array.reshape(parts, rows, -1) for array in (rest_kept, rest_taken)]
+    rest_kept, rest_given = fold([(rest_kept, rest_taken)], flag(*y_step), rows)
     rest_taken = swapped(rest_given, *y_step)
-    input_grad, proj_taken, rest_taken, down_given, up_given = hold(
-        (input_grad, proj_taken, rest_taken, down_given, up_given)
-    )
-    proj_share = reduced(*fold(proj_kept, proj_taken, flag(*x_step)), [x_step] + z_steps)
-    rest = reduced(*fold(rest_kept, rest_taken, flag(*x_step)), [x_step] + z_steps)
-    down_share = reduced(down_kept, down_given, z_steps)
-    up_share = reduced(up_kept, up_given, z_steps)
-    output = jnp.concatenate(output, axis=2)
     input_grad = jnp.concatenate(input_grad, axis=2)
-
-    proj_share = proj_share.reshape(-1, 2, 3, features // 2)
-    proj_share = jnp.swapaxes(proj_share, 1, 2).reshape(-1, 3 * features)
-    columns = rest.shape[1] // 2
-    ends = [features // 2, features // 2 + length // 2, columns]
-    out_share, kernel_share, packed = [
-        jnp.concatenate([rest[:, first:end], rest[:, columns + first : columns + end]], axis=1)
-        for first, end in zip([0] + ends, ends)
-    ]
-    packed = jnp.swapaxes(packed.reshape(2, rows, 2, 128), 1, 2)
-    packed = jnp.swapaxes(packed, 0, 1).reshape(-1)
+    proj_taken, rest_taken, out_taken, feed_taken, input_grad = hold(
+        (proj_taken, rest_taken, out_taken, feed_taken, input_grad)
+    )
+
+    mixer_kept, mixer_given = fold(
+        [(proj_kept, proj_taken), (out_kept, out_taken), (rest_kept, rest_taken)],
+        flag(*z_steps[0]),
+        rows,
+    )
+    mixer_taken = swapped(mixer_given, *z_steps[0])
+    feed_share = (feed_kept + feed_taken)[0]
+    feed_shares = gathered(feed_share)
+    mixer_taken, *feed_shares = hold((mixer_taken, *feed_shares))
+    mixer_kept, mixer_given = fold([(mixer_kept, mixer_taken)], flag(*z_steps[1]), rows)
+    mixer_taken = swapped(mixer_given, *z_steps[1])
+    down_share, up_share = unpacked(
+        feed_shares, [(hidden_units // parts, features), (features // parts, hidden_units)]
+    )
+    mixer_taken, down_share, up_share = hold((mixer_taken, down_share, up_share))
+    mixer_share = (mixer_kept + mixer_taken)[0]
+    proj_share, out_share, kernel_share, packed = unpacked(
+        gathered(mixer_share),
+        [
+            (features // parts, 3 * features),
+            (features // parts, features),
+            (features // parts, length),
+            (4 * rows, 128),
+        ],
+    )
+    packed = packed.reshape(-1)
     ends = np.cumsum(sizes)
     vectors = [packed[end - size : end] for size, end in zip(sizes, ends)]
     return (
@@ -1199,19 +1270,19 @@
         vectors[0],
         vectors[1],
         proj_share,
-        vectors[2],
-        vectors[3].reshape(-1, 3),
-        vectors[4],
+        vectors[6],
+        jnp.stack(vectors[2:5], axis=1),
+        vectors[5],
         kernel_share,
-        vectors[5],
+        vectors[7],
         out_share,
-        vectors[6],
-        vectors[7],
         vectors[8],
+        vectors[9],
+        vectors[10],
         up_share,
-        vectors[9],
+        vectors[11],
         down_share,
-        vectors[10],
+        vectors[12],
     )
 
 

time: 577 us -> 526 us (0.912)
  waiting for transfers between devices: 222 us -> 198 us
  other arithmetic: 39.9 us -> 22.9 us
  local copies, waits for them, and re-layouts: 30.4 us -> 22.6 us
    ppermute x35 -> x32, waiting for transfers between devices: 202 us -> 177 us  [swapped(): return lax.ppermute(array, axis, [(i, i ^ by) for i in range(count)])]
    ppermute x35 -> x32, starting transfers between devices: 35.7 us -> 28.2 us  [swapped(): return lax.ppermute(array, axis, [(i, i ^ by) for i in range(count)])]
    pallas_call x0 -> x2, Pallas kernels: none -> 6 us  [unpacked(): pl.pallas_call(unpack_kernel, in_specs=[pl.BlockSpec(memory_space=pltpu.S...]
    all_to_all x4 -> x5, starting transfers between devices: 19.3 us -> 24.4 us  [sent(): return lax.all_to_all(columns, 'seq', 0, 0, tiled=True)]
    pallas_call x12 -> x10, Pallas kernels: 35 us -> 35.3 us  [fold(): pl.pallas_call(fold_kernel, grid=(count // 2,), in_specs=[pl.BlockSpec(me...]
  transfers between devices with their start and end apart: 41 -> 39, of which waited for: 20 -> 19; matrix products, arithmetic and copies ran while one was open for 9% -> 6% of each run, Pallas kernels for 35% -> 38%
where the time goes in v2:
time: 526 us; the launch traced here: 524 us
  Pallas kernels  217 us (41%)
  waiting for transfers between devices  198 us (38%)
  starting transfers between devices  62.6 us (12%)
  other arithmetic  22.9 us (4%)
  local copies, waits for them, and re-layouts  22.6 us (4%)
    ppermute x32, waiting for transfers between devices, swapped(): return lax.ppermute(array, axis, [(i, i ^ by) for i in range(count)])  177 us
    pallas_call x4, Pallas kernels, by_rows(): pl.pallas_call(kernel, grid=(rows // height,), in_specs=[spec(array.shape...  65.8 us
    pallas_call x1, Pallas kernels, backward_convolution(): pl.pallas_call(backward_kernel, grid=(features // lanes,), in_specs=start...  36.5 us
    pallas_call x10, Pallas kernels, fold(): pl.pallas_call(fold_kernel, grid=(count // 2,), in_specs=[pl.BlockSpec(me...  35.3 us
    pallas_call x4, Pallas kernels, parted_product(): pl.pallas_call(parted_product_kernel, grid_spec=pltpu.PrefetchScalarGridS...  29.4 us
    ppermute x32, starting transfers between devices, swapped(): return lax.ppermute(array, axis, [(i, i ^ by) for i in range(count)])  28.2 us
    all_to_all x5, starting transfers between devices, sent(): return lax.all_to_all(columns, 'seq', 0, 0, tiled=True)  24.4 us
    pallas_call x4, Pallas kernels, half_product(): pl.pallas_call(product_kernel, grid_spec=pltpu.PrefetchScalarGridSpec(num...  24 us
  transfers between devices with their start and end apart: 39, of which 19 were waited for; matrix products, arithmetic and copies ran while one was open for 6% of the time, Pallas kernels for 38%

profile of v2, /device:TPU:0, one launch (start us, length us, event | category | flops | bytes accessed | tf_op | source)
XLA Modules:
  0.0 524.1 jit_solution(9631519276390037009)
XLA Ops:
  22.2 32.5 %collective-permute-done.3 = f32[4,1,192,128]{3,2,0,1:T(8,128)} collective-permute-done((f32[4,1,192,128]{3,2,0,1:T(8,128)S(1)}, f32[4,1,192,128]{3,2,0,1:T(8,128)}, u32[]{:S(2)}, u32[]{:S(2)}) %collective-permute-start.3) | collective-permute-done | bytes 393248 | tf_op jit(solution)/shard_map/ppermute | solution.py:971
  58.2 17.0 %collective-permute-done.4 = f32[8,192,128]{2,1,0:T(8,128)} collective-permute-done((f32[8,192,128]{2,1,0:T(8,128)}, f32[8,192,128]{2,1,0:T(8,128)}, u32[]{:S(2)}, u32[]{:S(2)}) %collective-permute-start.4) | collective-permute-done | bytes 786464 | tf_op jit(solution)/shard_map/ppermute | solution.py:971
  101.2 9.5 %project.1 = (bf16[1024,768]{1,0:T(8,128)(2,1)}, f32[1024,2304]{1,0:T(8,128)}) custom-call(f32[1024,768]{1,0:T(8,128)} %bitcast.52, f32[1,768]{1,0:T(1,128)} %broadcast_in_dim.34.gain_ref, f32[1,768]{1,0:T(1,128)} %broadcast_in_dim.35.bias_ref, bf16[768,2304]{1,0:T(8,128)(2,1)} %weight_ref.3, f32[1,2304]{1,0:T(1,128)} %broadcast_in_dim.36.offset_ref), custom_call_target="tpu_custom_call" | custom-call | tf_op jit(solution)/shard_map/project/pallas_call | solution.py:801
  110.7 19.7 %forward_convolution.1 = (f32[1024,768]{1,0:T(8,128)}, bf16[1024,768]{1,0:T(8,128)(2,1)}) custom-call(s32[2]{0:T(128)} %pad_add_fusion.start_ref, f32[1024,2304]{1,0:T(8,128)} %get-tuple-element.150.outer_ref.inner_ref.value_ref, f32[1024,2304]{1,0:T(8,128)} %get-tuple-element.150.outer_ref.inner_ref.value_ref, ...), custom_call_target="tpu_custom_call" | custom-call | tf_op jit(solution)/shard_map/forward_convolution/pallas_call | solution.py:601
  130.4 24.0 %feed.1 = (f32[1024,768]{1,0:T(8,128)}, bf16[1024,768]{1,0:T(8,128)(2,1)}, bf16[1024,3072]{1,0:T(8,128)(2,1)}, f32[1024,3072]{1,0:T(8,128)}, f32[1024,384]{1,0:T...) custom-call(f32[1024,768]{1,0:T(8,128)} %bitcast.53, bf16[1024,768]{1,0:T(8,128)(2,1)} %get-tuple-element.153.branch_ref.left_ref, ...), custom_call_target="tpu_custom_call" | custom-call | tf_op jit(solution)/shard_map/feed/pallas_call | solution.py:801
  154.4 13.5 %all-to-all-done.1 = f32[8,128,768]{2,1,0:T(8,128)S(1)} async-done(((f32[8,128,768]{2,1,0:T(8,128)}), f32[8,128,768]{2,1,0:T(8,128)S(1)}, u32[]{:S(2)}, u32[]{:S(2)}) %all-to-all-start.1) | async-done | bytes 3145760 | tf_op jit(solution)/shard_map/all_to_all | solution.py:1053
  169.5 7.9 %half_product.4 = f32[3072,384]{1,0:T(8,128)} custom-call(s32[1]{0:T(128)} %sub.38.half_ref, bf16[1024,3072]{1,0:T(8,128)(2,1)} %get-tuple-element.158.left_ref, f32[1024,768]{1,0:T(8,128)} %bitcast.49), custom_call_target="tpu_custom_call" | custom-call | tf_op jit(solution)/shard_map/half_product/pallas_call | solution.py:839
  181.1 22.2 %feed_back.1 = (bf16[1024,3072]{1,0:T(8,128)(2,1)}, f32[1024,768]{1,0:T(8,128)}, bf16[1024,768]{1,0:T(8,128)(2,1)}, f32[1024,768]{1,0:T(8,128)}, f32[4,768]{1,0:T(4,128)}, /*index=5*/f32[1,3072]{1,0:T(1,128)}) custom-call(f32[1024,768]{1,0:T(8,128)} %bitcast.50, f32[1024,768]{1,0:T(8,128)} %get-tuple-element.160.residual_ref, ...), custom_call_target="tpu_custom_call" | custom-call | tf_op jit(solution)/shard_map/feed_back/pallas_call | solution.py:801
  207.0 6.4 %half_product.5 = f32[768,1536]{1,0:T(8,128)} custom-call(s32[1]{0:T(128)} %sub.38.half_ref, bf16[1024,768]{1,0:T(8,128)(2,1)} %get-tuple-element.163.left_ref, bf16[1024,3072]{1,0:T(8,128)(2,1)} %get-tuple-element.164.right_ref), custom_call_target="tpu_custom_call" | custom-call | tf_op jit(solution)/shard_map/half_product/pallas_call | solution.py:839
  224.2 9.6 %parted_product.4 = (f32[8,192,384]{2,1,0:T(8,128)}, f32[8,192,384]{2,1,0:T(8,128)}) custom-call(s32[2]{0:T(128)} %pad_add_fusion.1.bits_ref, bf16[1024,3072]{1,0:T(8,128)(2,1)} %get-tuple-element.158.left_ref, f32[1024,768]{1,0:T(8,128)} %bitcast.51, f32[3072,384]{1,0:T(8,128)} %collective-permute-done.6.taken_ref), custom_call_target="tpu_custom_call" | custom-call | tf_op jit(solution)/shard_map/parted_product/pallas_call | solution.py:872
  239.5 7.8 %parted_product.5 = (f32[4,96,1536]{2,1,0:T(8,128)}, f32[4,96,1536]{2,1,0:T(8,128)}) custom-call(s32[2]{0:T(128)} %pad_add_fusion.2.bits_ref, bf16[1024,768]{1,0:T(8,128)(2,1)} %get-tuple-element.163.left_ref, bf16[1024,3072]{1,0:T(8,128)(2,1)} %get-tuple-element.164.right_ref, f32[768,1536]{1,0:T(8,128)} %collective-permute-done.7.taken_ref), custom_call_target="tpu_custom_call" | custom-call | tf_op jit(solution)/shard_map/parted_product/pallas_call | solution.py:872
  255.7 36.5 %backward_convolution.1 = (bf16[3,1024,768]{2,1,0:T(8,128)(2,1)}, f32[768,512]{1,0:T(8,128)}, f32[768,512]{1,0:T(8,128)}, f32[16,768]{1,0:T(8,128)}) custom-call(s32[2]{0:T(128)} %pad_add_fusion.start_ref, f32[1024,768]{1,0:T(8,128)} %get-tuple-element.180.grad_ref, f32[1024,768]{1,0:T(8,128)} %get-tuple-element.181.convolved_ref, ...), custom_call_target="tpu_custom_call" | custom-call | tf_op jit(solution)/shard_map/backward_convolution/pallas_call | solution.py:621
  292.3 6.1 %half_product.7 = f32[768,1152]{1,0:T(8,128)} custom-call(s32[1]{0:T(128)} %sub.38.half_ref, bf16[1024,768]{1,0:T(8,128)(2,1)} %get-tuple-element.186.left_ref, bf16[3,1024,768]{2,1,0:T(8,128)(2,1)} %get-tuple-element.204.mixed_ref.right_ref), custom_call_target="tpu_custom_call" | custom-call | tf_op jit(solution)/shard_map/half_product/pallas_call | solution.py:839
  298.3 10.1 %input_grad.1 = (f32[1024,512]{1,0:T(8,128)}, f32[1024,256]{1,0:T(8,128)}, f32[2,768]{1,0:T(2,128)}) custom-call(bf16[3,1024,768]{2,1,0:T(8,128)(2,1)} %get-tuple-element.204.mixed_ref.right_ref, bf16[768,2304]{1,0:T(8,128)(2,1)} %weight_ref.3, f32[1024,768]{1,0:T(8,128)} %bitcast.54, f32[1,768]{1,0:T(1,128)} %broadcast_in_dim.34.gain_ref, ...), custom_call_target="tpu_custom_call" | custom-call | tf_op jit(solution)/shard_map/input_grad/pallas_call | solution.py:801
  339.4 7.2 %parted_product.7 = (f32[8,48,1152]{2,1,0:T(8,128)}, f32[8,48,1152]{2,1,0:T(8,128)}) custom-call(s32[2]{0:T(128)} %pad_add_fusion.1.bits_ref, bf16[1024,768]{1,0:T(8,128)(2,1)} %get-tuple-element.186.left_ref, bf16[3,1024,768]{2,1,0:T(8,128)(2,1)} %get-tuple-element.204.mixed_ref.right_ref, f32[768,1152]{1,0:T(8,128)} %collective-permute-done.14.taken_ref), custom_call_target="tpu_custom_call" | custom-call | tf_op jit(solution)/shard_map/parted_product/pallas_call | solution.py:872
  346.6 16.3 %collective-permute-done.13.refs_1_ = f32[8,48,384]{2,1,0:T(8,128)S(1)} collective-permute-done((f32[8,48,384]{2,1,0:T(8,128)S(1)}, f32[8,48,384]{2,1,0:T(8,128)S(1)}, u32[]{:S(2)}, u32[]{:S(2)}) %collective-permute-start.13) | collective-permute-done | bytes 589856 | tf_op jit(solution)/shard_map/ppermute | solution.py:971
  366.0 7.4 %all-to-all-start.6 = ((f32[8,128,256]{2,1,0:T(8,128)}), f32[8,128,256]{2,1,0:T(8,128)S(1)}, u32[]{:S(2)}, u32[]{:S(2)}) async-start(f32[8,128,256]{2,1,0:T(8,128)} %bitcast.61), calls=%async_computation.6 | async-start | bytes 2097152 | tf_op jit(solution)/shard_map/all_to_all | solution.py:1099
  384.3 24.5 %collective-permute-done.18 = f32[4,96,640]{2,1,0:T(8,128)} collective-permute-done((f32[4,96,640]{2,1,0:T(8,128)}, f32[4,96,640]{2,1,0:T(8,128)}, u32[]{:S(2)}, u32[]{:S(2)}) %collective-permute-start.18) | collective-permute-done | bytes 983072 | tf_op jit(solution)/shard_map/ppermute | solution.py:971
  408.7 9.4 %collective-permute-done.19.refs_1_ = f32[2,48,3072]{2,1,0:T(8,128)} collective-permute-done((f32[2,48,3072]{2,1,0:T(8,128)}, f32[2,48,3072]{2,1,0:T(8,128)}, u32[]{:S(2)}, u32[]{:S(2)}) %collective-permute-start.19) | collective-permute-done | bytes 1179680 | tf_op jit(solution)/shard_map/ppermute | solution.py:971
  435.6 16.4 %collective-permute-done.22.refs_3_ = f32[4,48,384]{2,1,0:T(8,128)S(1)} collective-permute-done((f32[4,48,384]{2,1,0:T(8,128)S(1)}, f32[4,48,384]{2,1,0:T(8,128)S(1)}, u32[]{:S(2)}, u32[]{:S(2)}) %collective-permute-start.22) | collective-permute-done | bytes 294944 | tf_op jit(solution)/shard_map/ppermute | solution.py:971
  457.7 11.5 %collective-permute-done.25.y_ref = f32[48,3072]{1,0:T(8,128)S(1)} collective-permute-done((f32[48,3072]{1,0:T(8,128)S(1)}, f32[48,3072]{1,0:T(8,128)S(1)}, u32[]{:S(2)}, u32[]{:S(2)}) %collective-permute-start.25) | collective-permute-done | bytes 589856 | tf_op jit(solution)/shard_map/ppermute | solution.py:971
  469.2 9.1 %collective-permute-done.24.refs_1_ = f32[2,48,2176]{2,1,0:T(8,128)S(1)} collective-permute-done((f32[2,48,2176]{2,1,0:T(8,128)}, f32[2,48,2176]{2,1,0:T(8,128)S(1)}, u32[]{:S(2)}, u32[]{:S(2)}) %collective-permute-start.24) | collective-permute-done | bytes 835616 | tf_op jit(solution)/shard_map/ppermute | solution.py:971
  485.3 17.0 %collective-permute-done.28 = f32[1,48,2176]{2,1,0:T(8,128)S(1)} collective-permute-done((f32[1,48,2176]{2,1,0:T(8,128)}, f32[1,48,2176]{2,1,0:T(8,128)S(1)}, u32[]{:S(2)}, u32[]{:S(2)}) %collective-permute-start.28) | collective-permute-done | bytes 417824 | tf_op jit(solution)/shard_map/ppermute | solution.py:971
  503.2 10.8 %collective-permute-done.29.y_ref = f32[48,2176]{1,0:T(8,128)S(1)} collective-permute-done((f32[48,2176]{1,0:T(8,128)S(1)}, f32[48,2176]{1,0:T(8,128)S(1)}, u32[]{:S(2)}, u32[]{:S(2)}) %collective-permute-start.29) | collective-permute-done | bytes 417824 | tf_op jit(solution)/shard_map/ppermute | solution.py:971
  (231 shorter events, 170.3 us)
Async XLA Ops:
  15.3 74.4 %all-to-all-start = ((f32[8,128,768]{2,1,0:T(8,128)}), f32[8,128,768]{2,1,0:T(8,128)S(1)}, u32[]{:S(2)}, u32[]{:S(2)}) async-start(f32[8,128,768]{2,1,0:T(8,128)} %convert_element_type.8), calls=%async_computation | async-start | bytes 6291456 | tf_op jit(solution)/shard_map/all_to_all | solution.py:1044
  20.1 34.5 %collective-permute-start.3 = (f32[4,1,192,128]{3,2,0,1:T(8,128)S(1)}, f32[4,1,192,128]{3,2,0,1:T(8,128)}, u32[]{:S(2)}, u32[]{:S(2)}) collective-permute-start(f32[4,1,192,128]{3,2,0,1:T(8,128)S(1)} %bitcast.59), channel_id=1, source_target_pairs={{0,1},{1,0},{2,3},{3,2},{4,5},{5,4},{6,7},{7,6},{8,9},{9,8},{10,11... | collective-permute-start | bytes 1179656 | tf_op jit(solution)/shard_map/ppermute | solution.py:971
  91.3 76.6 %all-to-all-start.1 = ((f32[8,128,768]{2,1,0:T(8,128)}), f32[8,128,768]{2,1,0:T(8,128)S(1)}, u32[]{:S(2)}, u32[]{:S(2)}) async-start(f32[8,128,768]{2,1,0:T(8,128)} %convert_element_type.9), calls=%async_computation.1 | async-start | bytes 6291456 | tf_op jit(solution)/shard_map/all_to_all | solution.py:1053
  177.4 41.5 %collective-permute-start.6 = (f32[3072,384]{1,0:T(8,128)}, f32[3072,384]{1,0:T(8,128)}, u32[]{:S(2)}, u32[]{:S(2)}) collective-permute-start(f32[3072,384]{1,0:T(8,128)} %half_product.4), channel_id=1, source_target_pairs={{0,8},{8,0},{16,24},{24,16},{1,9},{9,1},{17,25},{25,17},{2,10},{10... | collective-permute-start | bytes 14155784 | tf_op jit(solution)/shard_map/ppermute | solution.py:971
  177.4 41.5 %all-to-all-start.2 = ((f32[8,128,384]{2,1,0:T(8,128)}), f32[8,128,384]{2,1,0:T(8,128)S(1)}, u32[]{:S(2)}, u32[]{:S(2)}) async-start(f32[8,128,384]{2,1,0:T(8,128)} %bitcast.58), calls=%async_computation.2 | async-start | bytes 3145728 | tf_op jit(solution)/shard_map/all_to_all | solution.py:1099
  218.8 20.6 %collective-permute-start.7 = (f32[768,1536]{1,0:T(8,128)}, f32[768,1536]{1,0:T(8,128)}, u32[]{:S(2)}, u32[]{:S(2)}) collective-permute-start(f32[768,1536]{1,0:T(8,128)} %half_product.5), channel_id=1, source_target_pairs={{0,8},{8,0},{16,24},{24,16},{1,9},{9,1},{17,25},{25,17},{2,10},{10... | collective-permute-start | bytes 14155784 | tf_op jit(solution)/shard_map/ppermute | solution.py:971
  218.9 30.2 %all-to-all-start.3 = ((f32[8,128,256]{2,1,0:T(8,128)}), f32[8,128,256]{2,1,0:T(8,128)S(1)}, u32[]{:S(2)}, u32[]{:S(2)}) async-start(f32[8,128,256]{2,1,0:T(8,128)} %bitcast.62), calls=%async_computation.3 | async-start | bytes 2097152 | tf_op jit(solution)/shard_map/all_to_all | solution.py:1099
  249.1 59.4 %collective-permute-start.10 = (f32[4,96,1536]{2,1,0:T(8,128)}, f32[4,96,1536]{2,1,0:T(8,128)}, u32[]{:S(2)}, u32[]{:S(2)}) collective-permute-start(f32[4,96,1536]{2,1,0:T(8,128)} %get-tuple-element.189), channel_id=1, source_target_pairs={{0,1},{1,0},{2,3},{3,2},{4,5},{5,4},{6,7},{7,6},{8,9},{9,8},{10,11... | collective-permute-start | bytes 7077896 | tf_op jit(solution)/shard_map/ppermute | solution.py:971
  250.5 58.0 %collective-permute-start.9 = (f32[8,192,384]{2,1,0:T(8,128)}, f32[8,192,384]{2,1,0:T(8,128)}, u32[]{:S(2)}, u32[]{:S(2)}) collective-permute-start(f32[8,192,384]{2,1,0:T(8,128)} %get-tuple-element.188), channel_id=1, source_target_pairs={{0,16},{8,24},{16,0},{24,8},{1,17},{9,25},{17,1},{25,9},{2,18},{10... | collective-permute-start | bytes 7077896 | tf_op jit(solution)/shard_map/ppermute | solution.py:971
  252.0 56.4 %all-to-all-start.4 = ((f32[8,128,128]{2,1,0:T(8,128)}), f32[8,128,128]{2,1,0:T(8,128)S(1)}, u32[]{:S(2)}, u32[]{:S(2)}) async-start(f32[8,128,128]{2,1,0:T(8,128)} %bitcast.17), calls=%async_computation.4 | async-start | bytes 1048576 | tf_op jit(solution)/shard_map/all_to_all | solution.py:1099
  309.2 56.8 %all-to-all-start.5 = ((f32[8,128,512]{2,1,0:T(8,128)}), f32[8,128,512]{2,1,0:T(8,128)S(1)}, u32[]{:S(2)}, u32[]{:S(2)}) async-start(f32[8,128,512]{2,1,0:T(8,128)} %bitcast.57), calls=%async_computation.5 | async-start | bytes 4194304 | tf_op jit(solution)/shard_map/all_to_all | solution.py:1099
  315.1 24.3 %collective-permute-start.14 = (f32[768,1152]{1,0:T(8,128)}, f32[768,1152]{1,0:T(8,128)}, u32[]{:S(2)}, u32[]{:S(2)}) collective-permute-start(f32[768,1152]{1,0:T(8,128)} %half_product.7), channel_id=1, source_target_pairs={{0,8},{8,0},{16,24},{24,16},{1,9},{9,1},{17,25},{25,17},{2,10},{10... | collective-permute-start | bytes 10616840 | tf_op jit(solution)/shard_map/ppermute | solution.py:971
  322.2 40.8 %collective-permute-start.12 = (f32[4,48,1536]{2,1,0:T(8,128)}, f32[4,48,1536]{2,1,0:T(8,128)}, u32[]{:S(2)}, u32[]{:S(2)}) collective-permute-start(f32[4,48,1536]{2,1,0:T(8,128)} %get-tuple-element.202), channel_id=1, source_target_pairs={{0,16},{8,24},{16,0},{24,8},{1,17},{9,25},{17,1},{25,9},{2,18},{10... | collective-permute-start | bytes 3538952 | tf_op jit(solution)/shard_map/ppermute | solution.py:971
  327.0 39.0 %collective-permute-start.11 = (f32[4,192,384]{2,1,0:T(8,128)}, f32[4,192,384]{2,1,0:T(8,128)}, u32[]{:S(2)}, u32[]{:S(2)}) collective-permute-start(f32[4,192,384]{2,1,0:T(8,128)} %get-tuple-element.199), channel_id=1, source_target_pairs={{0,1},{1,0},{2,3},{3,2},{4,5},{5,4},{6,7},{7,6},{8,9},{9,8},{10,11... | collective-permute-start | bytes 3538952 | tf_op jit(solution)/shard_map/ppermute | solution.py:971
  331.9 31.0 %collective-permute-start.13 = (f32[8,48,384]{2,1,0:T(8,128)S(1)}, f32[8,48,384]{2,1,0:T(8,128)S(1)}, u32[]{:S(2)}, u32[]{:S(2)}) collective-permute-start(f32[8,48,384]{2,1,0:T(8,128)S(1)} %copy-done.41), channel_id=1, source_target_pairs={{0,16},{8,24},{16,0},{24,8},{1,17},{9,25},{17,1},{25,9},{2,18},{10... | collective-permute-start | bytes 1769480 | tf_op jit(solution)/shard_map/ppermute | solution.py:971
  366.0 52.2 %all-to-all-start.6 = ((f32[8,128,256]{2,1,0:T(8,128)}), f32[8,128,256]{2,1,0:T(8,128)S(1)}, u32[]{:S(2)}, u32[]{:S(2)}) async-start(f32[8,128,256]{2,1,0:T(8,128)} %bitcast.61), calls=%async_computation.6 | async-start | bytes 2097152 | tf_op jit(solution)/shard_map/all_to_all | solution.py:1099
  373.4 44.8 %collective-permute-start.17 = (f32[8,48,1152]{2,1,0:T(8,128)}, f32[8,48,1152]{2,1,0:T(8,128)}, u32[]{:S(2)}, u32[]{:S(2)}) collective-permute-start(f32[8,48,1152]{2,1,0:T(8,128)} %get-tuple-element.226), channel_id=1, source_target_pairs={{0,16},{8,24},{16,0},{24,8},{1,17},{9,25},{17,1},{25,9},{2,18},{10... | collective-permute-start | bytes 5308424 | tf_op jit(solution)/shard_map/ppermute | solution.py:971
  377.4 40.7 %collective-permute-start.19 = (f32[2,48,3072]{2,1,0:T(8,128)}, f32[2,48,3072]{2,1,0:T(8,128)}, u32[]{:S(2)}, u32[]{:S(2)}) collective-permute-start(f32[2,48,3072]{2,1,0:T(8,128)} %get-tuple-element.231), channel_id=1, source_target_pairs={{0,2},{1,3},{2,0},{3,1},{4,6},{5,7},{6,4},{7,5},{8,10},{9,11},{10,... | collective-permute-start | bytes 3538952 | tf_op jit(solution)/shard_map/ppermute | solution.py:971
  379.5 29.3 %collective-permute-start.18 = (f32[4,96,640]{2,1,0:T(8,128)}, f32[4,96,640]{2,1,0:T(8,128)}, u32[]{:S(2)}, u32[]{:S(2)}) collective-permute-start(f32[4,96,640]{2,1,0:T(8,128)} %get-tuple-element.227), channel_id=1, source_target_pairs={{0,1},{1,0},{2,3},{3,2},{4,5},{5,4},{6,7},{7,6},{8,9},{9,8},{10,11... | collective-permute-start | bytes 2949128 | tf_op jit(solution)/shard_map/ppermute | solution.py:971
  425.0 28.7 %collective-permute-start.20 = (f32[4,48,1152]{2,1,0:T(8,128)}, f32[4,48,1152]{2,1,0:T(8,128)S(1)}, u32[]{:S(2)}, u32[]{:S(2)}) collective-permute-start(f32[4,48,1152]{2,1,0:T(8,128)} %get-tuple-element.237), channel_id=1, source_target_pairs={{0,1},{1,0},{2,3},{3,2},{4,5},{5,4},{6,7},{7,6},{8,9},{9,8},{10,11... | collective-permute-start | bytes 2654216 | tf_op jit(solution)/shard_map/ppermute | solution.py:971
  426.4 27.3 %collective-permute-start.23 = (f32[1,48,3072]{2,1,0:T(8,128)S(1)}, f32[1,48,3072]{2,1,0:T(8,128)S(1)}, u32[]{:S(2)}, u32[]{:S(2)}) collective-permute-start(f32[1,48,3072]{2,1,0:T(8,128)S(1)} %copy-done.42), channel_id=1, source_target_pairs={{0,4},{1,5},{2,6},{3,7},{4,0},{5,1},{6,2},{7,3},{8,12},{9,13},{10,... | collective-permute-start | bytes 1769480 | tf_op jit(solution)/shard_map/ppermute | solution.py:971
  432.4 19.5 %collective-permute-start.21 = (f32[4,48,640]{2,1,0:T(8,128)}, f32[4,48,640]{2,1,0:T(8,128)S(1)}, u32[]{:S(2)}, u32[]{:S(2)}) collective-permute-start(f32[4,48,640]{2,1,0:T(8,128)} %get-tuple-element.240), channel_id=1, source_target_pairs={{0,16},{8,24},{16,0},{24,8},{1,17},{9,25},{17,1},{25,9},{2,18},{10... | collective-permute-start | bytes 1474568 | tf_op jit(solution)/shard_map/ppermute | solution.py:971
  457.6 20.7 %collective-permute-start.24 = (f32[2,48,2176]{2,1,0:T(8,128)}, f32[2,48,2176]{2,1,0:T(8,128)S(1)}, u32[]{:S(2)}, u32[]{:S(2)}) collective-permute-start(f32[2,48,2176]{2,1,0:T(8,128)} %get-tuple-element.253), channel_id=1, source_target_pairs={{0,2},{1,3},{2,0},{3,1},{4,6},{5,7},{6,4},{7,5},{8,10},{9,11},{10,... | collective-permute-start | bytes 2506760 | tf_op jit(solution)/shard_map/ppermute | solution.py:971
  481.6 20.8 %collective-permute-start.28 = (f32[1,48,2176]{2,1,0:T(8,128)}, f32[1,48,2176]{2,1,0:T(8,128)S(1)}, u32[]{:S(2)}, u32[]{:S(2)}) collective-permute-start(f32[1,48,2176]{2,1,0:T(8,128)} %get-tuple-element.258), channel_id=1, source_target_pairs={{0,4},{1,5},{2,6},{3,7},{4,0},{5,1},{6,2},{7,3},{8,12},{9,13},{10,... | collective-permute-start | bytes 1253384 | tf_op jit(solution)/shard_map/ppermute | solution.py:971
  (60 other events, 508.0 us)

commit v3 on v2

--- a/solution.py
+++ b/solution.py
@@ -358,20 +358,15 @@
     return high, low
 
 
-def earlier(values, by):
-    rows = lax.broadcasted_iota(jnp.int32, values.shape, 0)
-    return jnp.where(rows >= by, pltpu.roll(values, by, 0), 0.0)
-
-
-def later(values, by):
-    count = values.shape[0]
-    rows = lax.broadcasted_iota(jnp.int32, values.shape, 0)
-    return jnp.where(rows < count - by, pltpu.roll(values, count - by, 0), 0.0)
-
-
-def short_filtered(mixed, taps):
+def short_filtered(padded_ref, mixed_ref, taps):
+    count, lanes = mixed_ref.shape
+    padded_ref[:8] = jnp.zeros((8, lanes), jnp.float32)
+    padded_ref[8 : 8 + count] = mixed_ref[...]
     return (
-        taps[0:1] * earlier(mixed, 2) + taps[1:2] * earlier(mixed, 1) + taps[2:3] * mixed + taps[3:4]
+        taps[0:1] * padded_ref[6 : 6 + count]
+        + taps[1:2] * padded_ref[7 : 7 + count]
+        + taps[2:3] * mixed_ref[...]
+        + taps[3:4]
     )
 
 
@@ -435,28 +430,29 @@
         left_imag = [left_ref[block, imag_rows] for block in range(blocks)]
         right_real = [right_ref[block, real_rows] for block in range(blocks)]
         right_imag = [right_ref[block, imag_rows] for block in range(blocks)]
+        left_sum = [
+            real - imag if reverse else real + imag for real, imag in zip(left_real, left_imag)
+        ]
+        right_sum = [real + imag for real, imag in zip(right_real, right_imag)]
+        right_gap = [imag - real for real, imag in zip(right_real, right_imag)]
         for m in range(blocks):
-            real = imag = None
+            one = two = three = 0.0
             for l in range(blocks - m if reverse else m + 1):
                 r = m + l if reverse else m - l
-                if reverse:
-                    new_real = left_real[l] * right_real[r] + left_imag[l] * right_imag[r]
-                    new_imag = left_real[l] * right_imag[r] - left_imag[l] * right_real[r]
-                else:
-                    new_real = left_real[l] * right_real[r] - left_imag[l] * right_imag[r]
-                    new_imag = left_real[l] * right_imag[r] + left_imag[l] * right_real[r]
-                real = new_real if real is None else real + new_real
-                imag = new_imag if imag is None else imag + new_imag
-            out_ref[m, real_rows] = real
-            out_ref[m, imag_rows] = imag
+                one = one + right_real[r] * left_sum[l]
+                two = two + left_real[l] * right_gap[r]
+                three = three + left_imag[l] * right_sum[r]
+            out_ref[m, real_rows] = one + three if reverse else one - three
+            out_ref[m, imag_rows] = one + two
         return carry
 
-    lax.fori_loop(0, width // 8, step, 0)
-
-
-def gates(start_ref, mixed_refs, taps_ref):
+    lax.fori_loop(0, width // 8, step, 0, unroll=2)
+
+
+def gates(start_ref, mixed_refs, taps_ref, padded_ref):
     outer, inner, values = [
-        short_filtered(ref[...], taps_ref[group]) for group, ref in enumerate(mixed_refs)
+        short_filtered(padded_ref.at[group], ref, taps_ref[group])
+        for group, ref in enumerate(mixed_refs)
     ]
     rows = lax.broadcasted_iota(jnp.int32, outer.shape, 0)
     live = (rows >= start_ref[0]).astype(jnp.float32)
@@ -478,9 +474,10 @@
     signal_spectra,
     kernel_spectra,
     spectra,
+    padded,
 ):
     width = kernel_ref.shape[2]
-    outer, inner, values, live = gates(start_ref, (outer_ref, inner_ref, value_ref), taps_ref)
+    outer, inner, values, live = gates(start_ref, (outer_ref, inner_ref, value_ref), taps_ref, padded)
     gated = values * inner * live
     analyse(gated, analysis_ref, signal_spectra)
     analyse_kernel(kernel_ref, analysis_ref, kernel_spectra)
@@ -524,10 +521,11 @@
     kernel_spectra,
     grad_spectra,
     spectra,
+    padded,
 ):
     width = kernel_ref.shape[2]
     mixed_refs = (outer_ref, inner_ref, value_ref)
-    outer, inner, values, live = gates(start_ref, mixed_refs, taps_ref)
+    outer, inner, values, live = gates(start_ref, mixed_refs, taps_ref, padded)
     gated = values * inner * live
     branch_grad = grad_ref[...]
     conv_grad = branch_grad * outer
@@ -551,11 +549,14 @@
     def total(array):
         return jnp.sum(array, axis=0, keepdims=True)
 
+    count = outer.shape[0]
     filter_rows, bias_rows, low_rows = [], [], []
     grads = (outer_grad, gated_grad * values, gated_grad * inner)
     for group in range(3):
         grad, mixed, taps = grads[group], mixed_refs[group][...], taps_ref[group]
-        next_one, next_two = later(grad, 1), later(grad, 2)
+        padded[group, :count] = grad
+        padded[group, count : count + 8] = jnp.zeros((8, grad.shape[1]), jnp.float32)
+        next_one, next_two = padded[group, 1 : 1 + count], padded[group, 2 : 2 + count]
         mixed_grad = taps[2:3] * grad + taps[1:2] * next_one + taps[0:1] * next_two
         low = mixed_grad.astype(jnp.bfloat16)
         mixed_grad_ref[group] = low
@@ -607,7 +608,7 @@
             jax.ShapeDtypeStruct((tokens, features), jnp.float32),
             jax.ShapeDtypeStruct((tokens, features), jnp.bfloat16),
         ),
-        scratch_shapes=[spectra] * 3,
+        scratch_shapes=[spectra] * 3 + [pltpu.VMEM((3, tokens + 8, lanes), jnp.float32)],
         compiler_params=kernel_parameters(),
         cost_estimate=NO_COST,
         name="forward_convolution",
@@ -634,7 +635,7 @@
             jax.ShapeDtypeStruct((features, tokens // 2), jnp.float32),
             jax.ShapeDtypeStruct((16, features), jnp.float32),
         ),
-        scratch_shapes=[spectra] * 4,
+        scratch_shapes=[spectra] * 4 + [pltpu.VMEM((3, tokens + 8, lanes), jnp.float32)],
         compiler_params=kernel_parameters(),
         cost_estimate=NO_COST,
         name="backward_convolution",
@@ -851,24 +852,52 @@
     )(half, left, right)
 
 
-def parted_product_kernel(bits_ref, left_ref, right_ref, taken_ref, kept_ref, given_ref):
+def whole_product_kernel(left_ref, right_ref, out_ref):
+    out_ref[...] = product(left_ref[...], right_ref[...])
+
+
+def whole_product(left, right):
+    tokens, rows = left.shape
+    return pl.pallas_call(
+        whole_product_kernel,
+        grid=(right.shape[1] // rows,),
+        in_specs=[
+            pl.BlockSpec((tokens, rows), lambda step: (0, 0)),
+            pl.BlockSpec((tokens, rows), lambda step: (0, step)),
+        ],
+        out_specs=pl.BlockSpec((rows, rows), lambda step: (0, step)),
+        out_shape=jax.ShapeDtypeStruct((rows, right.shape[1]), jnp.float32),
+        compiler_params=kernel_parameters(),
+        cost_estimate=NO_COST,
+        name="whole_product",
+    )(left, right)
+
+
+def parted_product_kernel(bits_ref, left_ref, right_ref, taken_ref, *out_refs):
     total = product_tile(left_ref, right_ref) + taken_ref[...]
-    pieces, rows, _ = kept_ref.shape
-    first = bits_ref[1] == 0
-    for piece in range(pieces):
-        one = total[2 * piece * rows : (2 * piece + 1) * rows]
-        two = total[(2 * piece + 1) * rows : (2 * piece + 2) * rows]
-        kept_ref[piece] = jnp.where(first, one, two)
-        given_ref[piece] = jnp.where(first, two, one)
-
-
-def parted_product(left, right, half, taken, which, pieces, tile=384):
+    left = 0
+    for part in range(len(out_refs) // 2):
+        kept_ref, given_ref = out_refs[2 * part : 2 * part + 2]
+        pieces, rows, columns = kept_ref.shape
+        first = bits_ref[1 + part] == 0
+        for piece in range(pieces):
+            one = total[2 * piece * rows : (2 * piece + 1) * rows, left : left + columns]
+            two = total[(2 * piece + 1) * rows : (2 * piece + 2) * rows, left : left + columns]
+            kept_ref[piece] = jnp.where(first, one, two)
+            given_ref[piece] = jnp.where(first, two, one)
+        left += columns
+
+
+def parted_product(left, right, half, taken, plan, tile=384):
     rows = left.shape[1]
     columns, left_spec, right_spec = product_specs(left, right, tile)
-    height = rows // (2 * pieces)
     steps = rows // tile
-    part = pl.BlockSpec((pieces // steps, height, columns), lambda step, bits_ref: (step, 0, 0))
-    shape = jax.ShapeDtypeStruct((pieces, height, columns), jnp.float32)
+    specs, shapes = [], []
+    for _, pieces in plan:
+        shape = (pieces, rows // (2 * pieces), columns // len(plan))
+        block = (pieces // steps,) + shape[1:]
+        specs += [pl.BlockSpec(block, lambda step, bits_ref: (step, 0, 0))] * 2
+        shapes += [jax.ShapeDtypeStruct(shape, jnp.float32)] * 2
     return pl.pallas_call(
         parted_product_kernel,
         grid_spec=pltpu.PrefetchScalarGridSpec(
@@ -879,13 +908,13 @@
                 right_spec,
                 pl.BlockSpec((tile, columns), lambda step, bits_ref: (step, 0)),
             ],
-            out_specs=(part, part),
+            out_specs=tuple(specs),
         ),
-        out_shape=(shape, shape),
+        out_shape=tuple(shapes),
         compiler_params=kernel_parameters(),
         cost_estimate=NO_COST,
         name="parted_product",
-    )(jnp.concatenate([half, which]), left, right, taken)
+    )(jnp.concatenate([half] + [which for which, _ in plan]), left, right, taken)
 
 
 def fold_kernel(bit_ref, *refs):
@@ -904,15 +933,19 @@
 
 def fold(pairs, which, height):
     count = pairs[0][0].shape[0]
-    operands = [array for pair in pairs for array in pair]
-    columns = sum(kept.shape[1] // height * kept.shape[2] for kept, _ in pairs)
+    operands, specs, columns = [], [], 0
+    for kept, taken, *share in pairs:
+        place, shares = share if share else (0, 1)
+        block = (2, kept.shape[1], kept.shape[2] // shares)
+        operands += [kept, taken]
+        specs += [pl.BlockSpec(block, lambda step, place=place: (step, 0, place))] * 2
+        columns += block[1] // height * block[2]
     one = pl.BlockSpec((1, height, columns), lambda step: (step, 0, 0))
     shape = jax.ShapeDtypeStruct((count // 2, height, columns), jnp.float32)
     return pl.pallas_call(
         fold_kernel,
         grid=(count // 2,),
-        in_specs=[pl.BlockSpec(memory_space=pltpu.SMEM)]
-        + [pl.BlockSpec((2,) + array.shape[1:], lambda step: (step, 0, 0)) for array in operands],
+        in_specs=[pl.BlockSpec(memory_space=pltpu.SMEM)] + specs,
         out_specs=(one, one),
         out_shape=(shape, shape),
         compiler_params=kernel_parameters(),
@@ -1087,9 +1120,8 @@
             ((length, features), low),
             ((length, hidden_units), low),
             ((length, hidden_units), single),
-            ((length, features // 2), single),
             ((length, features // 3), single),
-            ((length, features // 6), single),
+            ((length, features * 2 // 3), single),
         ],
     )
     upstream, output = hold((upstream, output))
@@ -1102,7 +1134,6 @@
     upstream = upstream.reshape(length, features)
     down_given = half_product(activated_low, upstream, other_core, 768)
     upstream, down_given = hold((upstream, down_given))
-
     down_taken = swapped(down_given, "dp", 1)
     expanded_low, residual_grad, residual_low, branch_grad, sums_two, wide_sums = by_rows(
         feed_back_kernel,
@@ -1126,31 +1157,17 @@
             ((1, hidden_units), single),
         ],
     )
-    up_given = half_product(normed_two_low, expanded_low, other_core)
-    out_given = half_product(branch_low, residual_low, other_core, 768)
-    branch_grad, up_given, out_given, down_taken, output = hold(
-        (branch_grad, up_given, out_given, down_taken, output)
-    )
+    expanded_low, residual_low, branch_grad = hold((expanded_low, residual_low, branch_grad))
+    side = whole_product(normed_two_low, expanded_low)
+    side, down_taken, output = hold((side, down_taken, output))
+    side = lax.psum_scatter(side, ("seq", "dp"), scatter_dimension=0, tiled=True)
+    down_kept, down_given = parted_product(
+        activated_low, upstream, core, down_taken, [(flag(*y_step), parts)], 768
+    )
+    branch_grad, down_given = hold((branch_grad, down_given))
 
     output[1] = sent(output[1])
-    up_taken = swapped(up_given, "dp", 1)
-    out_taken = swapped(out_given, "dp", 1)
-    down_kept, down_given = parted_product(
-        activated_low, upstream, core, down_taken, flag(*y_step), parts, 768
-    )
-    up_kept, up_given = parted_product(
-        normed_two_low, expanded_low, core, up_taken, flag(*x_step), parts // 2
-    )
-    out_kept, out_given = parted_product(
-        branch_low, residual_low, core, out_taken, flag(*y_step), parts, 768
-    )
-    branch_grad, down_given, up_given, out_given, output = hold(
-        (branch_grad, down_given, up_given, out_given, output)
-    )
-
-    output[2] = sent(output[2])
     down_taken = swapped(down_given, *y_step)
-    up_taken = swapped(up_given, *x_step)
     mixed_low, kernel_kept, kernel_given, sums = backward_convolution(
         scalars, branch_grad, convolved, mixed, kernel, taps, skip, tables
     )
@@ -1172,22 +1189,25 @@
             ((2, features), single),
         ],
     )
-    input_grad, mixed_low, proj_given, kernel_given, down_taken, up_taken, sums_one, sums, output = hold(
-        (input_grad, mixed_low, proj_given, kernel_given, down_taken, up_taken, sums_one, sums, output)
+    input_grad, mixed_low, proj_given, kernel_given, down_taken, sums_one, sums, output = hold(
+        (input_grad, mixed_low, proj_given, kernel_given, down_taken, sums_one, sums, output)
     )
 
     rows = features // (2 * parts)
     input_grad[0] = sent(input_grad[0])
-    out_taken = swapped(out_given, *y_step)
-    up_kept, up_taken = [array.reshape(parts, rows, -1) for array in (up_kept, up_taken)]
-    up_kept, up_given = fold([(up_kept, up_taken)], flag(*y_step), rows)
-    up_taken = swapped(up_given, *y_step)
     down_kept, down_given = fold([(down_kept, down_taken)], flag(*x_step), down_kept.shape[1])
     down_taken = swapped(down_given, *x_step)
     kernel_taken = swapped(kernel_given, "dp", 1)
     proj_taken = swapped(proj_given, "dp", 1)
     proj_kept, proj_given = parted_product(
-        normed_low, mixed_low, core, proj_taken, flag(*y_step), parts
+        normed_low, mixed_low, core, proj_taken, [(flag(*y_step), parts)]
+    )
+    proj_given, residual_low = hold((proj_given, residual_low))
+    proj_taken = swapped(proj_given, *y_step)
+    out_given = half_product(branch_low, residual_low, other_core, 768)
+    out_taken = swapped(out_given, "dp", 1)
+    out_kept, out_given = parted_product(
+        branch_low, residual_low, core, out_taken, [(flag(*y_step), parts)], 768
     )
     output = jnp.concatenate(output, axis=2)
     vectors = [sums_one[0], sums_one[1]]
@@ -1203,54 +1223,49 @@
     kernel_kept, kernel_taken = [
         array.reshape(parts, 2 * rows, -1) for array in (kernel_kept, kernel_taken)
     ]
+    kernel_kept, kernel_taken, packed_kept, packed_taken = [
+        array.reshape(2 * parts, rows, -1)
+        for array in (kernel_kept, kernel_taken, packed_kept, packed_taken)
+    ]
     rest_kept, rest_given = fold(
-        [(kernel_kept, kernel_taken), (packed_kept, packed_taken)], flag(*x_step), 2 * rows
-    )
-    input_grad, down_taken, up_taken, out_taken, proj_given, rest_given, output = hold(
-        (input_grad, down_taken, up_taken, out_taken, proj_given, rest_given, output)
+        [(kernel_kept, kernel_taken), (packed_kept, packed_taken)], flag(*y_step), rows
+    )
+    input_grad, down_taken, proj_taken, rest_given, out_given, output = hold(
+        (input_grad, down_taken, proj_taken, rest_given, out_given, output)
     )
 
     input_grad[1] = sent(input_grad[1])
-    proj_taken = swapped(proj_given, *y_step)
-    rest_taken = swapped(rest_given, *x_step)
-    feed_kept, feed_given = fold(
-        [(down_kept, down_taken), (up_kept, up_taken)], flag(*z_steps[0]), rows
-    )
-    feed_taken = swapped(feed_given, *z_steps[0])
-    out_kept, out_given = fold([(out_kept, out_taken)], flag(*x_step), rows)
-    input_grad, proj_taken, rest_taken, out_given, feed_taken = hold(
-        (input_grad, proj_taken, rest_taken, out_given, feed_taken)
-    )
-
-    feed_kept, feed_given = fold([(feed_kept, feed_taken)], flag(*z_steps[1]), rows)
-    feed_given, proj_taken, rest_taken = hold((feed_given, proj_taken, rest_taken))
-    feed_taken = swapped(feed_given, *z_steps[1])
-    out_taken = swapped(out_given, *x_step)
+    rest_taken = swapped(rest_given, *y_step)
+    out_taken = swapped(out_given, *y_step)
     proj_kept, proj_given = fold([(proj_kept, proj_taken)], flag(*x_step), rows)
     proj_taken = swapped(proj_given, *x_step)
-    rest_kept, rest_taken = [array.reshape(parts, rows, -1) for array in (rest_kept, rest_taken)]
-    rest_kept, rest_given = fold([(rest_kept, rest_taken)], flag(*y_step), rows)
-    rest_taken = swapped(rest_given, *y_step)
+    feed_kept, feed_given = fold([(down_kept, down_taken)], flag(*z_steps[0]), rows)
+    feed_taken = swapped(feed_given, *z_steps[0])
+    input_grad, proj_taken, rest_taken, out_taken, feed_taken = hold(
+        (input_grad, proj_taken, rest_taken, out_taken, feed_taken)
+    )
+
+    rest_kept, rest_given = fold(
+        [(out_kept, out_taken), (rest_kept, rest_taken)], flag(*x_step), rows
+    )
+    rest_given, feed_taken = hold((rest_given, feed_taken))
+    rest_taken = swapped(rest_given, *x_step)
+    feed_kept, feed_given = fold([(feed_kept, feed_taken)], flag(*z_steps[1]), rows)
+    feed_taken = swapped(feed_given, *z_steps[1])
     input_grad = jnp.concatenate(input_grad, axis=2)
-    proj_taken, rest_taken, out_taken, feed_taken, input_grad = hold(
-        (proj_taken, rest_taken, out_taken, feed_taken, input_grad)
-    )
-
     mixer_kept, mixer_given = fold(
-        [(proj_kept, proj_taken), (out_kept, out_taken), (rest_kept, rest_taken)],
-        flag(*z_steps[0]),
-        rows,
-    )
+        [(proj_kept, proj_taken), (rest_kept, rest_taken)], flag(*z_steps[0]), rows
+    )
+    feed_kept, mixer_given = hold((feed_kept, mixer_given))
     mixer_taken = swapped(mixer_given, *z_steps[0])
     feed_share = (feed_kept + feed_taken)[0]
     feed_shares = gathered(feed_share)
-    mixer_taken, *feed_shares = hold((mixer_taken, *feed_shares))
+    mixer_taken, input_grad, *feed_shares = hold((mixer_taken, input_grad, *feed_shares))
     mixer_kept, mixer_given = fold([(mixer_kept, mixer_taken)], flag(*z_steps[1]), rows)
     mixer_taken = swapped(mixer_given, *z_steps[1])
-    down_share, up_share = unpacked(
-        feed_shares, [(hidden_units // parts, features), (features // parts, hidden_units)]
-    )
-    mixer_taken, down_share, up_share = hold((mixer_taken, down_share, up_share))
+    (down_share,) = unpacked(feed_shares, [(hidden_units // parts, features)])
+    side = lax.all_gather(side, "dp", axis=0, tiled=True)
+    mixer_taken, down_share, up_share = hold((mixer_taken, down_share, side))
     mixer_share = (mixer_kept + mixer_taken)[0]
     proj_share, out_share, kernel_share, packed = unpacked(
         gathered(mixer_share),

time: 526 us -> 506 us (0.962)
  Pallas kernels: 217 us -> 199 us
  waiting for transfers between devices: 198 us -> 184 us
  between operations: 1.22 us -> 14.6 us
    pallas_call x0 -> x1, Pallas kernels: none -> 10.1 us  [whole_product(): pl.pallas_call(whole_product_kernel, grid=(right.shape[1] // rows,), in_s...]
    ppermute x32 -> x28, waiting for transfers between devices: 177 us -> 167 us  [swapped(): return lax.ppermute(array, axis, [(i, i ^ by) for i in range(count)])]
    pallas_call x4 -> x3, Pallas kernels: 29.4 us -> 22.2 us  [parted_product(): pl.pallas_call(parted_product_kernel, grid_spec=pltpu.PrefetchScalarGridS...]
    pallas_call x10 -> x8, Pallas kernels: 35.3 us -> 28.2 us  [fold(): pl.pallas_call(fold_kernel, grid=(count // 2,), in_specs=[pl.BlockSpec(me...]
    all_to_all x5 -> x4, waiting for transfers between devices: 7.14 us -> 0.01 us  [sent(): return lax.all_to_all(columns, 'seq', 0, 0, tiled=True)]
    pallas_call x4 -> x3, Pallas kernels: 24 us -> 17.6 us  [half_product(): pl.pallas_call(product_kernel, grid_spec=pltpu.PrefetchScalarGridSpec(num...]
    all_to_all x5 -> x4, starting transfers between devices: 24.4 us -> 20.2 us  [sent(): return lax.all_to_all(columns, 'seq', 0, 0, tiled=True)]
    unnamed x92 -> x85, local copies, waits for them, and re-layouts: 9.71 us -> 11.9 us
  transfers between devices with their start and end apart: 39 -> 36, of which waited for: 19 -> 15; matrix products, arithmetic and copies ran while one was open for 6% -> 6% of each run, Pallas kernels for 38% -> 37%
where the time goes in v3:
time: 506 us; the launch traced here: 504 us
  Pallas kernels  199 us (39%)
  waiting for transfers between devices  184 us (36%)
  starting transfers between devices  58.5 us (12%)
  local copies, waits for them, and re-layouts  24.8 us (5%)
  other arithmetic  23 us (5%)
  between operations  14.6 us (3%)
    ppermute x28, waiting for transfers between devices, swapped(): return lax.ppermute(array, axis, [(i, i ^ by) for i in range(count)])  167 us
    pallas_call x4, Pallas kernels, by_rows(): pl.pallas_call(kernel, grid=(rows // height,), in_specs=[spec(array.shape...  65.9 us
    pallas_call x1, Pallas kernels, backward_convolution(): pl.pallas_call(backward_kernel, grid=(features // lanes,), in_specs=start...  32.9 us
    pallas_call x8, Pallas kernels, fold(): pl.pallas_call(fold_kernel, grid=(count // 2,), in_specs=[pl.BlockSpec(me...  28.2 us
    ppermute x28, starting transfers between devices, swapped(): return lax.ppermute(array, axis, [(i, i ^ by) for i in range(count)])  27.4 us
    pallas_call x3, Pallas kernels, parted_product(): pl.pallas_call(parted_product_kernel, grid_spec=pltpu.PrefetchScalarGridS...  22.2 us
    all_to_all x4, starting transfers between devices, sent(): return lax.all_to_all(columns, 'seq', 0, 0, tiled=True)  20.2 us
    pallas_call x3, Pallas kernels, half_product(): pl.pallas_call(product_kernel, grid_spec=pltpu.PrefetchScalarGridSpec(num...  17.6 us
  transfers between devices with their start and end apart: 36, of which 15 were waited for; matrix products, arithmetic and copies ran while one was open for 6% of the time, Pallas kernels for 37%

profile of v3, /device:TPU:0, one launch (start us, length us, event | category | flops | bytes accessed | tf_op | source)
XLA Modules:
  0.0 504.4 jit_solution(5707255191742306091)
XLA Ops:
  20.6 5.8 %all-to-all-start = ((f32[8,128,768]{2,1,0:T(8,128)}), f32[8,128,768]{2,1,0:T(8,128)S(1)}, u32[]{:S(2)}, u32[]{:S(2)}) async-start(f32[8,128,768]{2,1,0:T(8,128)} %convert_element_type.8), calls=%async_computation | async-start | bytes 6291456 | tf_op jit(solution)/shard_map/all_to_all | solution.py:1077
  28.4 33.2 %collective-permute-done.3 = f32[4,1,192,128]{3,2,0,1:T(8,128)} collective-permute-done((f32[4,1,192,128]{3,2,0,1:T(8,128)S(1)}, f32[4,1,192,128]{3,2,0,1:T(8,128)}, u32[]{:S(2)}, u32[]{:S(2)}) %collective-permute-start.3) | collective-permute-done | bytes 393248 | tf_op jit(solution)/shard_map/ppermute | solution.py:1004
  65.1 17.4 %collective-permute-done.4 = f32[8,192,128]{2,1,0:T(8,128)} collective-permute-done((f32[8,192,128]{2,1,0:T(8,128)}, f32[8,192,128]{2,1,0:T(8,128)}, u32[]{:S(2)}, u32[]{:S(2)}) %collective-permute-start.4) | collective-permute-done | bytes 786464 | tf_op jit(solution)/shard_map/ppermute | solution.py:1004
  108.5 9.4 %project.1 = (bf16[1024,768]{1,0:T(8,128)(2,1)}, f32[1024,2304]{1,0:T(8,128)}) custom-call(f32[1024,768]{1,0:T(8,128)} %bitcast.47, f32[1,768]{1,0:T(1,128)} %broadcast_in_dim.34.gain_ref, f32[1,768]{1,0:T(1,128)} %broadcast_in_dim.35.bias_ref, bf16[768,2304]{1,0:T(8,128)(2,1)} %weight_ref.3, f32[1,2304]{1,0:T(1,128)} %broadcast_in_dim.36.offset_ref), custom_call_target="tpu_custom_call" | custom-call | tf_op jit(solution)/shard_map/project/pallas_call | solution.py:802
  118.0 17.4 %forward_convolution.1 = (f32[1024,768]{1,0:T(8,128)}, bf16[1024,768]{1,0:T(8,128)(2,1)}) custom-call(s32[2]{0:T(128)} %pad_add_fusion.start_ref, f32[1024,2304]{1,0:T(8,128)} %get-tuple-element.131.outer_ref.inner_ref.value_ref, f32[1024,2304]{1,0:T(8,128)} %get-tuple-element.131.outer_ref.inner_ref.value_ref, ...), custom_call_target="tpu_custom_call" | custom-call | tf_op jit(solution)/shard_map/forward_convolution/pallas_call | solution.py:602
  135.3 23.9 %feed.1 = (f32[1024,768]{1,0:T(8,128)}, bf16[1024,768]{1,0:T(8,128)(2,1)}, bf16[1024,3072]{1,0:T(8,128)(2,1)}, f32[1024,3072]{1,0:T(8,128)}, f32[1024,256]{1,0:T(8,128)}, /*index=5*/f32[1024,512]{1,0:T(8,128)}) custom-call(f32[1024,768]{1,0:T(8,128)} %bitcast.48, bf16[1024,768]{1,0:T(8,128)(2,1)} %get-tuple-element.134.branch_ref.left_ref, ...), custom_call_target="tpu_custom_call" | custom-call | tf_op jit(solution)/shard_map/feed/pallas_call | solution.py:802
  159.3 15.9 %all-to-all-done.1 = f32[8,128,768]{2,1,0:T(8,128)S(1)} async-done(((f32[8,128,768]{2,1,0:T(8,128)}), f32[8,128,768]{2,1,0:T(8,128)S(1)}, u32[]{:S(2)}, u32[]{:S(2)}) %all-to-all-start.1) | async-done | bytes 3145760 | tf_op jit(solution)/shard_map/all_to_all | solution.py:1086
  176.8 7.9 %half_product.3 = f32[3072,384]{1,0:T(8,128)} custom-call(s32[1]{0:T(128)} %sub.35.half_ref, bf16[1024,3072]{1,0:T(8,128)(2,1)} %get-tuple-element.138.left_ref, f32[1024,768]{1,0:T(8,128)} %bitcast.44), custom_call_target="tpu_custom_call" | custom-call | tf_op jit(solution)/shard_map/half_product/pallas_call | solution.py:840
  188.6 22.1 %feed_back.1 = (bf16[1024,3072]{1,0:T(8,128)(2,1)}, f32[1024,768]{1,0:T(8,128)}, bf16[1024,768]{1,0:T(8,128)(2,1)}, f32[1024,768]{1,0:T(8,128)}, f32[4,768]{1,0:T(4,128)}, /*index=5*/f32[1,3072]{1,0:T(1,128)}) custom-call(f32[1024,768]{1,0:T(8,128)} %bitcast.45, f32[1024,768]{1,0:T(8,128)} %get-tuple-element.140.residual_ref, ...), custom_call_target="tpu_custom_call" | custom-call | tf_op jit(solution)/shard_map/feed_back/pallas_call | solution.py:802
  210.7 10.1 %whole_product.1 = f32[768,3072]{1,0:T(8,128)} custom-call(bf16[1024,768]{1,0:T(8,128)(2,1)} %get-tuple-element.146.left_ref, bf16[1024,3072]{1,0:T(8,128)(2,1)} %get-tuple-element.147.right_ref), custom_call_target="tpu_custom_call" | custom-call | tf_op jit(solution)/shard_map/whole_product/pallas_call | solution.py:861
  227.2 10.0 %parted_product.3 = (f32[8,192,384]{2,1,0:T(8,128)}, f32[8,192,384]{2,1,0:T(8,128)}) custom-call(s32[2]{0:T(128)} %pad_add_fusion.1.bits_ref, bf16[1024,3072]{1,0:T(8,128)(2,1)} %get-tuple-element.138.left_ref, f32[1024,768]{1,0:T(8,128)} %bitcast.46, f32[3072,384]{1,0:T(8,128)} %collective-permute-done.6.taken_ref), custom_call_target="tpu_custom_call" | custom-call | tf_op jit(solution)/shard_map/parted_product/pallas_call | solution.py:901
  238.8 32.9 %backward_convolution.1 = (bf16[3,1024,768]{2,1,0:T(8,128)(2,1)}, f32[768,512]{1,0:T(8,128)}, f32[768,512]{1,0:T(8,128)}, f32[16,768]{1,0:T(8,128)}) custom-call(s32[2]{0:T(128)} %pad_add_fusion.start_ref, f32[1024,768]{1,0:T(8,128)} %get-tuple-element.153.grad_ref, f32[1024,768]{1,0:T(8,128)} %get-tuple-element.154.convolved_ref, ...), custom_call_target="tpu_custom_call" | custom-call | tf_op jit(solution)/shard_map/backward_convolution/pallas_call | solution.py:622
  271.7 10.4 %input_grad.1 = (f32[1024,512]{1,0:T(8,128)}, f32[1024,256]{1,0:T(8,128)}, f32[2,768]{1,0:T(2,128)}) custom-call(bf16[3,1024,768]{2,1,0:T(8,128)(2,1)} %get-tuple-element.171.mixed_ref.right_ref, bf16[768,2304]{1,0:T(8,128)(2,1)} %weight_ref.3, f32[1024,768]{1,0:T(8,128)} %bitcast.49, f32[1,768]{1,0:T(1,128)} %broadcast_in_dim.34.gain_ref, ...), custom_call_target="tpu_custom_call" | custom-call | tf_op jit(solution)/shard_map/input_grad/pallas_call | solution.py:802
  282.1 6.0 %half_product.4 = f32[768,1152]{1,0:T(8,128)} custom-call(s32[1]{0:T(128)} %sub.35.half_ref, bf16[1024,768]{1,0:T(8,128)(2,1)} %get-tuple-element.159.left_ref, bf16[3,1024,768]{2,1,0:T(8,128)(2,1)} %get-tuple-element.171.mixed_ref.right_ref), custom_call_target="tpu_custom_call" | custom-call | tf_op jit(solution)/shard_map/half_product/pallas_call | solution.py:840
  288.1 10.8 %collective-permute-done.7.refs_1_ = f32[8,192,384]{2,1,0:T(8,128)} collective-permute-done((f32[8,192,384]{2,1,0:T(8,128)}, f32[8,192,384]{2,1,0:T(8,128)}, u32[]{:S(2)}, u32[]{:S(2)}) %collective-permute-start.7) | collective-permute-done | bytes 2359328 | tf_op jit(solution)/shard_map/ppermute | solution.py:1004
  305.9 7.4 %parted_product.4 = (f32[8,48,1152]{2,1,0:T(8,128)}, f32[8,48,1152]{2,1,0:T(8,128)}) custom-call(s32[2]{0:T(128)} %pad_add_fusion.1.bits_ref, bf16[1024,768]{1,0:T(8,128)(2,1)} %get-tuple-element.159.left_ref, bf16[3,1024,768]{2,1,0:T(8,128)(2,1)} %get-tuple-element.171.mixed_ref.right_ref, f32[768,1152]{1,0:T(8,128)} %collective-permute-done.9.taken_ref), custom_call_target="tpu_custom_call" | custom-call | tf_op jit(solution)/shard_map/parted_product/pallas_call | solution.py:901
  332.2 6.0 %fold.9 = (f32[8,48,640]{2,1,0:T(8,128)}, f32[8,48,640]{2,1,0:T(8,128)}) custom-call(s32[1]{0:T(128)} %bitcast.13.bit_ref, f32[16,48,512]{2,1,0:T(8,128)} %bitcast.55, f32[16,48,512]{2,1,0:T(8,128)} %bitcast.19.refs_1_, f32[16,48,128]{2,1,0:T(8,128)} %bitcast.53, f32[16,48,128]{2,1,0:T(8,128)} %bitcast.58), custom_call_target="tpu_custom_call" | custom-call | tf_op jit(solution)/shard_map/fold/pallas_call | solution.py:945
  342.8 22.4 %collective-permute-done.8.refs_1_ = f32[4,192,384]{2,1,0:T(8,128)} collective-permute-done((f32[4,192,384]{2,1,0:T(8,128)}, f32[4,192,384]{2,1,0:T(8,128)}, u32[]{:S(2)}, u32[]{:S(2)}) %collective-permute-start.8) | collective-permute-done | bytes 1179680 | tf_op jit(solution)/shard_map/ppermute | solution.py:1004
  382.3 26.2 %collective-permute-done.17.refs_1_ = f32[2,48,1536]{2,1,0:T(8,128)S(1)} collective-permute-done((f32[2,48,1536]{2,1,0:T(8,128)}, f32[2,48,1536]{2,1,0:T(8,128)S(1)}, u32[]{:S(2)}, u32[]{:S(2)}) %collective-permute-start.17) | collective-permute-done | bytes 589856 | tf_op jit(solution)/shard_map/ppermute | solution.py:1004
  418.8 13.1 %collective-permute-done.18.refs_3_ = f32[4,48,1024]{2,1,0:T(8,128)} collective-permute-done((f32[4,48,1024]{2,1,0:T(8,128)}, f32[4,48,1024]{2,1,0:T(8,128)}, u32[]{:S(2)}, u32[]{:S(2)}) %collective-permute-start.18) | collective-permute-done | bytes 786464 | tf_op jit(solution)/shard_map/ppermute | solution.py:1004
  437.7 6.1 %collective-permute-done.21.y_ref = f32[48,1536]{1,0:T(8,128)S(1)} collective-permute-done((f32[48,1536]{1,0:T(8,128)S(1)}, f32[48,1536]{1,0:T(8,128)S(1)}, u32[]{:S(2)}, u32[]{:S(2)}) %collective-permute-start.21) | collective-permute-done | bytes 294944 | tf_op jit(solution)/shard_map/ppermute | solution.py:1004
  445.9 7.4 %collective-permute-done.19.refs_1_ = f32[2,48,2176]{2,1,0:T(8,128)S(1)} collective-permute-done((f32[2,48,2176]{2,1,0:T(8,128)}, f32[2,48,2176]{2,1,0:T(8,128)S(1)}, u32[]{:S(2)}, u32[]{:S(2)}) %collective-permute-start.19) | collective-permute-done | bytes 835616 | tf_op jit(solution)/shard_map/ppermute | solution.py:1004
  459.9 14.9 %collective-permute-done.24 = f32[1,48,2176]{2,1,0:T(8,128)S(1)} collective-permute-done((f32[1,48,2176]{2,1,0:T(8,128)}, f32[1,48,2176]{2,1,0:T(8,128)S(1)}, u32[]{:S(2)}, u32[]{:S(2)}) %collective-permute-start.24) | collective-permute-done | bytes 417824 | tf_op jit(solution)/shard_map/ppermute | solution.py:1004
  476.0 10.5 %collective-permute-done.25.y_ref = f32[48,2176]{1,0:T(8,128)S(1)} collective-permute-done((f32[48,2176]{1,0:T(8,128)S(1)}, f32[48,2176]{1,0:T(8,128)S(1)}, u32[]{:S(2)}, u32[]{:S(2)}) %collective-permute-start.25) | collective-permute-done | bytes 417824 | tf_op jit(solution)/shard_map/ppermute | solution.py:1004
  (216 shorter events, 142.5 us)
Async XLA Ops:
  20.6 76.7 %all-to-all-start = ((f32[8,128,768]{2,1,0:T(8,128)}), f32[8,128,768]{2,1,0:T(8,128)S(1)}, u32[]{:S(2)}, u32[]{:S(2)}) async-start(f32[8,128,768]{2,1,0:T(8,128)} %convert_element_type.8), calls=%async_computation | async-start | bytes 6291456 | tf_op jit(solution)/shard_map/all_to_all | solution.py:1077
  26.4 35.2 %collective-permute-start.3 = (f32[4,1,192,128]{3,2,0,1:T(8,128)S(1)}, f32[4,1,192,128]{3,2,0,1:T(8,128)}, u32[]{:S(2)}, u32[]{:S(2)}) collective-permute-start(f32[4,1,192,128]{3,2,0,1:T(8,128)S(1)} %bitcast.54), channel_id=1, source_target_pairs={{0,1},{1,0},{2,3},{3,2},{4,5},{5,4},{6,7},{7,6},{8,9},{9,8},{10,11... | collective-permute-start | bytes 1179656 | tf_op jit(solution)/shard_map/ppermute | solution.py:1004
  63.6 18.9 %collective-permute-start.4 = (f32[8,192,128]{2,1,0:T(8,128)}, f32[8,192,128]{2,1,0:T(8,128)}, u32[]{:S(2)}, u32[]{:S(2)}) collective-permute-start(f32[8,192,128]{2,1,0:T(8,128)} %bitcast.5), channel_id=1, source_target_pairs={{0,16},{8,24},{16,0},{24,8},{1,17},{9,25},{17,1},{25,9},{2,18},{10... | collective-permute-start | bytes 2359304 | tf_op jit(solution)/shard_map/ppermute | solution.py:1004
  98.9 76.2 %all-to-all-start.1 = ((f32[8,128,768]{2,1,0:T(8,128)}), f32[8,128,768]{2,1,0:T(8,128)S(1)}, u32[]{:S(2)}, u32[]{:S(2)}) async-start(f32[8,128,768]{2,1,0:T(8,128)} %convert_element_type.9), calls=%async_computation.1 | async-start | bytes 6291456 | tf_op jit(solution)/shard_map/all_to_all | solution.py:1086
  184.7 36.2 %collective-permute-start.6 = (f32[3072,384]{1,0:T(8,128)}, f32[3072,384]{1,0:T(8,128)}, u32[]{:S(2)}, u32[]{:S(2)}) collective-permute-start(f32[3072,384]{1,0:T(8,128)} %half_product.3), channel_id=1, source_target_pairs={{0,8},{8,0},{16,24},{24,16},{1,9},{9,1},{17,25},{25,17},{2,10},{10... | collective-permute-start | bytes 14155784 | tf_op jit(solution)/shard_map/ppermute | solution.py:1004
  184.7 36.2 %all-to-all-start.2 = ((f32[8,128,256]{2,1,0:T(8,128)}), f32[8,128,256]{2,1,0:T(8,128)S(1)}, u32[]{:S(2)}, u32[]{:S(2)}) async-start(f32[8,128,256]{2,1,0:T(8,128)} %bitcast.57), calls=%async_computation.2 | async-start | bytes 2097152 | tf_op jit(solution)/shard_map/all_to_all | solution.py:1131
  188.4 230.4 %reduce-scatter.2.cloned.1.call-start = ((), (), s32[]{:S(2)}) async-start(), calls=%async_computation.7 | async-start | bytes 9732096 | tf_op jit(solution)/shard_map/reduce_scatter | solution.py:1163
  220.9 78.0 %all-to-all-start.3 = ((f32[8,128,512]{2,1,0:T(8,128)}), f32[8,128,512]{2,1,0:T(8,128)S(1)}, u32[]{:S(2)}, u32[]{:S(2)}) async-start(f32[8,128,512]{2,1,0:T(8,128)} %bitcast.52), calls=%async_computation.3 | async-start | bytes 4194304 | tf_op jit(solution)/shard_map/all_to_all | solution.py:1131
  237.3 61.6 %collective-permute-start.7 = (f32[8,192,384]{2,1,0:T(8,128)}, f32[8,192,384]{2,1,0:T(8,128)}, u32[]{:S(2)}, u32[]{:S(2)}) collective-permute-start(f32[8,192,384]{2,1,0:T(8,128)} %get-tuple-element.161), channel_id=1, source_target_pairs={{0,16},{8,24},{16,0},{24,8},{1,17},{9,25},{17,1},{25,9},{2,18},{10... | collective-permute-start | bytes 7077896 | tf_op jit(solution)/shard_map/ppermute | solution.py:1004
  300.2 65.0 %all-to-all-start.4 = ((f32[8,128,512]{2,1,0:T(8,128)}), f32[8,128,512]{2,1,0:T(8,128)S(1)}, u32[]{:S(2)}, u32[]{:S(2)}) async-start(f32[8,128,512]{2,1,0:T(8,128)} %bitcast.51), calls=%async_computation.4 | async-start | bytes 4194304 | tf_op jit(solution)/shard_map/all_to_all | solution.py:1131
  313.4 51.8 %collective-permute-start.10 = (f32[8,48,1152]{2,1,0:T(8,128)}, f32[8,48,1152]{2,1,0:T(8,128)}, u32[]{:S(2)}, u32[]{:S(2)}) collective-permute-start(f32[8,48,1152]{2,1,0:T(8,128)} %get-tuple-element.175), channel_id=1, source_target_pairs={{0,16},{8,24},{16,0},{24,8},{1,17},{9,25},{17,1},{25,9},{2,18},{10... | collective-permute-start | bytes 5308424 | tf_op jit(solution)/shard_map/ppermute | solution.py:1004
  315.0 16.5 %collective-permute-start.11 = (f32[768,512]{1,0:T(8,128)}, f32[768,512]{1,0:T(8,128)}, u32[]{:S(2)}, u32[]{:S(2)}) collective-permute-start(f32[768,512]{1,0:T(8,128)} %get-tuple-element.177), channel_id=1, source_target_pairs={{0,8},{8,0},{16,24},{24,16},{1,9},{9,1},{17,25},{25,17},{2,10},{10... | collective-permute-start | bytes 4718600 | tf_op jit(solution)/shard_map/ppermute | solution.py:1004
  323.0 15.2 %collective-permute-start.13 = (f32[768,384]{1,0:T(8,128)}, f32[768,384]{1,0:T(8,128)}, u32[]{:S(2)}, u32[]{:S(2)}) collective-permute-start(f32[768,384]{1,0:T(8,128)} %half_product.5), channel_id=1, source_target_pairs={{0,8},{8,0},{16,24},{24,16},{1,9},{9,1},{17,25},{25,17},{2,10},{10... | collective-permute-start | bytes 3538952 | tf_op jit(solution)/shard_map/ppermute | solution.py:1004
  323.5 41.7 %collective-permute-start.8 = (f32[4,192,384]{2,1,0:T(8,128)}, f32[4,192,384]{2,1,0:T(8,128)}, u32[]{:S(2)}, u32[]{:S(2)}) collective-permute-start(f32[4,192,384]{2,1,0:T(8,128)} %get-tuple-element.170), channel_id=1, source_target_pairs={{0,1},{1,0},{2,3},{3,2},{4,5},{5,4},{6,7},{7,6},{8,9},{9,8},{10,11... | collective-permute-start | bytes 3538952 | tf_op jit(solution)/shard_map/ppermute | solution.py:1004
  365.2 44.4 %all-to-all-start.5 = ((f32[8,128,256]{2,1,0:T(8,128)}), f32[8,128,256]{2,1,0:T(8,128)S(1)}, u32[]{:S(2)}, u32[]{:S(2)}) async-start(f32[8,128,256]{2,1,0:T(8,128)} %bitcast.56), calls=%async_computation.5 | async-start | bytes 2097152 | tf_op jit(solution)/shard_map/all_to_all | solution.py:1131
  370.3 104.5 %all-gather.2.cloned.1.call-start = ((), (), s32[]{:S(2)}) async-start(), calls=%async_computation.8 | async-start | bytes 1474560 | tf_op jit(solution)/shard_map/all_gather | solution.py:1267
  370.3 39.2 %collective-permute-start.15 = (f32[8,48,640]{2,1,0:T(8,128)}, f32[8,48,640]{2,1,0:T(8,128)}, u32[]{:S(2)}, u32[]{:S(2)}) collective-permute-start(f32[8,48,640]{2,1,0:T(8,128)} %get-tuple-element.197), channel_id=1, source_target_pairs={{0,16},{8,24},{16,0},{24,8},{1,17},{9,25},{17,1},{25,9},{2,18},{10... | collective-permute-start | bytes 2949128 | tf_op jit(solution)/shard_map/ppermute | solution.py:1004
  375.0 33.6 %collective-permute-start.14 = (f32[4,48,1152]{2,1,0:T(8,128)}, f32[4,48,1152]{2,1,0:T(8,128)}, u32[]{:S(2)}, u32[]{:S(2)}) collective-permute-start(f32[4,48,1152]{2,1,0:T(8,128)} %get-tuple-element.196), channel_id=1, source_target_pairs={{0,1},{1,0},{2,3},{3,2},{4,5},{5,4},{6,7},{7,6},{8,9},{9,8},{10,11... | collective-permute-start | bytes 2654216 | tf_op jit(solution)/shard_map/ppermute | solution.py:1004
  379.4 29.1 %collective-permute-start.17 = (f32[2,48,1536]{2,1,0:T(8,128)}, f32[2,48,1536]{2,1,0:T(8,128)S(1)}, u32[]{:S(2)}, u32[]{:S(2)}) collective-permute-start(f32[2,48,1536]{2,1,0:T(8,128)} %get-tuple-element.199), channel_id=1, source_target_pairs={{0,2},{1,3},{2,0},{3,1},{4,6},{5,7},{6,4},{7,5},{8,10},{9,11},{10,... | collective-permute-start | bytes 1769480 | tf_op jit(solution)/shard_map/ppermute | solution.py:1004
  380.9 27.7 %collective-permute-start.16 = (f32[8,48,384]{2,1,0:T(8,128)S(1)}, f32[8,48,384]{2,1,0:T(8,128)S(1)}, u32[]{:S(2)}, u32[]{:S(2)}) collective-permute-start(f32[8,48,384]{2,1,0:T(8,128)S(1)} %copy-done.39), channel_id=1, source_target_pairs={{0,16},{8,24},{16,0},{24,8},{1,17},{9,25},{17,1},{25,9},{2,18},{10... | collective-permute-start | bytes 1769480 | tf_op jit(solution)/shard_map/ppermute | solution.py:1004
  413.5 18.4 %collective-permute-start.18 = (f32[4,48,1024]{2,1,0:T(8,128)}, f32[4,48,1024]{2,1,0:T(8,128)}, u32[]{:S(2)}, u32[]{:S(2)}) collective-permute-start(f32[4,48,1024]{2,1,0:T(8,128)} %get-tuple-element.210), channel_id=1, source_target_pairs={{0,1},{1,0},{2,3},{3,2},{4,5},{5,4},{6,7},{7,6},{8,9},{9,8},{10,11... | collective-permute-start | bytes 2359304 | tf_op jit(solution)/shard_map/ppermute | solution.py:1004
  416.4 19.7 %collective-permute-start.20 = (f32[1,48,1536]{2,1,0:T(8,128)}, f32[1,48,1536]{2,1,0:T(8,128)}, u32[]{:S(2)}, u32[]{:S(2)}) collective-permute-start(f32[1,48,1536]{2,1,0:T(8,128)} %get-tuple-element.216), channel_id=1, source_target_pairs={{0,4},{1,5},{2,6},{3,7},{4,0},{5,1},{6,2},{7,3},{8,12},{9,13},{10,... | collective-permute-start | bytes 884744 | tf_op jit(solution)/shard_map/ppermute | solution.py:1004
  434.8 18.4 %collective-permute-start.19 = (f32[2,48,2176]{2,1,0:T(8,128)}, f32[2,48,2176]{2,1,0:T(8,128)S(1)}, u32[]{:S(2)}, u32[]{:S(2)}) collective-permute-start(f32[2,48,2176]{2,1,0:T(8,128)} %get-tuple-element.212), channel_id=1, source_target_pairs={{0,2},{1,3},{2,0},{3,1},{4,6},{5,7},{6,4},{7,5},{8,10},{9,11},{10,... | collective-permute-start | bytes 2506760 | tf_op jit(solution)/shard_map/ppermute | solution.py:1004
  456.5 18.3 %collective-permute-start.24 = (f32[1,48,2176]{2,1,0:T(8,128)}, f32[1,48,2176]{2,1,0:T(8,128)S(1)}, u32[]{:S(2)}, u32[]{:S(2)}) collective-permute-start(f32[1,48,2176]{2,1,0:T(8,128)} %get-tuple-element.221), channel_id=1, source_target_pairs={{0,4},{1,5},{2,6},{3,7},{4,0},{5,1},{6,2},{7,3},{8,12},{9,13},{10,... | collective-permute-start | bytes 1253384 | tf_op jit(solution)/shard_map/ppermute | solution.py:1004
  (53 other events, 361.1 us)
Sparse Core Ops, SparseCore 0:
  221.0 176.1 reduce-scatter.1
  418.9 15.5 all-gather.1

commit v4 on v3

--- a/solution.py
+++ b/solution.py
@@ -568,10 +568,8 @@
     sums_ref[...] = jnp.concatenate(rows, axis=0)
 
 
-def kernel_parameters():
-    return pltpu.CompilerParams(
-        vmem_limit_bytes=56 * 1024 * 1024
-    )
+def kernel_parameters(mebibytes=56):
+    return pltpu.CompilerParams(vmem_limit_bytes=mebibytes * 1024 * 1024)
 
 
 def kernel_specs(tokens, parts, width, lanes, features):
@@ -948,7 +946,7 @@
         in_specs=[pl.BlockSpec(memory_space=pltpu.SMEM)] + specs,
         out_specs=(one, one),
         out_shape=(shape, shape),
-        compiler_params=kernel_parameters(),
+        compiler_params=kernel_parameters(24),
         cost_estimate=NO_COST,
         name="fold",
     )(which, *operands)
@@ -993,7 +991,7 @@
         in_specs=[pl.BlockSpec(memory_space=pltpu.SMEM)] + [pl.BlockSpec(memory_space=pltpu.VMEM)] * 4,
         out_specs=[pl.BlockSpec(memory_space=pltpu.VMEM)] * len(shapes),
         out_shape=[jax.ShapeDtypeStruct(shape, jnp.float32) for shape in shapes],
-        compiler_params=kernel_parameters(),
+        compiler_params=kernel_parameters(24),
         cost_estimate=NO_COST,
         name="unpack",
     )(jnp.concatenate([flag("dp", 1), flag("dp", 2)]), *shares)

time: 506 us -> 500 us (0.988)
  Pallas kernels: 199 us -> 185 us
    pallas_call x8, Pallas kernels: 28.2 us -> 15.2 us  [fold(): pl.pallas_call(fold_kernel, grid=(count // 2,), in_specs=[pl.BlockSpec(me...]
    unnamed x85 -> x97, local copies, waits for them, and re-layouts: 11.9 us -> 19.3 us
  transfers between devices with their start and end apart: 36 -> 36, of which waited for: 15 -> 17; matrix products, arithmetic and copies ran while one was open for 6% -> 7% of each run, Pallas kernels for 37% -> 35%
where the time goes in v4:
time: 500 us; the launch traced here: 499 us
  Pallas kernels  185 us (37%)
  waiting for transfers between devices  183 us (37%)
  starting transfers between devices  61 us (12%)
  local copies, waits for them, and re-layouts  29.2 us (6%)
  other arithmetic  26.4 us (5%)
  between operations  14.6 us (3%)
    ppermute x28, waiting for transfers between devices, swapped(): return lax.ppermute(array, axis, [(i, i ^ by) for i in range(count)])  165 us
    pallas_call x4, Pallas kernels, by_rows(): pl.pallas_call(kernel, grid=(rows // height,), in_specs=[spec(array.shape...  66.4 us
    pallas_call x1, Pallas kernels, backward_convolution(): pl.pallas_call(backward_kernel, grid=(features // lanes,), in_specs=start...  32.9 us
    ppermute x28, starting transfers between devices, swapped(): return lax.ppermute(array, axis, [(i, i ^ by) for i in range(count)])  29.8 us
    pallas_call x3, Pallas kernels, parted_product(): pl.pallas_call(parted_product_kernel, grid_spec=pltpu.PrefetchScalarGridS...  22.2 us
    all_to_all x4, starting transfers between devices, sent(): return lax.all_to_all(columns, 'seq', 0, 0, tiled=True)  20.3 us
    unnamed x97, local copies, waits for them, and re-layouts  19.3 us
    pallas_call x3, Pallas kernels, half_product(): pl.pallas_call(product_kernel, grid_spec=pltpu.PrefetchScalarGridSpec(num...  17.5 us
  transfers between devices with their start and end apart: 36, of which 17 were waited for; matrix products, arithmetic and copies ran while one was open for 7% of the time, Pallas kernels for 35%

profile of v4, /device:TPU:0, one launch (start us, length us, event | category | flops | bytes accessed | tf_op | source)
XLA Modules:
  0.0 498.9 jit_solution(9061580825106295654)
XLA Ops:
  20.6 5.8 %all-to-all-start = ((f32[8,128,768]{2,1,0:T(8,128)}), f32[8,128,768]{2,1,0:T(8,128)S(1)}, u32[]{:S(2)}, u32[]{:S(2)}) async-start(f32[8,128,768]{2,1,0:T(8,128)} %convert_element_type.8), calls=%async_computation | async-start | bytes 6291456 | tf_op jit(solution)/shard_map/all_to_all | solution.py:1075
  28.4 33.2 %collective-permute-done.3 = f32[4,1,192,128]{3,2,0,1:T(8,128)} collective-permute-done((f32[4,1,192,128]{3,2,0,1:T(8,128)S(1)}, f32[4,1,192,128]{3,2,0,1:T(8,128)}, u32[]{:S(2)}, u32[]{:S(2)}) %collective-permute-start.3) | collective-permute-done | bytes 393248 | tf_op jit(solution)/shard_map/ppermute | solution.py:1002
  65.1 17.4 %collective-permute-done.4 = f32[8,192,128]{2,1,0:T(8,128)} collective-permute-done((f32[8,192,128]{2,1,0:T(8,128)}, f32[8,192,128]{2,1,0:T(8,128)}, u32[]{:S(2)}, u32[]{:S(2)}) %collective-permute-start.4) | collective-permute-done | bytes 786464 | tf_op jit(solution)/shard_map/ppermute | solution.py:1002
  108.5 9.5 %project.1 = (bf16[1024,768]{1,0:T(8,128)(2,1)}, f32[1024,2304]{1,0:T(8,128)}) custom-call(f32[1024,768]{1,0:T(8,128)} %bitcast.53, f32[1,768]{1,0:T(1,128)} %broadcast_in_dim.34.gain_ref, f32[1,768]{1,0:T(1,128)} %broadcast_in_dim.35.bias_ref, bf16[768,2304]{1,0:T(8,128)(2,1)} %weight_ref.3, f32[1,2304]{1,0:T(1,128)} %broadcast_in_dim.36.offset_ref), custom_call_target="tpu_custom_call" | custom-call | tf_op jit(solution)/shard_map/project/pallas_call | solution.py:800
  118.0 17.4 %forward_convolution.1 = (f32[1024,768]{1,0:T(8,128)}, bf16[1024,768]{1,0:T(8,128)(2,1)}) custom-call(s32[2]{0:T(128)} %pad_add_fusion.start_ref, f32[1024,2304]{1,0:T(8,128)} %get-tuple-element.131.outer_ref.inner_ref.value_ref, f32[1024,2304]{1,0:T(8,128)} %get-tuple-element.131.outer_ref.inner_ref.value_ref, ...), custom_call_target="tpu_custom_call" | custom-call | tf_op jit(solution)/shard_map/forward_convolution/pallas_call | solution.py:600
  135.3 23.9 %feed.1 = (f32[1024,768]{1,0:T(8,128)}, bf16[1024,768]{1,0:T(8,128)(2,1)}, bf16[1024,3072]{1,0:T(8,128)(2,1)}, f32[1024,3072]{1,0:T(8,128)}, f32[1024,256]{1,0:T(8,128)}, /*index=5*/f32[1024,512]{1,0:T(8,128)}) custom-call(f32[1024,768]{1,0:T(8,128)} %bitcast.54, bf16[1024,768]{1,0:T(8,128)(2,1)} %get-tuple-element.134.branch_ref.left_ref, ...), custom_call_target="tpu_custom_call" | custom-call | tf_op jit(solution)/shard_map/feed/pallas_call | solution.py:800
  159.3 15.9 %all-to-all-done.1 = f32[8,128,768]{2,1,0:T(8,128)S(1)} async-done(((f32[8,128,768]{2,1,0:T(8,128)}), f32[8,128,768]{2,1,0:T(8,128)S(1)}, u32[]{:S(2)}, u32[]{:S(2)}) %all-to-all-start.1) | async-done | bytes 3145760 | tf_op jit(solution)/shard_map/all_to_all | solution.py:1084
  176.7 7.9 %half_product.3 = f32[3072,384]{1,0:T(8,128)} custom-call(s32[1]{0:T(128)} %sub.35.half_ref, bf16[1024,3072]{1,0:T(8,128)(2,1)} %get-tuple-element.138.left_ref, f32[1024,768]{1,0:T(8,128)} %bitcast.50), custom_call_target="tpu_custom_call" | custom-call | tf_op jit(solution)/shard_map/half_product/pallas_call | solution.py:838
  188.5 22.1 %feed_back.1 = (bf16[1024,3072]{1,0:T(8,128)(2,1)}, f32[1024,768]{1,0:T(8,128)}, bf16[1024,768]{1,0:T(8,128)(2,1)}, f32[1024,768]{1,0:T(8,128)}, f32[4,768]{1,0:T(4,128)}, /*index=5*/f32[1,3072]{1,0:T(1,128)}) custom-call(f32[1024,768]{1,0:T(8,128)} %bitcast.51, f32[1024,768]{1,0:T(8,128)} %get-tuple-element.140.residual_ref, ...), custom_call_target="tpu_custom_call" | custom-call | tf_op jit(solution)/shard_map/feed_back/pallas_call | solution.py:800
  210.6 10.1 %whole_product.1 = f32[768,3072]{1,0:T(8,128)} custom-call(bf16[1024,768]{1,0:T(8,128)(2,1)} %get-tuple-element.146.left_ref, bf16[1024,3072]{1,0:T(8,128)(2,1)} %get-tuple-element.147.right_ref), custom_call_target="tpu_custom_call" | custom-call | tf_op jit(solution)/shard_map/whole_product/pallas_call | solution.py:859
  221.8 5.8 %all-to-all-start.3 = ((f32[8,128,512]{2,1,0:T(8,128)}), f32[8,128,512]{2,1,0:T(8,128)}, u32[]{:S(2)}, u32[]{:S(2)}) async-start(f32[8,128,512]{2,1,0:T(8,128)} %bitcast.15), calls=%async_computation.3 | async-start | bytes 4194304 | tf_op jit(solution)/shard_map/all_to_all | solution.py:1129
  228.1 10.0 %parted_product.3 = (f32[8,192,384]{2,1,0:T(8,128)}, f32[8,192,384]{2,1,0:T(8,128)}) custom-call(s32[2]{0:T(128)} %pad_add_fusion.1.bits_ref, bf16[1024,3072]{1,0:T(8,128)(2,1)} %get-tuple-element.138.left_ref, f32[1024,768]{1,0:T(8,128)} %bitcast.52, f32[3072,384]{1,0:T(8,128)} %collective-permute-done.6.taken_ref), custom_call_target="tpu_custom_call" | custom-call | tf_op jit(solution)/shard_map/parted_product/pallas_call | solution.py:899
  239.7 32.9 %backward_convolution.1 = (bf16[3,1024,768]{2,1,0:T(8,128)(2,1)}, f32[768,512]{1,0:T(8,128)}, f32[768,512]{1,0:T(8,128)}, f32[16,768]{1,0:T(8,128)}) custom-call(s32[2]{0:T(128)} %pad_add_fusion.start_ref, f32[1024,768]{1,0:T(8,128)} %get-tuple-element.153.grad_ref, f32[1024,768]{1,0:T(8,128)} %get-tuple-element.154.convolved_ref, ...), custom_call_target="tpu_custom_call" | custom-call | tf_op jit(solution)/shard_map/backward_convolution/pallas_call | solution.py:620
  272.6 10.9 %input_grad.1 = (f32[1024,512]{1,0:T(8,128)}, f32[1024,256]{1,0:T(8,128)}, f32[2,768]{1,0:T(2,128)}) custom-call(bf16[3,1024,768]{2,1,0:T(8,128)(2,1)} %get-tuple-element.171.mixed_ref.right_ref, bf16[768,2304]{1,0:T(8,128)(2,1)} %weight_ref.3, f32[1024,768]{1,0:T(8,128)} %bitcast.55, f32[1,768]{1,0:T(1,128)} %broadcast_in_dim.34.gain_ref, ...), custom_call_target="tpu_custom_call" | custom-call | tf_op jit(solution)/shard_map/input_grad/pallas_call | solution.py:800
  283.5 6.0 %half_product.4 = f32[768,1152]{1,0:T(8,128)} custom-call(s32[1]{0:T(128)} %sub.35.half_ref, bf16[1024,768]{1,0:T(8,128)(2,1)} %get-tuple-element.159.left_ref, bf16[3,1024,768]{2,1,0:T(8,128)(2,1)} %get-tuple-element.171.mixed_ref.right_ref), custom_call_target="tpu_custom_call" | custom-call | tf_op jit(solution)/shard_map/half_product/pallas_call | solution.py:838
  289.4 10.3 %collective-permute-done.7.refs_1_ = f32[8,192,384]{2,1,0:T(8,128)S(1)} collective-permute-done((f32[8,192,384]{2,1,0:T(8,128)}, f32[8,192,384]{2,1,0:T(8,128)S(1)}, u32[]{:S(2)}, u32[]{:S(2)}) %collective-permute-start.7) | collective-permute-done | bytes 2359328 | tf_op jit(solution)/shard_map/ppermute | solution.py:1002
  299.7 5.7 %all-to-all-start.4 = ((f32[8,128,512]{2,1,0:T(8,128)}), f32[8,128,512]{2,1,0:T(8,128)}, u32[]{:S(2)}, u32[]{:S(2)}) async-start(f32[8,128,512]{2,1,0:T(8,128)} %bitcast.57), calls=%async_computation.4 | async-start | bytes 4194304 | tf_op jit(solution)/shard_map/all_to_all | solution.py:1129
  306.3 7.5 %parted_product.4 = (f32[8,48,1152]{2,1,0:T(8,128)}, f32[8,48,1152]{2,1,0:T(8,128)}) custom-call(s32[2]{0:T(128)} %pad_add_fusion.1.bits_ref, bf16[1024,768]{1,0:T(8,128)(2,1)} %get-tuple-element.159.left_ref, bf16[3,1024,768]{2,1,0:T(8,128)(2,1)} %get-tuple-element.171.mixed_ref.right_ref, f32[768,1152]{1,0:T(8,128)} %collective-permute-done.9.taken_ref), custom_call_target="tpu_custom_call" | custom-call | tf_op jit(solution)/shard_map/parted_product/pallas_call | solution.py:899
  340.6 24.7 %collective-permute-done.8.refs_1_ = f32[4,192,384]{2,1,0:T(8,128)} collective-permute-done((f32[4,192,384]{2,1,0:T(8,128)}, f32[4,192,384]{2,1,0:T(8,128)}, u32[]{:S(2)}, u32[]{:S(2)}) %collective-permute-start.8) | collective-permute-done | bytes 1179680 | tf_op jit(solution)/shard_map/ppermute | solution.py:1002
  382.6 26.2 %collective-permute-done.17.refs_1_ = f32[2,48,1536]{2,1,0:T(8,128)S(1)} collective-permute-done((f32[2,48,1536]{2,1,0:T(8,128)S(1)}, f32[2,48,1536]{2,1,0:T(8,128)S(1)}, u32[]{:S(2)}, u32[]{:S(2)}) %collective-permute-start.17) | collective-permute-done | bytes 589856 | tf_op jit(solution)/shard_map/ppermute | solution.py:1002
  424.5 11.3 %collective-permute-done.18.refs_3_ = f32[4,48,1024]{2,1,0:T(8,128)S(1)} collective-permute-done((f32[4,48,1024]{2,1,0:T(8,128)}, f32[4,48,1024]{2,1,0:T(8,128)S(1)}, u32[]{:S(2)}, u32[]{:S(2)}) %collective-permute-start.18) | collective-permute-done | bytes 786464 | tf_op jit(solution)/shard_map/ppermute | solution.py:1002
  439.8 7.3 %collective-permute-done.21.y_ref = f32[48,1536]{1,0:T(8,128)S(1)} collective-permute-done((f32[48,1536]{1,0:T(8,128)S(1)}, f32[48,1536]{1,0:T(8,128)S(1)}, u32[]{:S(2)}, u32[]{:S(2)}) %collective-permute-start.21) | collective-permute-done | bytes 294944 | tf_op jit(solution)/shard_map/ppermute | solution.py:1002
  458.8 15.0 %collective-permute-done.24 = f32[1,48,2176]{2,1,0:T(8,128)S(1)} collective-permute-done((f32[1,48,2176]{2,1,0:T(8,128)S(1)}, f32[1,48,2176]{2,1,0:T(8,128)S(1)}, u32[]{:S(2)}, u32[]{:S(2)}) %collective-permute-start.24) | collective-permute-done | bytes 417824 | tf_op jit(solution)/shard_map/ppermute | solution.py:1002
  475.8 9.1 %collective-permute-done.25.y_ref = f32[48,2176]{1,0:T(8,128)S(1)} collective-permute-done((f32[48,2176]{1,0:T(8,128)S(1)}, f32[48,2176]{1,0:T(8,128)S(1)}, u32[]{:S(2)}, u32[]{:S(2)}) %collective-permute-start.25) | collective-permute-done | bytes 417824 | tf_op jit(solution)/shard_map/ppermute | solution.py:1002
  (228 shorter events, 138.4 us)
Async XLA Ops:
  20.6 76.7 %all-to-all-start = ((f32[8,128,768]{2,1,0:T(8,128)}), f32[8,128,768]{2,1,0:T(8,128)S(1)}, u32[]{:S(2)}, u32[]{:S(2)}) async-start(f32[8,128,768]{2,1,0:T(8,128)} %convert_element_type.8), calls=%async_computation | async-start | bytes 6291456 | tf_op jit(solution)/shard_map/all_to_all | solution.py:1075
  26.4 35.2 %collective-permute-start.3 = (f32[4,1,192,128]{3,2,0,1:T(8,128)S(1)}, f32[4,1,192,128]{3,2,0,1:T(8,128)}, u32[]{:S(2)}, u32[]{:S(2)}) collective-permute-start(f32[4,1,192,128]{3,2,0,1:T(8,128)S(1)} %bitcast.58), channel_id=1, source_target_pairs={{0,1},{1,0},{2,3},{3,2},{4,5},{5,4},{6,7},{7,6},{8,9},{9,8},{10,11... | collective-permute-start | bytes 1179656 | tf_op jit(solution)/shard_map/ppermute | solution.py:1002
  63.6 18.9 %collective-permute-start.4 = (f32[8,192,128]{2,1,0:T(8,128)}, f32[8,192,128]{2,1,0:T(8,128)}, u32[]{:S(2)}, u32[]{:S(2)}) collective-permute-start(f32[8,192,128]{2,1,0:T(8,128)} %bitcast.5), channel_id=1, source_target_pairs={{0,16},{8,24},{16,0},{24,8},{1,17},{9,25},{17,1},{25,9},{2,18},{10... | collective-permute-start | bytes 2359304 | tf_op jit(solution)/shard_map/ppermute | solution.py:1002
  98.9 76.2 %all-to-all-start.1 = ((f32[8,128,768]{2,1,0:T(8,128)}), f32[8,128,768]{2,1,0:T(8,128)S(1)}, u32[]{:S(2)}, u32[]{:S(2)}) async-start(f32[8,128,768]{2,1,0:T(8,128)} %convert_element_type.9), calls=%async_computation.1 | async-start | bytes 6291456 | tf_op jit(solution)/shard_map/all_to_all | solution.py:1084
  184.6 36.1 %collective-permute-start.6 = (f32[3072,384]{1,0:T(8,128)}, f32[3072,384]{1,0:T(8,128)}, u32[]{:S(2)}, u32[]{:S(2)}) collective-permute-start(f32[3072,384]{1,0:T(8,128)} %half_product.3), channel_id=1, source_target_pairs={{0,8},{8,0},{16,24},{24,16},{1,9},{9,1},{17,25},{25,17},{2,10},{10... | collective-permute-start | bytes 14155784 | tf_op jit(solution)/shard_map/ppermute | solution.py:1002
  184.6 36.1 %all-to-all-start.2 = ((f32[8,128,256]{2,1,0:T(8,128)}), f32[8,128,256]{2,1,0:T(8,128)S(1)}, u32[]{:S(2)}, u32[]{:S(2)}) async-start(f32[8,128,256]{2,1,0:T(8,128)} %bitcast.60), calls=%async_computation.2 | async-start | bytes 2097152 | tf_op jit(solution)/shard_map/all_to_all | solution.py:1129
  188.3 236.2 %reduce-scatter.2.cloned.1.call-start = ((), (), s32[]{:S(2)}) async-start(), calls=%async_computation.7 | async-start | bytes 9732096 | tf_op jit(solution)/shard_map/reduce_scatter | solution.py:1161
  221.8 77.9 %all-to-all-start.3 = ((f32[8,128,512]{2,1,0:T(8,128)}), f32[8,128,512]{2,1,0:T(8,128)}, u32[]{:S(2)}, u32[]{:S(2)}) async-start(f32[8,128,512]{2,1,0:T(8,128)} %bitcast.15), calls=%async_computation.3 | async-start | bytes 4194304 | tf_op jit(solution)/shard_map/all_to_all | solution.py:1129
  238.2 61.5 %collective-permute-start.7 = (f32[8,192,384]{2,1,0:T(8,128)}, f32[8,192,384]{2,1,0:T(8,128)S(1)}, u32[]{:S(2)}, u32[]{:S(2)}) collective-permute-start(f32[8,192,384]{2,1,0:T(8,128)} %get-tuple-element.161), channel_id=1, source_target_pairs={{0,16},{8,24},{16,0},{24,8},{1,17},{9,25},{17,1},{25,9},{2,18},{10... | collective-permute-start | bytes 7077896 | tf_op jit(solution)/shard_map/ppermute | solution.py:1002
  299.7 65.6 %all-to-all-start.4 = ((f32[8,128,512]{2,1,0:T(8,128)}), f32[8,128,512]{2,1,0:T(8,128)}, u32[]{:S(2)}, u32[]{:S(2)}) async-start(f32[8,128,512]{2,1,0:T(8,128)} %bitcast.57), calls=%async_computation.4 | async-start | bytes 4194304 | tf_op jit(solution)/shard_map/all_to_all | solution.py:1129
  313.7 51.6 %collective-permute-start.10 = (f32[8,48,1152]{2,1,0:T(8,128)}, f32[8,48,1152]{2,1,0:T(8,128)}, u32[]{:S(2)}, u32[]{:S(2)}) collective-permute-start(f32[8,48,1152]{2,1,0:T(8,128)} %get-tuple-element.175), channel_id=1, source_target_pairs={{0,16},{8,24},{16,0},{24,8},{1,17},{9,25},{17,1},{25,9},{2,18},{10... | collective-permute-start | bytes 5308424 | tf_op jit(solution)/shard_map/ppermute | solution.py:1002
  315.2 14.7 %collective-permute-start.11 = (f32[768,512]{1,0:T(8,128)}, f32[768,512]{1,0:T(8,128)}, u32[]{:S(2)}, u32[]{:S(2)}) collective-permute-start(f32[768,512]{1,0:T(8,128)} %get-tuple-element.177), channel_id=1, source_target_pairs={{0,8},{8,0},{16,24},{24,16},{1,9},{9,1},{17,25},{25,17},{2,10},{10... | collective-permute-start | bytes 4718600 | tf_op jit(solution)/shard_map/ppermute | solution.py:1002
  320.6 15.3 %collective-permute-start.13 = (f32[768,384]{1,0:T(8,128)}, f32[768,384]{1,0:T(8,128)}, u32[]{:S(2)}, u32[]{:S(2)}) collective-permute-start(f32[768,384]{1,0:T(8,128)} %half_product.5), channel_id=1, source_target_pairs={{0,8},{8,0},{16,24},{24,16},{1,9},{9,1},{17,25},{25,17},{2,10},{10... | collective-permute-start | bytes 3538952 | tf_op jit(solution)/shard_map/ppermute | solution.py:1002
  321.1 44.2 %collective-permute-start.8 = (f32[4,192,384]{2,1,0:T(8,128)}, f32[4,192,384]{2,1,0:T(8,128)}, u32[]{:S(2)}, u32[]{:S(2)}) collective-permute-start(f32[4,192,384]{2,1,0:T(8,128)} %get-tuple-element.170), channel_id=1, source_target_pairs={{0,1},{1,0},{2,3},{3,2},{4,5},{5,4},{6,7},{7,6},{8,9},{9,8},{10,11... | collective-permute-start | bytes 3538952 | tf_op jit(solution)/shard_map/ppermute | solution.py:1002
  365.3 46.1 %all-to-all-start.5 = ((f32[8,128,256]{2,1,0:T(8,128)}), f32[8,128,256]{2,1,0:T(8,128)}, u32[]{:S(2)}, u32[]{:S(2)}) async-start(f32[8,128,256]{2,1,0:T(8,128)} %bitcast.59), calls=%async_computation.5 | async-start | bytes 2097152 | tf_op jit(solution)/shard_map/all_to_all | solution.py:1129
  370.4 103.5 %all-gather.2.cloned.1.call-start = ((), (), s32[]{:S(2)}) async-start(), calls=%async_computation.8 | async-start | bytes 1474560 | tf_op jit(solution)/shard_map/all_gather | solution.py:1265
  370.5 40.9 %collective-permute-start.15 = (f32[8,48,640]{2,1,0:T(8,128)}, f32[8,48,640]{2,1,0:T(8,128)}, u32[]{:S(2)}, u32[]{:S(2)}) collective-permute-start(f32[8,48,640]{2,1,0:T(8,128)} %copy-done.21), channel_id=1, source_target_pairs={{0,16},{8,24},{16,0},{24,8},{1,17},{9,25},{17,1},{25,9},{2,18},{10... | collective-permute-start | bytes 2949128 | tf_op jit(solution)/shard_map/ppermute | solution.py:1002
  376.5 34.0 %collective-permute-start.14 = (f32[4,48,1152]{2,1,0:T(8,128)}, f32[4,48,1152]{2,1,0:T(8,128)S(1)}, u32[]{:S(2)}, u32[]{:S(2)}) collective-permute-start(f32[4,48,1152]{2,1,0:T(8,128)} %get-tuple-element.196), channel_id=1, source_target_pairs={{0,1},{1,0},{2,3},{3,2},{4,5},{5,4},{6,7},{7,6},{8,9},{9,8},{10,11... | collective-permute-start | bytes 2654216 | tf_op jit(solution)/shard_map/ppermute | solution.py:1002
  380.6 28.2 %collective-permute-start.17 = (f32[2,48,1536]{2,1,0:T(8,128)S(1)}, f32[2,48,1536]{2,1,0:T(8,128)S(1)}, u32[]{:S(2)}, u32[]{:S(2)}) collective-permute-start(f32[2,48,1536]{2,1,0:T(8,128)S(1)} %get-tuple-element.199), channel_id=1, source_target_pairs={{0,2},{1,3},{2,0},{3,1},{4,6},{5,7},{6,4},{7,5},{8,10},{9,11},{10,... | collective-permute-start | bytes 1769480 | tf_op jit(solution)/shard_map/ppermute | solution.py:1002
  382.1 27.6 %collective-permute-start.16 = (f32[8,48,384]{2,1,0:T(8,128)S(1)}, f32[8,48,384]{2,1,0:T(8,128)S(1)}, u32[]{:S(2)}, u32[]{:S(2)}) collective-permute-start(f32[8,48,384]{2,1,0:T(8,128)S(1)} %copy-done.45), channel_id=1, source_target_pairs={{0,16},{8,24},{16,0},{24,8},{1,17},{9,25},{17,1},{25,9},{2,18},{10... | collective-permute-start | bytes 1769480 | tf_op jit(solution)/shard_map/ppermute | solution.py:1002
  417.0 18.8 %collective-permute-start.18 = (f32[4,48,1024]{2,1,0:T(8,128)}, f32[4,48,1024]{2,1,0:T(8,128)S(1)}, u32[]{:S(2)}, u32[]{:S(2)}) collective-permute-start(f32[4,48,1024]{2,1,0:T(8,128)} %get-tuple-element.210), channel_id=1, source_target_pairs={{0,1},{1,0},{2,3},{3,2},{4,5},{5,4},{6,7},{7,6},{8,9},{9,8},{10,11... | collective-permute-start | bytes 2359304 | tf_op jit(solution)/shard_map/ppermute | solution.py:1002
  422.1 15.1 %collective-permute-start.20 = (f32[1,48,1536]{2,1,0:T(8,128)}, f32[1,48,1536]{2,1,0:T(8,128)}, u32[]{:S(2)}, u32[]{:S(2)}) collective-permute-start(f32[1,48,1536]{2,1,0:T(8,128)} %get-tuple-element.216), channel_id=1, source_target_pairs={{0,4},{1,5},{2,6},{3,7},{4,0},{5,1},{6,2},{7,3},{8,12},{9,13},{10,... | collective-permute-start | bytes 884744 | tf_op jit(solution)/shard_map/ppermute | solution.py:1002
  436.0 18.9 %collective-permute-start.19 = (f32[2,48,2176]{2,1,0:T(8,128)S(1)}, f32[2,48,2176]{2,1,0:T(8,128)S(1)}, u32[]{:S(2)}, u32[]{:S(2)}) collective-permute-start(f32[2,48,2176]{2,1,0:T(8,128)S(1)} %get-tuple-element.212), channel_id=1, source_target_pairs={{0,2},{1,3},{2,0},{3,1},{4,6},{5,7},{6,4},{7,5},{8,10},{9,11},{10,... | collective-permute-start | bytes 2506760 | tf_op jit(solution)/shard_map/ppermute | solution.py:1002
  455.0 18.9 %collective-permute-start.24 = (f32[1,48,2176]{2,1,0:T(8,128)S(1)}, f32[1,48,2176]{2,1,0:T(8,128)S(1)}, u32[]{:S(2)}, u32[]{:S(2)}) collective-permute-start(f32[1,48,2176]{2,1,0:T(8,128)S(1)} %get-tuple-element.221), channel_id=1, source_target_pairs={{0,4},{1,5},{2,6},{3,7},{4,0},{5,1},{6,2},{7,3},{8,12},{9,13},{10,... | collective-permute-start | bytes 1253384 | tf_op jit(solution)/shard_map/ppermute | solution.py:1002
  (59 other events, 433.5 us)
Sparse Core Ops, SparseCore 0:
  220.9 172.1 reduce-scatter.1
  424.6 15.0 all-gather.1

commit v5 on v4

--- a/solution.py
+++ b/solution.py
@@ -844,7 +844,7 @@
             out_specs=pl.BlockSpec((tile, columns), lambda step, half_ref: (step, 0)),
         ),
         out_shape=jax.ShapeDtypeStruct((rows, columns), jnp.float32),
-        compiler_params=kernel_parameters(),
+        compiler_params=kernel_parameters(24),
         cost_estimate=NO_COST,
         name="half_product",
     )(half, left, right)
@@ -909,7 +909,7 @@
             out_specs=tuple(specs),
         ),
         out_shape=tuple(shapes),
-        compiler_params=kernel_parameters(),
+        compiler_params=kernel_parameters(24),
         cost_estimate=NO_COST,
         name="parted_product",
     )(jnp.concatenate([half] + [which for which, _ in plan]), left, right, taken)

time: 500 us -> 503 us (level)
  Pallas kernels: 185 us -> 175 us
  local copies, waits for them, and re-layouts: 29.2 us -> 38.7 us
    unnamed x97 -> x115, local copies, waits for them, and re-layouts: 19.3 us -> 28.9 us
    pallas_call x3, Pallas kernels: 17.5 us -> 11 us  [half_product(): pl.pallas_call(product_kernel, grid_spec=pltpu.PrefetchScalarGridSpec(num...]
    pallas_call x3, Pallas kernels: 22.2 us -> 16.6 us  [parted_product(): pl.pallas_call(parted_product_kernel, grid_spec=pltpu.PrefetchScalarGridS...]
  transfers between devices with their start and end apart: 36 -> 36, of which waited for: 17 -> 17; matrix products, arithmetic and copies ran while one was open for 7% -> 6% of each run, Pallas kernels for 35% -> 33%
where the time goes in v5:
time: 503 us; the launch traced here: 502 us
  waiting for transfers between devices  188 us (37%)
  Pallas kernels  175 us (35%)
  starting transfers between devices  60.4 us (12%)
  local copies, waits for them, and re-layouts  38.7 us (8%)
  other arithmetic  24.9 us (5%)
  between operations  14.7 us (3%)
    ppermute x28, waiting for transfers between devices, swapped(): return lax.ppermute(array, axis, [(i, i ^ by) for i in range(count)])  168 us
    pallas_call x4, Pallas kernels, by_rows(): pl.pallas_call(kernel, grid=(rows // height,), in_specs=[spec(array.shape...  65.9 us
    pallas_call x1, Pallas kernels, backward_convolution(): pl.pallas_call(backward_kernel, grid=(features // lanes,), in_specs=start...  32.9 us
    ppermute x28, starting transfers between devices, swapped(): return lax.ppermute(array, axis, [(i, i ^ by) for i in range(count)])  29.9 us
    unnamed x115, local copies, waits for them, and re-layouts  28.9 us
    all_to_all x4, starting transfers between devices, sent(): return lax.all_to_all(columns, 'seq', 0, 0, tiled=True)  19.6 us
    pallas_call x8, Pallas kernels, fold(): pl.pallas_call(fold_kernel, grid=(count // 2,), in_specs=[pl.BlockSpec(me...  17.7 us
    pallas_call x1, Pallas kernels, forward_convolution(): pl.pallas_call(forward_kernel, grid=(features // lanes,), in_specs=start_...  17.3 us
  transfers between devices with their start and end apart: 36, of which 17 were waited for; matrix products, arithmetic and copies ran while one was open for 6% of the time, Pallas kernels for 33%

profile of v5, /device:TPU:0, one launch (start us, length us, event | category | flops | bytes accessed | tf_op | source)
XLA Modules:
  0.0 501.8 jit_solution(9737777655432021549)
XLA Ops:
  20.6 5.8 %all-to-all-start = ((f32[8,128,768]{2,1,0:T(8,128)}), f32[8,128,768]{2,1,0:T(8,128)S(1)}, u32[]{:S(2)}, u32[]{:S(2)}) async-start(f32[8,128,768]{2,1,0:T(8,128)} %convert_element_type.8), calls=%async_computation | async-start | bytes 6291456 | tf_op jit(solution)/shard_map/all_to_all | solution.py:1075
  28.4 33.2 %collective-permute-done.3 = f32[4,1,192,128]{3,2,0,1:T(8,128)} collective-permute-done((f32[4,1,192,128]{3,2,0,1:T(8,128)S(1)}, f32[4,1,192,128]{3,2,0,1:T(8,128)}, u32[]{:S(2)}, u32[]{:S(2)}) %collective-permute-start.3) | collective-permute-done | bytes 393248 | tf_op jit(solution)/shard_map/ppermute | solution.py:1002
  65.1 17.4 %collective-permute-done.4 = f32[8,192,128]{2,1,0:T(8,128)} collective-permute-done((f32[8,192,128]{2,1,0:T(8,128)}, f32[8,192,128]{2,1,0:T(8,128)}, u32[]{:S(2)}, u32[]{:S(2)}) %collective-permute-start.4) | collective-permute-done | bytes 786464 | tf_op jit(solution)/shard_map/ppermute | solution.py:1002
  108.5 9.5 %project.1 = (bf16[1024,768]{1,0:T(8,128)(2,1)}, f32[1024,2304]{1,0:T(8,128)}) custom-call(f32[1024,768]{1,0:T(8,128)} %bitcast.53, f32[1,768]{1,0:T(1,128)} %broadcast_in_dim.34.gain_ref, f32[1,768]{1,0:T(1,128)} %broadcast_in_dim.35.bias_ref, bf16[768,2304]{1,0:T(8,128)(2,1)} %weight_ref.3, f32[1,2304]{1,0:T(1,128)} %broadcast_in_dim.36.offset_ref), custom_call_target="tpu_custom_call" | custom-call | tf_op jit(solution)/shard_map/project/pallas_call | solution.py:800
  118.0 17.3 %forward_convolution.1 = (f32[1024,768]{1,0:T(8,128)}, bf16[1024,768]{1,0:T(8,128)(2,1)}) custom-call(s32[2]{0:T(128)} %pad_add_fusion.start_ref, f32[1024,2304]{1,0:T(8,128)} %get-tuple-element.131.outer_ref.inner_ref.value_ref, f32[1024,2304]{1,0:T(8,128)} %get-tuple-element.131.outer_ref.inner_ref.value_ref, ...), custom_call_target="tpu_custom_call" | custom-call | tf_op jit(solution)/shard_map/forward_convolution/pallas_call | solution.py:600
  135.3 23.9 %feed.1 = (f32[1024,768]{1,0:T(8,128)}, bf16[1024,768]{1,0:T(8,128)(2,1)}, bf16[1024,3072]{1,0:T(8,128)(2,1)}, f32[1024,3072]{1,0:T(8,128)}, f32[1024,256]{1,0:T(8,128)}, /*index=5*/f32[1024,512]{1,0:T(8,128)}) custom-call(f32[1024,768]{1,0:T(8,128)} %bitcast.54, bf16[1024,768]{1,0:T(8,128)(2,1)} %get-tuple-element.134.branch_ref.left_ref, ...), custom_call_target="tpu_custom_call" | custom-call | tf_op jit(solution)/shard_map/feed/pallas_call | solution.py:800
  159.2 15.9 %all-to-all-done.1 = f32[8,128,768]{2,1,0:T(8,128)S(1)} async-done(((f32[8,128,768]{2,1,0:T(8,128)}), f32[8,128,768]{2,1,0:T(8,128)S(1)}, u32[]{:S(2)}, u32[]{:S(2)}) %all-to-all-start.1) | async-done | bytes 3145760 | tf_op jit(solution)/shard_map/all_to_all | solution.py:1084
  179.0 5.6 %half_product.3 = f32[3072,384]{1,0:T(8,128)} custom-call(s32[1]{0:T(128)} %sub.35.half_ref, bf16[1024,3072]{1,0:T(8,128)(2,1)S(1)} %copy-done.6, f32[1024,768]{1,0:T(8,128)S(1)} %bitcast.44), custom_call_target="tpu_custom_call" | custom-call | tf_op jit(solution)/shard_map/half_product/pallas_call | solution.py:838
  188.6 22.2 %feed_back.1 = (bf16[1024,3072]{1,0:T(8,128)(2,1)}, f32[1024,768]{1,0:T(8,128)}, bf16[1024,768]{1,0:T(8,128)(2,1)}, f32[1024,768]{1,0:T(8,128)}, f32[4,768]{1,0:T(4,128)}, /*index=5*/f32[1,3072]{1,0:T(1,128)}) custom-call(f32[1024,768]{1,0:T(8,128)} %bitcast.45, f32[1024,768]{1,0:T(8,128)} %get-tuple-element.140.residual_ref, ...), custom_call_target="tpu_custom_call" | custom-call | tf_op jit(solution)/shard_map/feed_back/pallas_call | solution.py:800
  210.7 10.1 %whole_product.1 = f32[768,3072]{1,0:T(8,128)} custom-call(bf16[1024,768]{1,0:T(8,128)(2,1)} %get-tuple-element.146.left_ref, bf16[1024,3072]{1,0:T(8,128)(2,1)} %get-tuple-element.147.right_ref), custom_call_target="tpu_custom_call" | custom-call | tf_op jit(solution)/shard_map/whole_product/pallas_call | solution.py:859
  221.9 6.0 %all-to-all-start.3 = ((f32[8,128,512]{2,1,0:T(8,128)}), f32[8,128,512]{2,1,0:T(8,128)}, u32[]{:S(2)}, u32[]{:S(2)}) async-start(f32[8,128,512]{2,1,0:T(8,128)} %bitcast.58), calls=%async_computation.3 | async-start | bytes 4194304 | tf_op jit(solution)/shard_map/all_to_all | solution.py:1129
  231.0 7.6 %parted_product.3 = (f32[8,192,384]{2,1,0:T(8,128)S(1)}, f32[8,192,384]{2,1,0:T(8,128)}) custom-call(s32[2]{0:T(128)S(1)} %pad_add_fusion.1.bits_ref, bf16[1024,3072]{1,0:T(8,128)(2,1)S(1)} %copy-done.7, f32[1024,768]{1,0:T(8,128)S(1)} %bitcast.46, f32[3072,384]{1,0:T(8,128)} %collective-permute-done.6.taken_ref), custom_call_target="tpu_custom_call" | custom-call | tf_op jit(solution)/shard_map/parted_product/pallas_call | solution.py:899
  241.6 32.9 %backward_convolution.1 = (bf16[3,1024,768]{2,1,0:T(8,128)(2,1)}, f32[768,512]{1,0:T(8,128)}, f32[768,512]{1,0:T(8,128)}, f32[16,768]{1,0:T(8,128)}) custom-call(s32[2]{0:T(128)} %pad_add_fusion.start_ref, f32[1024,768]{1,0:T(8,128)} %get-tuple-element.153.grad_ref, f32[1024,768]{1,0:T(8,128)} %get-tuple-element.154.convolved_ref, ...), custom_call_target="tpu_custom_call" | custom-call | tf_op jit(solution)/shard_map/backward_convolution/pallas_call | solution.py:620
  274.6 10.3 %input_grad.1 = (f32[1024,512]{1,0:T(8,128)}, f32[1024,256]{1,0:T(8,128)}, f32[2,768]{1,0:T(2,128)}) custom-call(bf16[3,1024,768]{2,1,0:T(8,128)(2,1)} %get-tuple-element.171.mixed_ref.right_ref, bf16[768,2304]{1,0:T(8,128)(2,1)} %weight_ref.3, f32[1024,768]{1,0:T(8,128)} %bitcast.55, f32[1,768]{1,0:T(1,128)} %broadcast_in_dim.34.gain_ref, ...), custom_call_target="tpu_custom_call" | custom-call | tf_op jit(solution)/shard_map/input_grad/pallas_call | solution.py:800
  290.1 11.7 %collective-permute-done.7.refs_1_ = f32[8,192,384]{2,1,0:T(8,128)} collective-permute-done((f32[8,192,384]{2,1,0:T(8,128)}, f32[8,192,384]{2,1,0:T(8,128)}, u32[]{:S(2)}, u32[]{:S(2)}) %collective-permute-start.7) | collective-permute-done | bytes 2359328 | tf_op jit(solution)/shard_map/ppermute | solution.py:1002
  301.8 5.7 %all-to-all-start.4 = ((f32[8,128,512]{2,1,0:T(8,128)}), f32[8,128,512]{2,1,0:T(8,128)}, u32[]{:S(2)}, u32[]{:S(2)}) async-start(f32[8,128,512]{2,1,0:T(8,128)} %bitcast.57), calls=%async_computation.4 | async-start | bytes 4194304 | tf_op jit(solution)/shard_map/all_to_all | solution.py:1129
  310.9 6.0 %parted_product.4 = (f32[8,48,1152]{2,1,0:T(8,128)S(1)}, f32[8,48,1152]{2,1,0:T(8,128)}) custom-call(s32[2]{0:T(128)S(1)} %pad_add_fusion.1.bits_ref, bf16[1024,768]{1,0:T(8,128)(2,1)S(1)} %copy-done.9, bf16[3,1024,768]{2,1,0:T(8,128)(2,1)S(1)} %copy-done.5, f32[768,1152]{1,0:T(8,128)} %collective-permute-done.9.taken_ref), custom_call_target="tpu_custom_call" | custom-call | tf_op jit(solution)/shard_map/parted_product/pallas_call | solution.py:899
  342.3 24.1 %collective-permute-done.8.refs_1_ = f32[4,192,384]{2,1,0:T(8,128)} collective-permute-done((f32[4,192,384]{2,1,0:T(8,128)}, f32[4,192,384]{2,1,0:T(8,128)}, u32[]{:S(2)}, u32[]{:S(2)}) %collective-permute-start.8) | collective-permute-done | bytes 1179680 | tf_op jit(solution)/shard_map/ppermute | solution.py:1002
  385.5 25.6 %collective-permute-done.17.refs_1_ = f32[2,48,1536]{2,1,0:T(8,128)S(1)} collective-permute-done((f32[2,48,1536]{2,1,0:T(8,128)S(1)}, f32[2,48,1536]{2,1,0:T(8,128)S(1)}, u32[]{:S(2)}, u32[]{:S(2)}) %collective-permute-start.17) | collective-permute-done | bytes 589856 | tf_op jit(solution)/shard_map/ppermute | solution.py:1002
  424.6 12.6 %collective-permute-done.18.refs_3_ = f32[4,48,1024]{2,1,0:T(8,128)S(1)} collective-permute-done((f32[4,48,1024]{2,1,0:T(8,128)}, f32[4,48,1024]{2,1,0:T(8,128)S(1)}, u32[]{:S(2)}, u32[]{:S(2)}) %collective-permute-start.18) | collective-permute-done | bytes 786464 | tf_op jit(solution)/shard_map/ppermute | solution.py:1002
  441.6 5.5 %collective-permute-done.21.y_ref = f32[48,1536]{1,0:T(8,128)S(1)} collective-permute-done((f32[48,1536]{1,0:T(8,128)S(1)}, f32[48,1536]{1,0:T(8,128)S(1)}, u32[]{:S(2)}, u32[]{:S(2)}) %collective-permute-start.21) | collective-permute-done | bytes 294944 | tf_op jit(solution)/shard_map/ppermute | solution.py:1002
  450.9 6.4 %collective-permute-done.19.refs_1_ = f32[2,48,2176]{2,1,0:T(8,128)S(1)} collective-permute-done((f32[2,48,2176]{2,1,0:T(8,128)S(1)}, f32[2,48,2176]{2,1,0:T(8,128)S(1)}, u32[]{:S(2)}, u32[]{:S(2)}) %collective-permute-start.19) | collective-permute-done | bytes 835616 | tf_op jit(solution)/shard_map/ppermute | solution.py:1002
  460.8 15.5 %collective-permute-done.24 = f32[1,48,2176]{2,1,0:T(8,128)S(1)} collective-permute-done((f32[1,48,2176]{2,1,0:T(8,128)S(1)}, f32[1,48,2176]{2,1,0:T(8,128)S(1)}, u32[]{:S(2)}, u32[]{:S(2)}) %collective-permute-start.24) | collective-permute-done | bytes 417824 | tf_op jit(solution)/shard_map/ppermute | solution.py:1002
  477.9 10.0 %collective-permute-done.25.y_ref = f32[48,2176]{1,0:T(8,128)S(1)} collective-permute-done((f32[48,2176]{1,0:T(8,128)S(1)}, f32[48,2176]{1,0:T(8,128)S(1)}, u32[]{:S(2)}, u32[]{:S(2)}) %collective-permute-start.25) | collective-permute-done | bytes 417824 | tf_op jit(solution)/shard_map/ppermute | solution.py:1002
  (246 shorter events, 146.3 us)
Async XLA Ops:
  20.6 76.7 %all-to-all-start = ((f32[8,128,768]{2,1,0:T(8,128)}), f32[8,128,768]{2,1,0:T(8,128)S(1)}, u32[]{:S(2)}, u32[]{:S(2)}) async-start(f32[8,128,768]{2,1,0:T(8,128)} %convert_element_type.8), calls=%async_computation | async-start | bytes 6291456 | tf_op jit(solution)/shard_map/all_to_all | solution.py:1075
  26.4 35.2 %collective-permute-start.3 = (f32[4,1,192,128]{3,2,0,1:T(8,128)S(1)}, f32[4,1,192,128]{3,2,0,1:T(8,128)}, u32[]{:S(2)}, u32[]{:S(2)}) collective-permute-start(f32[4,1,192,128]{3,2,0,1:T(8,128)S(1)} %bitcast.59), channel_id=1, source_target_pairs={{0,1},{1,0},{2,3},{3,2},{4,5},{5,4},{6,7},{7,6},{8,9},{9,8},{10,11... | collective-permute-start | bytes 1179656 | tf_op jit(solution)/shard_map/ppermute | solution.py:1002
  63.6 18.9 %collective-permute-start.4 = (f32[8,192,128]{2,1,0:T(8,128)}, f32[8,192,128]{2,1,0:T(8,128)}, u32[]{:S(2)}, u32[]{:S(2)}) collective-permute-start(f32[8,192,128]{2,1,0:T(8,128)} %bitcast.5), channel_id=1, source_target_pairs={{0,16},{8,24},{16,0},{24,8},{1,17},{9,25},{17,1},{25,9},{2,18},{10... | collective-permute-start | bytes 2359304 | tf_op jit(solution)/shard_map/ppermute | solution.py:1002
  98.9 76.2 %all-to-all-start.1 = ((f32[8,128,768]{2,1,0:T(8,128)}), f32[8,128,768]{2,1,0:T(8,128)S(1)}, u32[]{:S(2)}, u32[]{:S(2)}) async-start(f32[8,128,768]{2,1,0:T(8,128)} %convert_element_type.9), calls=%async_computation.1 | async-start | bytes 6291456 | tf_op jit(solution)/shard_map/all_to_all | solution.py:1084
  184.7 36.2 %collective-permute-start.6 = (f32[3072,384]{1,0:T(8,128)}, f32[3072,384]{1,0:T(8,128)}, u32[]{:S(2)}, u32[]{:S(2)}) collective-permute-start(f32[3072,384]{1,0:T(8,128)} %half_product.3), channel_id=1, source_target_pairs={{0,8},{8,0},{16,24},{24,16},{1,9},{9,1},{17,25},{25,17},{2,10},{10... | collective-permute-start | bytes 14155784 | tf_op jit(solution)/shard_map/ppermute | solution.py:1002
  184.7 36.2 %all-to-all-start.2 = ((f32[8,128,256]{2,1,0:T(8,128)}), f32[8,128,256]{2,1,0:T(8,128)S(1)}, u32[]{:S(2)}, u32[]{:S(2)}) async-start(f32[8,128,256]{2,1,0:T(8,128)} %bitcast.61), calls=%async_computation.2 | async-start | bytes 2097152 | tf_op jit(solution)/shard_map/all_to_all | solution.py:1129
  188.3 236.2 %reduce-scatter.2.cloned.1.call-start = ((), (), s32[]{:S(2)}) async-start(), calls=%async_computation.7 | async-start | bytes 9732096 | tf_op jit(solution)/shard_map/reduce_scatter | solution.py:1161
  221.9 79.9 %all-to-all-start.3 = ((f32[8,128,512]{2,1,0:T(8,128)}), f32[8,128,512]{2,1,0:T(8,128)}, u32[]{:S(2)}, u32[]{:S(2)}) async-start(f32[8,128,512]{2,1,0:T(8,128)} %bitcast.58), calls=%async_computation.3 | async-start | bytes 4194304 | tf_op jit(solution)/shard_map/all_to_all | solution.py:1129
  240.2 61.6 %collective-permute-start.7 = (f32[8,192,384]{2,1,0:T(8,128)}, f32[8,192,384]{2,1,0:T(8,128)}, u32[]{:S(2)}, u32[]{:S(2)}) collective-permute-start(f32[8,192,384]{2,1,0:T(8,128)} %get-tuple-element.161), channel_id=1, source_target_pairs={{0,16},{8,24},{16,0},{24,8},{1,17},{9,25},{17,1},{25,9},{2,18},{10... | collective-permute-start | bytes 7077896 | tf_op jit(solution)/shard_map/ppermute | solution.py:1002
  301.8 67.4 %all-to-all-start.4 = ((f32[8,128,512]{2,1,0:T(8,128)}), f32[8,128,512]{2,1,0:T(8,128)}, u32[]{:S(2)}, u32[]{:S(2)}) async-start(f32[8,128,512]{2,1,0:T(8,128)} %bitcast.57), calls=%async_computation.4 | async-start | bytes 4194304 | tf_op jit(solution)/shard_map/all_to_all | solution.py:1129
  316.8 52.3 %collective-permute-start.10 = (f32[8,48,1152]{2,1,0:T(8,128)}, f32[8,48,1152]{2,1,0:T(8,128)}, u32[]{:S(2)}, u32[]{:S(2)}) collective-permute-start(f32[8,48,1152]{2,1,0:T(8,128)} %get-tuple-element.175), channel_id=1, source_target_pairs={{0,16},{8,24},{16,0},{24,8},{1,17},{9,25},{17,1},{25,9},{2,18},{10... | collective-permute-start | bytes 5308424 | tf_op jit(solution)/shard_map/ppermute | solution.py:1002
  318.2 15.3 %collective-permute-start.11 = (f32[768,512]{1,0:T(8,128)}, f32[768,512]{1,0:T(8,128)}, u32[]{:S(2)}, u32[]{:S(2)}) collective-permute-start(f32[768,512]{1,0:T(8,128)} %get-tuple-element.177), channel_id=1, source_target_pairs={{0,8},{8,0},{16,24},{24,16},{1,9},{9,1},{17,25},{25,17},{2,10},{10... | collective-permute-start | bytes 4718600 | tf_op jit(solution)/shard_map/ppermute | solution.py:1002
  324.2 13.3 %collective-permute-start.13 = (f32[768,384]{1,0:T(8,128)}, f32[768,384]{1,0:T(8,128)}, u32[]{:S(2)}, u32[]{:S(2)}) collective-permute-start(f32[768,384]{1,0:T(8,128)} %half_product.5), channel_id=1, source_target_pairs={{0,8},{8,0},{16,24},{24,16},{1,9},{9,1},{17,25},{25,17},{2,10},{10... | collective-permute-start | bytes 3538952 | tf_op jit(solution)/shard_map/ppermute | solution.py:1002
  324.7 41.7 %collective-permute-start.8 = (f32[4,192,384]{2,1,0:T(8,128)}, f32[4,192,384]{2,1,0:T(8,128)}, u32[]{:S(2)}, u32[]{:S(2)}) collective-permute-start(f32[4,192,384]{2,1,0:T(8,128)} %get-tuple-element.170), channel_id=1, source_target_pairs={{0,1},{1,0},{2,3},{3,2},{4,5},{5,4},{6,7},{7,6},{8,9},{9,8},{10,11... | collective-permute-start | bytes 3538952 | tf_op jit(solution)/shard_map/ppermute | solution.py:1002
  369.2 43.7 %all-to-all-start.5 = ((f32[8,128,256]{2,1,0:T(8,128)}), f32[8,128,256]{2,1,0:T(8,128)}, u32[]{:S(2)}, u32[]{:S(2)}) async-start(f32[8,128,256]{2,1,0:T(8,128)} %bitcast.60), calls=%async_computation.5 | async-start | bytes 2097152 | tf_op jit(solution)/shard_map/all_to_all | solution.py:1129
  373.4 102.8 %all-gather.2.cloned.1.call-start = ((), (), s32[]{:S(2)}) async-start(), calls=%async_computation.8 | async-start | bytes 1474560 | tf_op jit(solution)/shard_map/all_gather | solution.py:1265
  373.5 39.4 %collective-permute-start.15 = (f32[8,48,640]{2,1,0:T(8,128)}, f32[8,48,640]{2,1,0:T(8,128)}, u32[]{:S(2)}, u32[]{:S(2)}) collective-permute-start(f32[8,48,640]{2,1,0:T(8,128)} %copy-done.31), channel_id=1, source_target_pairs={{0,16},{8,24},{16,0},{24,8},{1,17},{9,25},{17,1},{25,9},{2,18},{10... | collective-permute-start | bytes 2949128 | tf_op jit(solution)/shard_map/ppermute | solution.py:1002
  379.5 33.4 %collective-permute-start.14 = (f32[4,48,1152]{2,1,0:T(8,128)}, f32[4,48,1152]{2,1,0:T(8,128)}, u32[]{:S(2)}, u32[]{:S(2)}) collective-permute-start(f32[4,48,1152]{2,1,0:T(8,128)} %get-tuple-element.196), channel_id=1, source_target_pairs={{0,1},{1,0},{2,3},{3,2},{4,5},{5,4},{6,7},{7,6},{8,9},{9,8},{10,11... | collective-permute-start | bytes 2654216 | tf_op jit(solution)/shard_map/ppermute | solution.py:1002
  383.5 27.7 %collective-permute-start.17 = (f32[2,48,1536]{2,1,0:T(8,128)S(1)}, f32[2,48,1536]{2,1,0:T(8,128)S(1)}, u32[]{:S(2)}, u32[]{:S(2)}) collective-permute-start(f32[2,48,1536]{2,1,0:T(8,128)S(1)} %get-tuple-element.199), channel_id=1, source_target_pairs={{0,2},{1,3},{2,0},{3,1},{4,6},{5,7},{6,4},{7,5},{8,10},{9,11},{10,... | collective-permute-start | bytes 1769480 | tf_op jit(solution)/shard_map/ppermute | solution.py:1002
  384.9 27.1 %collective-permute-start.16 = (f32[8,48,384]{2,1,0:T(8,128)}, f32[8,48,384]{2,1,0:T(8,128)S(1)}, u32[]{:S(2)}, u32[]{:S(2)}) collective-permute-start(f32[8,48,384]{2,1,0:T(8,128)} %copy-done.32), channel_id=1, source_target_pairs={{0,16},{8,24},{16,0},{24,8},{1,17},{9,25},{17,1},{25,9},{2,18},{10... | collective-permute-start | bytes 1769480 | tf_op jit(solution)/shard_map/ppermute | solution.py:1002
  418.4 18.7 %collective-permute-start.18 = (f32[4,48,1024]{2,1,0:T(8,128)}, f32[4,48,1024]{2,1,0:T(8,128)S(1)}, u32[]{:S(2)}, u32[]{:S(2)}) collective-permute-start(f32[4,48,1024]{2,1,0:T(8,128)} %get-tuple-element.210), channel_id=1, source_target_pairs={{0,1},{1,0},{2,3},{3,2},{4,5},{5,4},{6,7},{7,6},{8,9},{9,8},{10,11... | collective-permute-start | bytes 2359304 | tf_op jit(solution)/shard_map/ppermute | solution.py:1002
  422.1 17.1 %collective-permute-start.20 = (f32[1,48,1536]{2,1,0:T(8,128)S(1)}, f32[1,48,1536]{2,1,0:T(8,128)S(1)}, u32[]{:S(2)}, u32[]{:S(2)}) collective-permute-start(f32[1,48,1536]{2,1,0:T(8,128)S(1)} %get-tuple-element.216), channel_id=1, source_target_pairs={{0,4},{1,5},{2,6},{3,7},{4,0},{5,1},{6,2},{7,3},{8,12},{9,13},{10,... | collective-permute-start | bytes 884744 | tf_op jit(solution)/shard_map/ppermute | solution.py:1002
  438.5 18.8 %collective-permute-start.19 = (f32[2,48,2176]{2,1,0:T(8,128)S(1)}, f32[2,48,2176]{2,1,0:T(8,128)S(1)}, u32[]{:S(2)}, u32[]{:S(2)}) collective-permute-start(f32[2,48,2176]{2,1,0:T(8,128)S(1)} %get-tuple-element.212), channel_id=1, source_target_pairs={{0,2},{1,3},{2,0},{3,1},{4,6},{5,7},{6,4},{7,5},{8,10},{9,11},{10,... | collective-permute-start | bytes 2506760 | tf_op jit(solution)/shard_map/ppermute | solution.py:1002
  457.4 18.8 %collective-permute-start.24 = (f32[1,48,2176]{2,1,0:T(8,128)S(1)}, f32[1,48,2176]{2,1,0:T(8,128)S(1)}, u32[]{:S(2)}, u32[]{:S(2)}) collective-permute-start(f32[1,48,2176]{2,1,0:T(8,128)S(1)} %get-tuple-element.221), channel_id=1, source_target_pairs={{0,4},{1,5},{2,6},{3,7},{4,0},{5,1},{6,2},{7,3},{8,12},{9,13},{10,... | collective-permute-start | bytes 1253384 | tf_op jit(solution)/shard_map/ppermute | solution.py:1002
  (68 other events, 441.0 us)
Sparse Core Ops, SparseCore 0:
  221.0 173.0 reduce-scatter.1
  424.7 15.2 all-gather.1
